TPU v7x, 32 devices: a whole 2x2x4 slice. The times are simulated.
32 devices in a mesh: col: 8 (over z, y), ch: 4 (over x, core).
Axes of the slice: x: 2, y: 2, z: 4, core: 2. Of those that a mesh axis runs over, the one named last changes fastest.
Arguments:
- features: bfloat16 [64, 8, 8, 1024], P('ch', None, 'col'), may hold values from -6 to 6
- solid_mask: int32 [8, 8, 1024], P(None, 'col'), may hold values 0 or 1
- weight_one: bfloat16 [64, 27, 64], P('ch'), may hold values from -0.15625 to 0.15625
- bias_one: float32 [64], P('ch'), may hold values from -3 to 3
- weight_two: bfloat16 [64, 27, 64], P('ch'), may hold values from -0.15625 to 0.15625
- bias_two: float32 [64], P('ch'), may hold values from -3 to 3
Outputs:
- activations: bfloat16 [64, 8, 8, 1024], P('ch', None, 'col')
All inputs are finite; a program needn't handle non-finite values. No bound on the sum of `solid_mask` on one device may be relied on, other than what follows from the above.
Results may differ from a plain program's by a relative error of at most 0.013.
Values may be sent and summed in bfloat16 or wider, within the bound.
No kernel may reach another device: no remote copies, remote signals or barrier semaphores. Data moves between devices by JAX's collectives and lax.ppermute only.
A program may use at most 64 MiB of HBM per device.

v0:
```python
import jax
import jax.numpy as jnp
from jax import lax
from jax.sharding import PartitionSpec as P

CY = 32
CZ = 32


def passed_along(block, axis, distance):
    devices = range(lax.axis_size(axis))
    route = [(i - distance, i) for i in devices if i - distance in devices]
    return lax.ppermute(block, axis, route)


def kernel_of(weight):
    outputs = weight.shape[0]
    inputs = weight.shape[2]
    return weight.reshape(outputs, 3, 3, 3, inputs).transpose(0, 4, 1, 2, 3)


def on_device(features, solid_mask, weight_one, bias_one, weight_two, bias_two):
    cells = features.shape[3]
    columns = lax.axis_size("col")
    grid_z = min(8, columns)
    open_cells = (1 - solid_mask).astype(jnp.float32)

    def pad_columns(field):
        depth = field.shape[0]
        depth_x = field.shape[1]
        cube = field.reshape(depth, depth_x, CY, CZ)
        below = passed_along(cube[:, :, :, CZ - 1 :], "col", 1)
        above = passed_along(cube[:, :, :, :1], "col", -1)
        place = lax.axis_index("col") % grid_z
        below = jnp.where(place > 0, below, jnp.zeros_like(below))
        above = jnp.where(place < grid_z - 1, above, jnp.zeros_like(above))
        cube = jnp.concatenate([below, cube, above], axis=3)
        south = passed_along(cube[:, :, CY - 1 :, :], "col", grid_z)
        north = passed_along(cube[:, :, :1, :], "col", -grid_z)
        return jnp.concatenate([south, cube, north], axis=2)

    def pad_planes(framed):
        return jnp.pad(framed, ((0, 0), (1, 1), (0, 0), (0, 0)))

    def padded_inputs(field):
        whole = lax.all_gather(field, "ch", axis=0, tiled=True)
        framed = pad_columns(whole)
        return pad_planes(framed)

    def convolve(framed, weight):
        depth_x = framed.shape[1] - 2
        result = lax.conv_general_dilated(
            framed[None],
            kernel_of(weight),
            (1, 1, 1),
            "VALID",
            dimension_numbers=("NCDHW", "OIDHW", "NCDHW"),
            preferred_element_type=jnp.float32,
        )
        return result[0].reshape(weight.shape[0], depth_x, 1, cells)

    def finish(total, bias, opened):
        return (jnp.maximum(total + bias[:, None, None, None], 0.0) * opened[None]).astype(
            jnp.bfloat16
        )

    hidden = finish(convolve(padded_inputs(features), weight_one), bias_one, open_cells)
    total = convolve(padded_inputs(hidden), weight_two)
    return finish(total, bias_two, open_cells)


def solution(mesh):
    in_specs = (
        P("ch", None, "col", None),
        P(None, "col", None),
        P("ch", None, None),
        P("ch"),
        P("ch", None, None),
        P("ch"),
    )
    out_specs = P("ch", None, "col", None)
    return jax.shard_map(
        on_device, mesh=mesh, in_specs=in_specs, out_specs=out_specs, check_vma=False
    )
```

profile of v0, /device:TPU:0, one launch (start us, length us, event | category | flops | bytes accessed | tf_op | source)
XLA Modules:
  0.0 154.1 jit_solution(9514300812282072571)
XLA Ops:
  6.5 0.0 copy-start
  6.5 0.0 copy-start.1
  6.5 0.0 all-gather.3.cloned.1.call-start
  6.5 0.7 all-gather.3.cloned.1.call-update
  7.3 0.0 all-gather.5.cloned.1.call-start
  7.3 21.1 %all-gather.3.cloned.1.call-done = bf16[64,8,1,1024]{3,1,2,0:T(8,128)(2,1)} async-done(((bf16[16,8,1,1024]{3,1,2,0:T(8,128)(2,1)}), bf16[64,8,1,1024]{3,1,2,0:T(8,128)(2,1)}) %all-gather.3.cloned.1.call-update) | async-done | bytes 1048592 | tf_op jit(solution)/shard_map/all_gather | solution.py:46
  28.4 2.4 %copy.31 = bf16[64,8,1,1024]{0,3,1,2:T(8,128)(2,1)S(1)} copy(bf16[64,8,1,1024]{3,1,2,0:T(8,128)(2,1)} %all-gather.3.cloned.1.call-done) | data formatting | bytes 2097152 | tf_op jit(solution)/shard_map/all_gather | solution.py:46
  30.7 0.3 fusion.39
  31.0 3.4 %collective-permute-start = (bf16[64,8,32,1]{0,3,2,1:T(2,128)(2,1)S(1)}, bf16[64,8,32,1]{0,3,2,1:T(2,128)(2,1)S(1)}, u32[]{:S(2)}, u32[]{:S(2)}) collective-permute-start(bf16[64,8,32,1]{0,3,2,1:T(2,128)(2,1)S(1)} %get-tuple-element.11), channel_id=1, source_target_pairs={{0,4},{4,8},{8,12},{12,16},{16,20},{20,24},{24,28},{1,5},{5,9},{9,... | collective-permute-start | bytes 98312 | tf_op jit(solution)/shard_map/ppermute | solution.py:13
  34.4 1.3 collective-permute-start.1
  35.7 1.8 %collective-permute-done = bf16[64,8,32,1]{0,3,2,1:T(2,128)(2,1)S(1)} collective-permute-done((bf16[64,8,32,1]{0,3,2,1:T(2,128)(2,1)S(1)}, bf16[64,8,32,1]{0,3,2,1:T(2,128)(2,1)S(1)}, u32[]{:S(2)}, u32[]{:S(2)}) %collective-permute-start) | collective-permute-done | bytes 32800 | tf_op jit(solution)/shard_map/ppermute | solution.py:13
  37.5 0.1 broadcast_select_fusion.5
  37.7 4.0 %collective-permute-done.1 = bf16[64,8,32,1]{0,3,2,1:T(2,128)(2,1)S(1)} collective-permute-done((bf16[64,8,32,1]{0,3,2,1:T(2,128)(2,1)S(1)}, bf16[64,8,32,1]{0,3,2,1:T(2,128)(2,1)S(1)}, u32[]{:S(2)}, u32[]{:S(2)}) %collective-permute-start.1) | collective-permute-done | bytes 32800 | tf_op jit(solution)/shard_map/ppermute | solution.py:13
  41.7 0.1 broadcast_select_fusion.3
  41.8 0.1 pad_maximum_fusion.5
  41.9 0.7 collective-permute-start.2
  42.6 0.7 collective-permute-start.3
  43.2 0.0 copy-done.1
  43.3 0.0 collective-permute-done.2
  43.3 0.0 collective-permute-done.3
  43.3 2.6 %fusion.18 = bf16[64,10,34,1,34]{0,4,2,1,3:T(8,128)(2,1)S(1)} fusion(bf16[64,8,1,34]{0,3,2,1:T(8,128)(2,1)S(1)} %collective-permute-done.3, bf16[64,8,1,34]{0,3,2,1:T(8,128)(2,1)S(1)} %collective-permute-done.2, bf16[64,8,32,1]{0,3,2,1:T(2,128)(2,1)S(1)} %broadcast_select_fusion.3, bf16[64,8,32,32]{0,3,2,1:T(8,128)(2,1)S(1)} %bitcast.42, ...), kind=kLoop, calls=%fused_computation.24 | loop fusion | flops 13317120 | bytes 2663424 | tf_op jit(solution)/shard_map/broadcast_in_dim | solution.py:53
  45.9 0.5 copy.46
  46.4 0.9 pad.9.clone
  47.3 0.0 copy-start.5
  47.3 0.5 copy.34
  47.8 0.4 slice.38
  48.2 0.0 copy-done
  48.2 0.0 copy-done.5
  48.2 21.4 %broadcast_select_fusion.1 = f32[8,32,8,5,16]{4,2,3,1,0:T(8,128)} fusion(pred[8,5]{0,1:T(8,128)(4,1)S(1)} %copy-done.5, bf16[16,3,3,3,64]{4,0,3,2,1:T(8,128)(2,1)S(1)} %bitcast.39, bf16[64,10,34,1,7,2]{0,4,5,2,1,3:T(8,128)(2,1)S(1)} %slice.38, bf16[64,10,34,1,8,5]{0,4,5,2,1,3:T(8,128)(2,1)S(1)} %copy.34), kind=kOutput, calls=%fused_computation.32 | convolution fusion | flops 573706240 | bytes 3060776 | tf_op jit(solution)/shard_map/conv_general_dilated | solution.py:52
  69.6 4.5 %copy.35 = f32[8,32,8,5,16]{1,4,3,2,0:T(8,128)S(1)} copy(f32[8,32,8,5,16]{4,2,3,1,0:T(8,128)} %broadcast_select_fusion.1) | data formatting | bytes 1310720 | tf_op jit(solution)/shard_map/conv_general_dilated | solution.py:52
  74.2 1.6 %slice_bitcast_fusion.1 = f32[1,16,8,32,32]{3,1,4,2,0:T(8,128)} fusion(f32[8,32,1,40,16]{1,4,3,0,2:T(8,128)S(1)} %bitcast.48), kind=kLoop, calls=%fused_computation.36 | loop fusion | bytes 1048576 | tf_op jit(solution)/shard_map/conv_general_dilated | solution.py:52
  75.7 1.9 %copy.36 = f32[1,16,8,32,32]{4,3,2,1,0:T(8,128)S(1)} copy(f32[1,16,8,32,32]{3,1,4,2,0:T(8,128)} %slice_bitcast_fusion.1) | data formatting | bytes 1048576 | tf_op jit(solution)/shard_map/conv_general_dilated | solution.py:52
  77.7 1.0 reshape_squeeze.6
  78.6 0.0 copy-done.2
  78.7 0.8 fusion.30
  79.5 0.0 all-gather.5.cloned.1.call-update
  79.5 16.9 %all-gather.5.cloned.1.call-done = bf16[64,8,1,1024]{3,1,2,0:T(8,128)(2,1)} async-done(((bf16[16,8,1,1024]{3,1,2,0:T(8,128)(2,1)}), bf16[64,8,1,1024]{3,1,2,0:T(8,128)(2,1)}) %all-gather.5.cloned.1.call-update) | async-done | bytes 1048592 | tf_op jit(solution)/shard_map/all_gather | solution.py:46
  96.4 2.4 %copy.38 = bf16[64,8,1,1024]{0,3,1,2:T(8,128)(2,1)S(1)} copy(bf16[64,8,1,1024]{3,1,2,0:T(8,128)(2,1)} %all-gather.5.cloned.1.call-done) | data formatting | bytes 2097152 | tf_op jit(solution)/shard_map/all_gather | solution.py:46
  98.7 0.3 fusion.38
  99.0 3.4 %collective-permute-start.4 = (bf16[64,8,32,1]{0,3,2,1:T(2,128)(2,1)S(1)}, bf16[64,8,32,1]{0,3,2,1:T(2,128)(2,1)S(1)}, u32[]{:S(2)}, u32[]{:S(2)}) collective-permute-start(bf16[64,8,32,1]{0,3,2,1:T(2,128)(2,1)S(1)} %get-tuple-element.9), channel_id=1, source_target_pairs={{0,4},{4,8},{8,12},{12,16},{16,20},{20,24},{24,28},{1,5},{5,9},{9,... | collective-permute-start | bytes 98312 | tf_op jit(solution)/shard_map/ppermute | solution.py:13
  102.4 1.3 collective-permute-start.5
  103.7 1.8 %collective-permute-done.4 = bf16[64,8,32,1]{0,3,2,1:T(2,128)(2,1)S(1)} collective-permute-done((bf16[64,8,32,1]{0,3,2,1:T(2,128)(2,1)S(1)}, bf16[64,8,32,1]{0,3,2,1:T(2,128)(2,1)S(1)}, u32[]{:S(2)}, u32[]{:S(2)}) %collective-permute-start.4) | collective-permute-done | bytes 32800 | tf_op jit(solution)/shard_map/ppermute | solution.py:13
  105.5 0.1 broadcast_select_fusion.4
  105.7 4.0 %collective-permute-done.5 = bf16[64,8,32,1]{0,3,2,1:T(2,128)(2,1)S(1)} collective-permute-done((bf16[64,8,32,1]{0,3,2,1:T(2,128)(2,1)S(1)}, bf16[64,8,32,1]{0,3,2,1:T(2,128)(2,1)S(1)}, u32[]{:S(2)}, u32[]{:S(2)}) %collective-permute-start.5) | collective-permute-done | bytes 32800 | tf_op jit(solution)/shard_map/ppermute | solution.py:13
  109.6 0.1 broadcast_select_fusion.2
  109.8 0.1 pad_maximum_fusion.2
  109.9 0.7 collective-permute-start.6
  110.5 0.7 collective-permute-start.7
  111.2 0.0 collective-permute-done.6
  111.2 0.0 collective-permute-done.7
  111.2 2.6 %fusion.17 = bf16[64,10,34,1,34]{0,4,2,1,3:T(8,128)(2,1)S(1)} fusion(bf16[64,8,1,34]{0,3,2,1:T(8,128)(2,1)S(1)} %collective-permute-done.7, bf16[64,8,1,34]{0,3,2,1:T(8,128)(2,1)S(1)} %collective-permute-done.6, bf16[64,8,32,1]{0,3,2,1:T(2,128)(2,1)S(1)} %broadcast_select_fusion.2, bf16[64,8,32,32]{0,3,2,1:T(8,128)(2,1)S(1)} %bitcast.45, ...), kind=kLoop, calls=%fused_computation.19 | loop fusion | flops 13317120 | bytes 2663424 | tf_op jit(solution)/shard_map/broadcast_in_dim | solution.py:53
  113.8 0.5 copy.47
  114.3 0.9 pad.11.clone
  115.2 0.0 copy-start.4
  115.3 0.5 copy.41
  115.7 0.4 slice.42
  116.1 0.1 copy-done.4
  116.1 21.2 %broadcast_select_fusion = f32[8,32,8,5,16]{4,2,3,1,0:T(8,128)} fusion(pred[8,5]{0,1:T(8,128)(4,1)S(1)} %copy-done.5, bf16[16,3,3,3,64]{4,0,3,2,1:T(8,128)(2,1)S(1)} %bitcast.52, bf16[64,10,34,1,7,2]{0,4,5,2,1,3:T(8,128)(2,1)S(1)} %slice.42, bf16[64,10,34,1,8,5]{0,4,5,2,1,3:T(8,128)(2,1)S(1)} %copy.41), kind=kOutput, calls=%fused_computation.31 | convolution fusion | flops 573706240 | bytes 3060776 | tf_op jit(solution)/shard_map/conv_general_dilated | solution.py:52
  137.4 4.5 %copy.42 = f32[8,32,8,5,16]{1,4,3,2,0:T(8,128)S(1)} copy(f32[8,32,8,5,16]{4,2,3,1,0:T(8,128)} %broadcast_select_fusion) | data formatting | bytes 1310720 | tf_op jit(solution)/shard_map/conv_general_dilated | solution.py:52
  141.9 1.6 %slice_bitcast_fusion = f32[1,16,8,32,32]{3,1,4,2,0:T(8,128)} fusion(f32[8,32,1,40,16]{1,4,3,0,2:T(8,128)S(1)} %bitcast.49), kind=kLoop, calls=%fused_computation.35 | loop fusion | bytes 1048576 | tf_op jit(solution)/shard_map/conv_general_dilated | solution.py:52
  143.5 1.9 %copy.43 = f32[1,16,8,32,32]{4,3,2,1,0:T(8,128)S(1)} copy(f32[1,16,8,32,32]{3,1,4,2,0:T(8,128)} %slice_bitcast_fusion) | data formatting | bytes 1048576 | tf_op jit(solution)/shard_map/conv_general_dilated | solution.py:52
  145.4 1.0 reshape_squeeze.7
  146.4 0.0 copy-done.3
  146.4 0.8 fusion.31
  (4 shorter events, 0.0 us)
Async XLA Ops:
  6.5 41.6 %copy-start = (bf16[16,27,64]{2,0,1:T(8,128)(2,1)S(1)}, bf16[16,27,64]{2,0,1:T(8,128)(2,1)}, u32[]{:S(2)}) copy-start(bf16[16,27,64]{2,0,1:T(8,128)(2,1)} %param.8) | copy-start | bytes 165892
  6.5 36.7 %copy-start.1 = (s32[8,1,1024]{2,1,0:T(1,128)S(1)}, s32[8,1,1024]{2,1,0:T(1,128)}, u32[]{:S(2)}) copy-start(s32[8,1,1024]{2,1,0:T(1,128)} %param.7) | copy-start | bytes 98308
  6.5 21.8 %all-gather.3.cloned.1.call-start = ((), (), s32[]{:S(2)}) async-start(), calls=%async_computation | async-start | bytes 1310720 | tf_op jit(solution)/shard_map/all_gather | solution.py:46
  7.3 89.1 %all-gather.5.cloned.1.call-start = ((), (), s32[]{:S(2)}) async-start(), calls=%async_computation.1 | async-start | bytes 1310720 | tf_op jit(solution)/shard_map/all_gather | solution.py:46
  31.0 6.5 %collective-permute-start = (bf16[64,8,32,1]{0,3,2,1:T(2,128)(2,1)S(1)}, bf16[64,8,32,1]{0,3,2,1:T(2,128)(2,1)S(1)}, u32[]{:S(2)}, u32[]{:S(2)}) collective-permute-start(bf16[64,8,32,1]{0,3,2,1:T(2,128)(2,1)S(1)} %get-tuple-element.11), channel_id=1, source_target_pairs={{0,4},{4,8},{8,12},{12,16},{16,20},{20,24},{24,28},{1,5},{5,9},{9,... | collective-permute-start | bytes 98312 | tf_op jit(solution)/shard_map/ppermute | solution.py:13
  34.4 7.2 %collective-permute-start.1 = (bf16[64,8,32,1]{0,3,2,1:T(2,128)(2,1)S(1)}, bf16[64,8,32,1]{0,3,2,1:T(2,128)(2,1)S(1)}, u32[]{:S(2)}, u32[]{:S(2)}) collective-permute-start(bf16[64,8,32,1]{0,3,2,1:T(2,128)(2,1)S(1)} %get-tuple-element.12), channel_id=1, source_target_pairs={{4,0},{8,4},{12,8},{16,12},{20,16},{24,20},{28,24},{5,1},{9,5},{13... | collective-permute-start | bytes 98312 | tf_op jit(solution)/shard_map/ppermute | solution.py:13
  41.9 1.4 collective-permute-start.2
  42.6 0.7 collective-permute-start.3
  47.3 0.9 copy-start.5
  75.7 2.9 %copy-start.2 = (f32[16]{0:T(128)S(1)}, f32[16]{0:T(128)}, u32[]{:S(2)}) copy-start(f32[16]{0:T(128)} %param.9) | copy-start | bytes 196
  99.0 6.5 %collective-permute-start.4 = (bf16[64,8,32,1]{0,3,2,1:T(2,128)(2,1)S(1)}, bf16[64,8,32,1]{0,3,2,1:T(2,128)(2,1)S(1)}, u32[]{:S(2)}, u32[]{:S(2)}) collective-permute-start(bf16[64,8,32,1]{0,3,2,1:T(2,128)(2,1)S(1)} %get-tuple-element.9), channel_id=1, source_target_pairs={{0,4},{4,8},{8,12},{12,16},{16,20},{20,24},{24,28},{1,5},{5,9},{9,... | collective-permute-start | bytes 98312 | tf_op jit(solution)/shard_map/ppermute | solution.py:13
  102.4 7.2 %collective-permute-start.5 = (bf16[64,8,32,1]{0,3,2,1:T(2,128)(2,1)S(1)}, bf16[64,8,32,1]{0,3,2,1:T(2,128)(2,1)S(1)}, u32[]{:S(2)}, u32[]{:S(2)}) collective-permute-start(bf16[64,8,32,1]{0,3,2,1:T(2,128)(2,1)S(1)} %get-tuple-element.10), channel_id=1, source_target_pairs={{4,0},{8,4},{12,8},{16,12},{20,16},{24,20},{28,24},{5,1},{9,5},{13... | collective-permute-start | bytes 98312 | tf_op jit(solution)/shard_map/ppermute | solution.py:13
  109.9 1.3 collective-permute-start.6
  110.5 0.7 collective-permute-start.7
  115.2 0.9 copy-start.4
  143.5 2.9 %copy-start.3 = (f32[16]{0:T(128)S(1)}, f32[16]{0:T(128)}, u32[]{:S(2)}) copy-start(f32[16]{0:T(128)} %param.11) | copy-start | bytes 196
Sparse Core Ops, SparseCore 0:
  8.9 19.4 all-gather.2
  79.6 16.6 all-gather.4
where the time goes:
time: 154 us
  waiting for transfers between devices  50.3 us (33%)
  matrix products  42.7 us (28%)
  local copies, waits for them, and re-layouts  27.7 us (18%)
  between operations  13.7 us (9%)
  starting transfers between devices  12 us (8%)
  other arithmetic  7.67 us (5%)
    conv_general_dilated x2, matrix products, convolve(): lax.conv_general_dilated(framed[None], kernel_of(weight), (1, 1, 1), 'VAL...  42.7 us
    all_gather x2, waiting for transfers between devices, padded_inputs(): whole = lax.all_gather(field, 'ch', axis=0, tiled=True)  37.9 us
    conv_general_dilated x10, local copies, waits for them, and re-layouts, convolve(): lax.conv_general_dilated(framed[None], kernel_of(weight), (1, 1, 1), 'VAL...  17.7 us
    ppermute x8, starting transfers between devices, passed_along(): return lax.ppermute(block, axis, route)  12 us
    ppermute x8, waiting for transfers between devices, passed_along(): return lax.ppermute(block, axis, route)  11.6 us
    broadcast_in_dim x2, other arithmetic, convolve(): framed[None]  5.23 us
    all_gather x2, local copies, waits for them, and re-layouts, padded_inputs(): whole = lax.all_gather(field, 'ch', axis=0, tiled=True)  4.72 us
  transfers between devices with their start and end apart: 10, of which 6 were waited for; matrix products, arithmetic and copies ran while one was open for 0% of the time, Pallas kernels for 0%

commit v1 on v0

v1 whole, which is shorter than its diff:
```python
import functools

import jax
import jax.numpy as jnp
import numpy as np
from jax import lax
from jax.experimental import pallas as pl
from jax.experimental.pallas import tpu as pltpu
from jax.sharding import PartitionSpec as P

CY = 32
CZ = 32
PITCH = CZ + 4
BF = jnp.bfloat16
F32 = jnp.float32


def frame_sources(rows, lanes):
    sources = np.full(lanes, -1)
    for lane in range(PITCH * (CY + 2 * rows)):
        y, z = lane // PITCH - rows, lane % PITCH - 2
        if 0 <= y < CY:
            if 0 <= z < CZ:
                sources[lane] = CZ * y + z
            elif z >= CZ:
                sources[lane] = 1024 + 2 * y + z - CZ
            else:
                sources[lane] = 1024 + 64 + 2 * y + z + 2
        elif rows == 2:
            sources[lane] = 1024 + (128 + PITCH * (y + 2) if y < 0 else 256 + PITCH * (y - CY)) + z + 2
    return sources


def windows(sources, limit, tile=256):
    spans = []
    for start in range(0, len(sources), tile):
        part = sources[start : start + tile]
        part = part[(part >= 0) & (part < limit)]
        low = int(part.min()) // 128 * 128 if len(part) else 0
        high = -(-(int(part.max()) + 1) // 128) * 128 if len(part) else 128
        spans.append((start, min(tile, len(sources) - start), low, high))
    return spans


def one_hot(sources, count):
    return (np.arange(count)[:, None] == sources[None, :]).astype(np.float32)


def dot(a, b):
    return jnp.dot(a, b, preferred_element_type=F32)


def roll(x, shift):
    n = x.shape[1]
    return x if shift % n == 0 else pltpu.roll(x, (-shift) % n, 1)


def swap_rows(outer, inner):
    row = lax.broadcasted_iota(jnp.int32, (128, 128), 0)
    col = lax.broadcasted_iota(jnp.int32, (128, 128), 1)
    return ((row % outer) * inner + row // outer == col).astype(F32).astype(BF)


def pack_kernel(f_ref, mask_ref, select_ref, halo_ref):
    opened = jnp.concatenate([(1 - mask_ref[x]).astype(F32) for x in range(8)] + [jnp.zeros((8, 1024), F32)], 0)
    halo_ref[0:128] = dot(f_ref[...], select_ref[...]).astype(BF)
    halo_ref[128:144] = dot(opened.astype(BF), select_ref[...]).astype(BF)


def main_kernel(rows, spans, back, me_ref, f0, f1, f2, f3, h0, h1, h2, h3, w0, w1, w2, w3, mask_ref, mask_halo, own, bias_ref,
                frame_ref, halo_frame_ref, back_ref, out_ref, field, hidden, first, second, bias_one, opened, last):
    lanes = opened.shape[1]
    me = me_ref[0]
    to_plane = swap_rows(16, 8)
    zero = jnp.zeros((192, lanes), BF)
    field[0:192] = zero
    field[9 * 192 : 10 * 192] = zero
    hidden[0:64] = zero[0:64]
    hidden[9 * 64 : 10 * 64] = zero[0:64]

    def framed(cells, halo):
        parts = []
        for start, size, low, high in spans:
            part = dot(halo, halo_frame_ref[:, start : start + size])
            part += dot(cells[:, low:high], frame_ref[low:high, start : start + size])
            parts.append(part)
        return jnp.concatenate(parts, 1)

    cells_open = jnp.concatenate([(1 - mask_ref[x]).astype(F32) for x in range(8)] + [jnp.zeros((8, 1024), F32)], 0)
    opened[...] = framed(cells_open.astype(BF), mask_halo[...])

    for k, (f, h, w) in enumerate(((f0, h0, w0), (f1, h1, w1), (f2, h2, w2), (f3, h3, w3))):
        base = pl.multiple_of((me ^ k) * 16, 16)
        planes = dot(to_plane, framed(f[...], h[...]).astype(BF))
        for e in range(3):
            moved = roll(planes, e - 1).astype(BF)
            for x in range(8):
                field[pl.ds(192 * (x + 1) + 64 * e + base, 16)] = moved[16 * x : 16 * x + 16]

        def tap(t):
            block = w[16 * (t % 14) : 16 * (t % 14) + 16]
            return block[:, 0:64] if t < 14 else block[:, 64:128]

        blank = jnp.zeros((16, 192), BF)
        for b in range(3):
            taps = [tap(9 * a + 3 * b + e) for a in range(3) for e in range(3)]
            first[pl.ds(128 * b + base, 16)] = jnp.concatenate(taps + [blank], 1)
            first[pl.ds(128 * b + 64 + base, 16)] = jnp.concatenate([blank] + taps, 1)
        tail = w[16 * 13 : 16 * 14].astype(F32)
        total = tail[:, 64:65] + tail[:, 65:66] + tail[:, 66:67]
        bias_one[pl.ds(base, 16)] = jnp.broadcast_to(total, (16, 128))

    blank = jnp.zeros((16, 64), BF)
    for b in range(3):
        for e in range(3):
            taps = [own[9 * a + 3 * b + e] for a in range(3)]
            row = 32 * (3 * b + e)
            second[row : row + 16] = jnp.concatenate(taps + [blank], 1)
            second[row + 16 : row + 32] = jnp.concatenate([blank] + taps, 1)

    column = bias_one[:, 0:1]
    for q in range(4):
        sums = dot(first[...], field[384 * q : 384 * q + 768])
        total = roll(sums[0:128], -PITCH) + sums[128:256] + roll(sums[256:384], PITCH)
        for half in range(2):
            x = 2 * q + half
            value = jnp.maximum(total[64 * half : 64 * half + 64] + column, 0.0) * opened[x : x + 1]
            hidden[64 * (x + 1) : 64 * (x + 2)] = value.astype(BF)

    column = jnp.broadcast_to(bias_ref[...], (16, 128))[:, 0:1]
    for q in range(4):
        sums = dot(second[...], hidden[128 * q : 128 * q + 256])
        total = sums[32 * 4 : 32 * 5]
        for b in range(3):
            for e in range(3):
                if (b, e) != (1, 1):
                    row = 32 * (3 * b + e)
                    total += roll(sums[row : row + 32], PITCH * (b - 1) + e - 1)
        for half in range(2):
            x = 2 * q + half
            value = jnp.maximum(total[16 * half : 16 * half + 16] + column, 0.0) * opened[x : x + 1]
            last[16 * x : 16 * x + 16] = value.astype(BF)

    parts = [dot(last[:, low:high], back_ref[low:high, start : start + size]) for start, size, low, high in back]
    cells = jnp.concatenate(parts, 1).astype(BF)
    out_ref[...] = dot(swap_rows(8, 16), cells).astype(BF)


def on_device(features, solid_mask, weight_one, bias_one, weight_two, bias_two):
    columns = lax.axis_size("col")
    grid_z = min(8, columns)
    grid_y = columns // grid_z
    rows = 1 if grid_y == 1 else 2
    lanes = -(-PITCH * (CY + 2 * rows) // 128) * 128
    me = lax.axis_index("ch").astype(jnp.int32).reshape(1)

    def across(v, bit):
        return lax.ppermute(v, "ch", [(i, i ^ bit) for i in range(lax.axis_size("ch"))])

    def along_z(v, step):
        route = [(c, c + step) for c in range(columns) if 0 <= c % grid_z + step < grid_z]
        return lax.ppermute(v, "col", route)

    def along_y(v, step):
        route = [(c, c + step * grid_z) for c in range(columns) if 0 <= c // grid_z + step < grid_y]
        return lax.ppermute(v, "col", route)

    cells = features.reshape(128, 1024)
    far = across(cells, 2)
    near = across(cells, 1)

    taps = weight_one.transpose(1, 0, 2)
    high = bias_one.astype(BF)
    rest = bias_one - high.astype(F32)
    middle = rest.astype(BF)
    low = (rest - middle.astype(F32)).astype(BF)
    terms = jnp.pad(jnp.stack([high, middle, low], 1), ((0, 0), (0, 61)))
    weights = jnp.concatenate([taps[:14], jnp.concatenate([taps[14:], terms[None]], 0)], 2).reshape(224, 128)

    edge = np.array([32 * (n // 2) + n % 2 + (30 if n >= 64 else 0) - (1024 if n >= 64 else 0) for n in range(128)])
    select = jnp.asarray(one_hot(edge, 1024), BF)
    rims = pl.pallas_call(
        pack_kernel,
        out_shape=jax.ShapeDtypeStruct((144, 128), BF),
        compiler_params=pltpu.CompilerParams(vmem_limit_bytes=32 << 20),
        name="pack",
    )(cells, solid_mask, select)
    after, before = along_z(rims, -1), along_z(rims, 1)
    side = lax.broadcasted_iota(jnp.int32, (144, 128), 1)
    halo = jnp.where(side < 64, after, before)
    if grid_y > 1:
        opened = (1 - solid_mask).astype(BF).reshape(8, 1024)
        whole = jnp.concatenate([cells, opened, jnp.zeros((8, 1024), BF)], 0).reshape(144, CY, CZ)
        upper = halo[:, :64].reshape(144, CY, 2)
        lower = halo[:, 64:].reshape(144, CY, 2)
        wide = jnp.concatenate([lower, whole, upper], 2)
        south = along_y(wide[:, CY - 2 :], 1).reshape(144, 2 * PITCH)
        north = along_y(wide[:, :2], -1).reshape(144, 2 * PITCH)
        edges = [jnp.pad(v, ((0, 0), (0, 128 - 2 * PITCH))) for v in (south, north)]
        halo = jnp.concatenate([halo] + edges, 1)
    mask_halo = halo[128:]
    halo = halo[:128]

    halo_far, weights_far = across(halo, 2), across(weights, 2)
    halo_near, weights_near = across(halo, 1), across(weights, 1)
    cross = across(far, 1)
    halo_cross, weights_cross = across(halo_far, 1), across(weights_far, 1)

    sources = frame_sources(rows, lanes)
    frame = jnp.asarray(one_hot(sources, 1024), BF)
    halo_frame = jnp.asarray(one_hot(sources - 1024, halo.shape[1]), BF)
    back_sources = np.array([PITCH * (n // CZ + rows) + n % CZ + 2 for n in range(1024)])
    back = jnp.asarray(one_hot(back_sources, lanes), BF)

    vmem = pl.BlockSpec(memory_space=pltpu.VMEM)
    result = pl.pallas_call(
        functools.partial(main_kernel, rows, windows(sources, 1024), windows(back_sources, lanes)),
        out_shape=jax.ShapeDtypeStruct((128, 1024), BF),
        in_specs=[pl.BlockSpec(memory_space=pltpu.SMEM)] + [vmem] * 19,
        out_specs=vmem,
        scratch_shapes=[
            pltpu.VMEM((10 * 192, lanes), BF),
            pltpu.VMEM((10 * 64, lanes), BF),
            pltpu.VMEM((384, 768), BF),
            pltpu.VMEM((288, 256), BF),
            pltpu.VMEM((64, 128), F32),
            pltpu.VMEM((16, lanes), F32),
            pltpu.VMEM((128, lanes), BF),
        ],
        compiler_params=pltpu.CompilerParams(vmem_limit_bytes=48 << 20),
        name="layers",
    )(
        me, cells, near, far, cross, halo, halo_near, halo_far, halo_cross,
        weights, weights_near, weights_far, weights_cross, solid_mask, mask_halo,
        weight_two.transpose(1, 0, 2), bias_two.reshape(16, 1), frame, halo_frame, back,
    )
    return result.reshape(16, 8, 1, 1024)


def solution(mesh):
    in_specs = (
        P("ch", None, "col", None),
        P(None, "col", None),
        P("ch", None, None),
        P("ch"),
        P("ch", None, None),
        P("ch"),
    )
    out_specs = P("ch", None, "col", None)
    return jax.shard_map(
        on_device, mesh=mesh, in_specs=in_specs, out_specs=out_specs, check_vma=False
    )
```

time: 154 us -> 38.6 us (0.25)
  the two profiles are of different devices: /device:TPU:0 before, /device:TPU:25 now
where the time goes in v1:
time: 38.6 us; the launch traced here: 38 us
  starting transfers between devices  15.3 us (40%)
  Pallas kernels  11.2 us (29%)
  local copies, waits for them, and re-layouts  8.52 us (22%)
  waiting for transfers between devices  1.98 us (5%)
  other arithmetic  0.86 us (2%)
    pallas_call x1, Pallas kernels, on_device(): pl.pallas_call(functools.partial(main_kernel, rows, windows(sources, 1024...  10 us
    ppermute x9, starting transfers between devices, across(): lax.ppermute(v, 'ch', [(i, i ^ bit) for i in range(lax.axis_size('ch'))])  9.17 us
    ppermute x2, starting transfers between devices, along_z(): return lax.ppermute(v, 'col', route)  6.18 us
    unnamed x12, local copies, waits for them, and re-layouts  6.07 us
    ppermute x9, waiting for transfers between devices, across(): lax.ppermute(v, 'ch', [(i, i ^ bit) for i in range(lax.axis_size('ch'))])  1.98 us
    pallas_call x1, Pallas kernels, on_device(): pl.pallas_call(pack_kernel, out_shape=jax.ShapeDtypeStruct((144, 128), BF...  1.19 us
    slice x1, local copies, waits for them, and re-layouts, on_device(): taps[:14]  0.82 us
    slice x1, local copies, waits for them, and re-layouts, on_device(): taps[14:]  0.82 us
  transfers between devices with their start and end apart: 11, of which 3 were waited for; matrix products, arithmetic and copies ran while one was open for 9% of the time, Pallas kernels for 0%

profile of v1, /device:TPU:25, one launch (start us, length us, event | category | flops | bytes accessed | tf_op | source)
XLA Modules:
  0.0 38.0 jit_solution(15030405066174281952)
XLA Ops:
  0.0 0.0 copy-start.2
  0.0 0.9 %copy-done.2 = bf16[1024,128]{1,0:T(8,128)(2,1)S(1)} copy-done((bf16[1024,128]{1,0:T(8,128)(2,1)S(1)}, bf16[1024,128]{1,0:T(8,128)(2,1)}, u32[]{:S(2)}) %copy-start.2) | copy-done | bytes 262168
  1.0 0.0 copy-start.3
  1.0 0.8 %copy-done.3 = s32[8,1,1024]{2,1,0:T(1,128)S(1)} copy-done((s32[8,1,1024]{2,1,0:T(1,128)S(1)}, s32[8,1,1024]{2,1,0:T(1,128)}, u32[]{:S(2)}) %copy-start.3) | copy-done | bytes 32792
  1.7 1.2 %pack.1 = bf16[144,128]{1,0:T(8,128)(2,1)S(1)} custom-call(bf16[128,1024]{1,0:T(8,128)(2,1)} %bitcast.1.f_ref.f0, s32[8,1,1024]{2,1,0:T(1,128)S(1)} %copy-done.3, bf16[1024,128]{1,0:T(8,128)(2,1)S(1)} %copy-done.2), custom_call_target="tpu_custom_call" | custom-call | tf_op jit(solution)/shard_map/pack/pallas_call | solution.py:182
  2.9 3.1 %collective-permute-start.4 = (bf16[144,128]{1,0:T(8,128)(2,1)S(1)}, bf16[144,128]{1,0:T(8,128)(2,1)S(1)}, u32[]{:S(2)}, u32[]{:S(2)}) collective-permute-start(bf16[144,128]{1,0:T(8,128)(2,1)S(1)} %pack.1), channel_id=1, source_target_pairs={{0,4},{4,8},{8,12},{12,16},{16,20},{20,24},{24,28},{1,5},{5,9},{9,... | collective-permute-start | bytes 110600 | tf_op jit(solution)/shard_map/ppermute | solution.py:162
  6.0 3.0 %collective-permute-start.3 = (bf16[144,128]{1,0:T(8,128)(2,1)S(1)}, bf16[144,128]{1,0:T(8,128)(2,1)S(1)}, u32[]{:S(2)}, u32[]{:S(2)}) collective-permute-start(bf16[144,128]{1,0:T(8,128)(2,1)S(1)} %pack.1), channel_id=1, source_target_pairs={{4,0},{8,4},{12,8},{16,12},{20,16},{24,20},{28,24},{5,1},{9,5},{13... | collective-permute-start | bytes 110600 | tf_op jit(solution)/shard_map/ppermute | solution.py:162
  9.1 1.3 %collective-permute-start.1 = (bf16[128,1024]{1,0:T(8,128)(2,1)}, bf16[128,1024]{1,0:T(8,128)(2,1)S(1)}, u32[]{:S(2)}, u32[]{:S(2)}) collective-permute-start(bf16[128,1024]{1,0:T(8,128)(2,1)} %bitcast.1.f_ref.f0), channel_id=1, source_target_pairs={{0,2},{1,3},{2,0},{3,1},{4,6},{5,7},{6,4},{7,5},{8,10},{9,11},{10,... | collective-permute-start | bytes 786440 | tf_op jit(solution)/shard_map/ppermute | solution.py:158
  10.4 0.7 %convert_bitcast_fusion.2 = (bf16[16,1]{0,1:T(2,128)(2,1)S(1)}, bf16[16,1]{0,1:T(2,128)(2,1)S(1)}, bf16[16,1]{0,1:T(2,128)(2,1)S(1)}) fusion(f32[16]{0:T(128)} %param.13), kind=kLoop, calls=%fused_computation.12 | loop fusion | flops 112 | bytes 160 | tf_op jit(solution)/shard_map/stack | solution.py:177
  11.1 0.8 %slice.18 = bf16[13,16,64]{2,1,0:T(8,128)(2,1)S(1)} slice(bf16[27,16,64]{2,1,0:T(8,128)(2,1)} %bitcast.21), slice={[14:27], [0:16], [0:64]} | slice | bytes 53248 | tf_op jit(solution)/shard_map/slice | solution.py:178
  11.9 0.8 %slice.17 = bf16[14,16,64]{2,1,0:T(8,128)(2,1)S(1)} slice(bf16[27,16,64]{2,1,0:T(8,128)(2,1)} %bitcast.22), slice={[0:14], [0:16], [0:64]} | slice | bytes 57344 | tf_op jit(solution)/shard_map/slice | solution.py:178
  12.8 0.1 copy.11
  12.8 0.1 maximum_maximum_fusion
  12.9 0.3 collective-permute-start.9
  13.3 1.8 %collective-permute-start.8 = (bf16[224,128]{1,0:T(8,128)(2,1)S(1)}, bf16[224,128]{1,0:T(8,128)(2,1)S(1)}, u32[]{:S(2)}, u32[]{:S(2)}) collective-permute-start(bf16[224,128]{1,0:T(8,128)(2,1)S(1)} %bitcast.18), channel_id=1, source_target_pairs={{0,1},{1,0},{2,3},{3,2},{4,5},{5,4},{6,7},{7,6},{8,9},{9,8},{10,11... | collective-permute-start | bytes 172040 | tf_op jit(solution)/shard_map/ppermute | solution.py:158
  15.1 0.0 collective-permute-done.4
  15.1 0.1 collective-permute-start
  15.1 0.8 %collective-permute-done.1.f2 = bf16[128,1024]{1,0:T(8,128)(2,1)S(1)} collective-permute-done((bf16[128,1024]{1,0:T(8,128)(2,1)}, bf16[128,1024]{1,0:T(8,128)(2,1)S(1)}, u32[]{:S(2)}, u32[]{:S(2)}) %collective-permute-start.1) | collective-permute-done | bytes 262176 | tf_op jit(solution)/shard_map/ppermute | solution.py:158
  15.9 2.8 %collective-permute-start.2 = (bf16[128,1024]{1,0:T(8,128)(2,1)S(1)}, bf16[128,1024]{1,0:T(8,128)(2,1)S(1)}, u32[]{:S(2)}, u32[]{:S(2)}) collective-permute-start(bf16[128,1024]{1,0:T(8,128)(2,1)S(1)} %collective-permute-done.1.f2), channel_id=1, source_target_pairs={{0,1},{1,0},{2,3},{3,2},{4,5},{5,4},{6,7},{7,6},{8,9},{9,8},{10,11... | collective-permute-start | bytes 786440 | tf_op jit(solution)/shard_map/ppermute | solution.py:158
  18.7 0.0 collective-permute-done.3
  18.7 1.3 %collective-permute-start.6 = (bf16[128,128]{1,0:T(8,128)(2,1)S(1)}, bf16[128,128]{1,0:T(8,128)(2,1)S(1)}, u32[]{:S(2)}, u32[]{:S(2)}) collective-permute-start(bf16[128,128]{1,0:T(8,128)(2,1)S(1)} %slice.16.h0), channel_id=1, source_target_pairs={{0,2},{1,3},{2,0},{3,1},{4,6},{5,7},{6,4},{7,5},{8,10},{9,11},{10,... | collective-permute-start | bytes 98312 | tf_op jit(solution)/shard_map/ppermute | solution.py:158
  20.0 0.0 collective-permute-done.9.w2
  20.0 0.3 collective-permute-start.10
  20.3 0.0 collective-permute-done.8.w1
  20.3 0.2 collective-permute-start.5
  20.5 1.0 %collective-permute-done.6.h2 = bf16[128,128]{1,0:T(8,128)(2,1)S(1)} collective-permute-done((bf16[128,128]{1,0:T(8,128)(2,1)S(1)}, bf16[128,128]{1,0:T(8,128)(2,1)S(1)}, u32[]{:S(2)}, u32[]{:S(2)}) %collective-permute-start.6) | collective-permute-done | bytes 32800 | tf_op jit(solution)/shard_map/ppermute | solution.py:158
  21.6 1.2 %collective-permute-start.7 = (bf16[128,128]{1,0:T(8,128)(2,1)S(1)}, bf16[128,128]{1,0:T(8,128)(2,1)S(1)}, u32[]{:S(2)}, u32[]{:S(2)}) collective-permute-start(bf16[128,128]{1,0:T(8,128)(2,1)S(1)} %collective-permute-done.6.h2), channel_id=1, source_target_pairs={{0,1},{1,0},{2,3},{3,2},{4,5},{5,4},{6,7},{7,6},{8,9},{9,8},{10,11... | collective-permute-start | bytes 98312 | tf_op jit(solution)/shard_map/ppermute | solution.py:158
  22.7 0.7 %copy.12.bias_ref = f32[16,1]{1,0:T(8,128)S(1)} copy(f32[16,1]{0,1:T(1,128)} %bitcast.23) | data formatting | bytes 128 | tf_op jit(solution)/shard_map/reshape | solution.py:235
  23.4 0.0 collective-permute-done.5.h1
  23.5 0.1 collective-permute-done.7.h3
  23.6 0.0 collective-permute-done.10.w3
  23.6 0.0 collective-permute-done.f1
  23.6 0.0 collective-permute-done.2.f3
  23.6 0.0 copy-start
  23.6 1.7 %copy-done = bf16[1024,1280]{1,0:T(8,128)(2,1)S(1)} copy-done((bf16[1024,1280]{1,0:T(8,128)(2,1)S(1)}, bf16[1024,1280]{1,0:T(8,128)(2,1)}, u32[]{:S(2)}) %copy-start) | copy-done | bytes 2621464
  25.3 0.0 copy-start.1
  25.3 1.0 %copy-done.1 = bf16[128,1280]{1,0:T(8,128)(2,1)S(1)} copy-done((bf16[128,1280]{1,0:T(8,128)(2,1)S(1)}, bf16[128,1280]{1,0:T(8,128)(2,1)}, u32[]{:S(2)}) %copy-start.1) | copy-done | bytes 327704
  26.3 0.0 copy-start.4
  26.3 0.8 %copy-done.4 = s32[8,1,1024]{2,1,0:T(1,128)S(1)} copy-done((s32[8,1,1024]{2,1,0:T(1,128)S(1)}, s32[8,1,1024]{2,1,0:T(1,128)}, u32[]{:S(2)}) %copy-start.4) | copy-done | bytes 32792
  27.1 0.0 copy-start.5
  27.1 0.9 %copy-done.5 = bf16[16,27,64]{2,0,1:T(8,128)(2,1)S(1)} copy-done((bf16[16,27,64]{2,0,1:T(8,128)(2,1)S(1)}, bf16[16,27,64]{2,0,1:T(8,128)(2,1)}, u32[]{:S(2)}) %copy-start.5) | copy-done | bytes 55320
  28.0 10.0 %layers.1 = bf16[128,1024]{1,0:T(8,128)(2,1)} custom-call(s32[1]{0:T(128)} %bitcast.me_ref, bf16[128,1024]{1,0:T(8,128)(2,1)} %bitcast.1.f_ref.f0, bf16[128,1024]{1,0:T(8,128)(2,1)S(1)} %collective-permute-done.f1, bf16[128,1024]{1,0:T(8,128)(2,1)S(1)} %collective-permute-done.1.f2, bf16[128,1024]{1,0:T(8,128)(2,1)S(1)} %collective-permute-done.2.f3, ...), custom_call_target="tpu_custom_call" | custom-call | tf_op jit(solution)/shard_map/layers/pallas_call | solution.py:216
  (5 shorter events, 0.0 us)
Async XLA Ops:
  0.0 0.9 %copy-start.2 = (bf16[1024,128]{1,0:T(8,128)(2,1)S(1)}, bf16[1024,128]{1,0:T(8,128)(2,1)}, u32[]{:S(2)}) copy-start(bf16[1024,128]{1,0:T(8,128)(2,1)} %constant.17.clone.select_ref) | copy-start | bytes 786436
  1.0 0.8 %copy-start.3 = (s32[8,1,1024]{2,1,0:T(1,128)S(1)}, s32[8,1,1024]{2,1,0:T(1,128)}, u32[]{:S(2)}) copy-start(s32[8,1,1024]{2,1,0:T(1,128)} %mask_ref.3) | copy-start | bytes 98308
  2.9 12.2 %collective-permute-start.4 = (bf16[144,128]{1,0:T(8,128)(2,1)S(1)}, bf16[144,128]{1,0:T(8,128)(2,1)S(1)}, u32[]{:S(2)}, u32[]{:S(2)}) collective-permute-start(bf16[144,128]{1,0:T(8,128)(2,1)S(1)} %pack.1), channel_id=1, source_target_pairs={{0,4},{4,8},{8,12},{12,16},{16,20},{20,24},{24,28},{1,5},{5,9},{9,... | collective-permute-start | bytes 110600 | tf_op jit(solution)/shard_map/ppermute | solution.py:162
  6.0 12.7 %collective-permute-start.3 = (bf16[144,128]{1,0:T(8,128)(2,1)S(1)}, bf16[144,128]{1,0:T(8,128)(2,1)S(1)}, u32[]{:S(2)}, u32[]{:S(2)}) collective-permute-start(bf16[144,128]{1,0:T(8,128)(2,1)S(1)} %pack.1), channel_id=1, source_target_pairs={{4,0},{8,4},{12,8},{16,12},{20,16},{24,20},{28,24},{5,1},{9,5},{13... | collective-permute-start | bytes 110600 | tf_op jit(solution)/shard_map/ppermute | solution.py:162
  9.1 6.8 %collective-permute-start.1 = (bf16[128,1024]{1,0:T(8,128)(2,1)}, bf16[128,1024]{1,0:T(8,128)(2,1)S(1)}, u32[]{:S(2)}, u32[]{:S(2)}) collective-permute-start(bf16[128,1024]{1,0:T(8,128)(2,1)} %bitcast.1.f_ref.f0), channel_id=1, source_target_pairs={{0,2},{1,3},{2,0},{3,1},{4,6},{5,7},{6,4},{7,5},{8,10},{9,11},{10,... | collective-permute-start | bytes 786440 | tf_op jit(solution)/shard_map/ppermute | solution.py:158
  12.9 7.1 %collective-permute-start.9 = (bf16[224,128]{1,0:T(8,128)(2,1)S(1)}, bf16[224,128]{1,0:T(8,128)(2,1)S(1)}, u32[]{:S(2)}, u32[]{:S(2)}) collective-permute-start(bf16[224,128]{1,0:T(8,128)(2,1)S(1)} %bitcast.17), channel_id=1, source_target_pairs={{0,2},{1,3},{2,0},{3,1},{4,6},{5,7},{6,4},{7,5},{8,10},{9,11},{10,... | collective-permute-start | bytes 172040 | tf_op jit(solution)/shard_map/ppermute | solution.py:158
  13.3 7.0 %collective-permute-start.8 = (bf16[224,128]{1,0:T(8,128)(2,1)S(1)}, bf16[224,128]{1,0:T(8,128)(2,1)S(1)}, u32[]{:S(2)}, u32[]{:S(2)}) collective-permute-start(bf16[224,128]{1,0:T(8,128)(2,1)S(1)} %bitcast.18), channel_id=1, source_target_pairs={{0,1},{1,0},{2,3},{3,2},{4,5},{5,4},{6,7},{7,6},{8,9},{9,8},{10,11... | collective-permute-start | bytes 172040 | tf_op jit(solution)/shard_map/ppermute | solution.py:158
  15.1 8.5 %collective-permute-start = (bf16[128,1024]{1,0:T(8,128)(2,1)}, bf16[128,1024]{1,0:T(8,128)(2,1)S(1)}, u32[]{:S(2)}, u32[]{:S(2)}) collective-permute-start(bf16[128,1024]{1,0:T(8,128)(2,1)} %bitcast.1.f_ref.f0), channel_id=1, source_target_pairs={{0,1},{1,0},{2,3},{3,2},{4,5},{5,4},{6,7},{7,6},{8,9},{9,8},{10,11... | collective-permute-start | bytes 786440 | tf_op jit(solution)/shard_map/ppermute | solution.py:158
  15.9 7.7 %collective-permute-start.2 = (bf16[128,1024]{1,0:T(8,128)(2,1)S(1)}, bf16[128,1024]{1,0:T(8,128)(2,1)S(1)}, u32[]{:S(2)}, u32[]{:S(2)}) collective-permute-start(bf16[128,1024]{1,0:T(8,128)(2,1)S(1)} %collective-permute-done.1.f2), channel_id=1, source_target_pairs={{0,1},{1,0},{2,3},{3,2},{4,5},{5,4},{6,7},{7,6},{8,9},{9,8},{10,11... | collective-permute-start | bytes 786440 | tf_op jit(solution)/shard_map/ppermute | solution.py:158
  18.7 2.8 %collective-permute-start.6 = (bf16[128,128]{1,0:T(8,128)(2,1)S(1)}, bf16[128,128]{1,0:T(8,128)(2,1)S(1)}, u32[]{:S(2)}, u32[]{:S(2)}) collective-permute-start(bf16[128,128]{1,0:T(8,128)(2,1)S(1)} %slice.16.h0), channel_id=1, source_target_pairs={{0,2},{1,3},{2,0},{3,1},{4,6},{5,7},{6,4},{7,5},{8,10},{9,11},{10,... | collective-permute-start | bytes 98312 | tf_op jit(solution)/shard_map/ppermute | solution.py:158
  20.0 3.6 %collective-permute-start.10 = (bf16[224,128]{1,0:T(8,128)(2,1)S(1)}, bf16[224,128]{1,0:T(8,128)(2,1)S(1)}, u32[]{:S(2)}, u32[]{:S(2)}) collective-permute-start(bf16[224,128]{1,0:T(8,128)(2,1)S(1)} %collective-permute-done.9.w2), channel_id=1, source_target_pairs={{0,1},{1,0},{2,3},{3,2},{4,5},{5,4},{6,7},{7,6},{8,9},{9,8},{10,11... | collective-permute-start | bytes 172040 | tf_op jit(solution)/shard_map/ppermute | solution.py:158
  20.3 3.2 %collective-permute-start.5 = (bf16[128,128]{1,0:T(8,128)(2,1)S(1)}, bf16[128,128]{1,0:T(8,128)(2,1)S(1)}, u32[]{:S(2)}, u32[]{:S(2)}) collective-permute-start(bf16[128,128]{1,0:T(8,128)(2,1)S(1)} %slice.16.h0), channel_id=1, source_target_pairs={{0,1},{1,0},{2,3},{3,2},{4,5},{5,4},{6,7},{7,6},{8,9},{9,8},{10,11... | collective-permute-start | bytes 98312 | tf_op jit(solution)/shard_map/ppermute | solution.py:158
  21.6 2.0 %collective-permute-start.7 = (bf16[128,128]{1,0:T(8,128)(2,1)S(1)}, bf16[128,128]{1,0:T(8,128)(2,1)S(1)}, u32[]{:S(2)}, u32[]{:S(2)}) collective-permute-start(bf16[128,128]{1,0:T(8,128)(2,1)S(1)} %collective-permute-done.6.h2), channel_id=1, source_target_pairs={{0,1},{1,0},{2,3},{3,2},{4,5},{5,4},{6,7},{7,6},{8,9},{9,8},{10,11... | collective-permute-start | bytes 98312 | tf_op jit(solution)/shard_map/ppermute | solution.py:158
  23.6 1.7 %copy-start = (bf16[1024,1280]{1,0:T(8,128)(2,1)S(1)}, bf16[1024,1280]{1,0:T(8,128)(2,1)}, u32[]{:S(2)}) copy-start(bf16[1024,1280]{1,0:T(8,128)(2,1)} %constant.18.clone.frame_ref) | copy-start | bytes 7864324
  25.3 1.0 %copy-start.1 = (bf16[128,1280]{1,0:T(8,128)(2,1)S(1)}, bf16[128,1280]{1,0:T(8,128)(2,1)}, u32[]{:S(2)}) copy-start(bf16[128,1280]{1,0:T(8,128)(2,1)} %constant.19.clone.halo_frame_ref) | copy-start | bytes 983044
  26.3 0.8 %copy-start.4 = (s32[8,1,1024]{2,1,0:T(1,128)S(1)}, s32[8,1,1024]{2,1,0:T(1,128)}, u32[]{:S(2)}) copy-start(s32[8,1,1024]{2,1,0:T(1,128)} %mask_ref.3) | copy-start | bytes 98308
  27.1 0.9 %copy-start.5 = (bf16[16,27,64]{2,0,1:T(8,128)(2,1)S(1)}, bf16[16,27,64]{2,0,1:T(8,128)(2,1)}, u32[]{:S(2)}) copy-start(bf16[16,27,64]{2,0,1:T(8,128)(2,1)} %param.14) | copy-start | bytes 165892

commit v2 on v0

--- a/solution.py
+++ b/solution.py
@@ -1,10 +1,337 @@
 import jax
 import jax.numpy as jnp
 from jax import lax
+from jax.experimental import pallas as pl
+from jax.experimental.pallas import tpu as pltpu
 from jax.sharding import PartitionSpec as P
 
 CY = 32
 CZ = 32
+BF = jnp.bfloat16
+F32 = jnp.float32
+WHOLE = 63000000
+
+
+def iota(shape, dimension):
+    return lax.broadcasted_iota(jnp.int32, shape, dimension)
+
+
+def dot(a, b):
+    return jnp.dot(a, b, preferred_element_type=F32)
+
+
+def roll(x, shift):
+    n = x.shape[1]
+    return x if shift % n == 0 else pltpu.roll(x, (-shift) % n, 1)
+
+
+def swap_rows(outer, inner):
+    row, col = iota((128, 128), 0), iota((128, 128), 1)
+    return jnp.where((row % outer) * inner + row // outer == col, 1.0, 0.0).astype(BF)
+
+
+def pick_columns(zs):
+    lane = iota((8, 128), 1)[0:1]
+    group = lane >> 5
+    z = jnp.where(group == 0, zs[0], jnp.where(group == 1, zs[1], jnp.where(group == 2, zs[2], zs[3])))
+    return jnp.where(iota((CY * CZ, 128), 0) == (lane & 31) * CZ + z, 1.0, 0.0).astype(BF)
+
+
+def with_neighbours(outer, inner):
+    lane = iota(outer.shape, 1)
+    middle = jnp.where(
+        lane < 64,
+        jnp.where(lane < 32, roll(outer, 32), roll(inner, -32)),
+        jnp.where(lane < 96, roll(inner, 32), roll(outer, -32)),
+    )
+    return jnp.where(lane < 64, outer, inner), middle, jnp.where(lane < 64, inner, outer)
+
+
+def fetch(sources, targets, sems):
+    copies = [pltpu.make_async_copy(s, t, sems.at[k]) for k, (s, t) in enumerate(zip(sources, targets))]
+    for copy in copies:
+        copy.start()
+    return copies
+
+
+def open_cells(mask):
+    return jnp.concatenate([(1 - mask[x]).astype(F32) for x in range(8)], 0)
+
+
+def bias_column(bias, shape):
+    row = iota(shape, 0)
+    column = jnp.zeros(shape, F32)
+    for o in range(16):
+        column = jnp.where(row == o, bias[o], column)
+    return column
+
+
+def first_kernel(f_hbm, mask_hbm, one_hbm, bias_hbm, rims, weights, f, mask, one, bias, sems):
+    copies = fetch((one_hbm, bias_hbm, mask_hbm, f_hbm), (one, bias, mask, f), sems)
+    select = pick_columns((30, 31, 0, 1))
+    place = iota((16, 64), 1)
+    copies[0].wait()
+    copies[1].wait()
+    column = bias_column(bias, (16, 64))
+    high = column.astype(BF).astype(F32)
+    middle = (column - high).astype(BF).astype(F32)
+    terms = jnp.where(place == 0, high, jnp.where(place == 1, middle, jnp.where(place == 2, column - high - middle, 0.0)))
+    for t in range(14):
+        other = one[t + 14] if t < 13 else terms.astype(BF)
+        weights[16 * t : 16 * t + 16] = jnp.concatenate([one[t], other], 1)
+    copies[2].wait()
+    opened = jnp.concatenate([open_cells(mask), jnp.zeros((8, CY * CZ), F32)], 0)
+    rims[128:144] = dot(opened.astype(BF), select).astype(BF)
+    copies[3].wait()
+    rims[0:128] = dot(f[...], select).astype(BF)
+
+
+def place_inputs(base, f, w, field, first, bias_one):
+    planes = dot(swap_rows(16, 8), f[...])
+    for e in range(3):
+        moved = roll(planes, e - 1).astype(BF)
+        for x in range(8):
+            field[pl.ds(192 * (x + 1) + 64 * e + base, 16)] = moved[16 * x : 16 * x + 16]
+
+    def tap(t):
+        block = w[16 * (t % 14) : 16 * (t % 14) + 16]
+        return block[:, 0:64] if t < 14 else block[:, 64:128]
+
+    blank = jnp.zeros((16, 192), BF)
+    for b in range(3):
+        taps = [tap(9 * a + 3 * b + e) for a in range(3) for e in range(3)]
+        first[pl.ds(128 * b + base, 16)] = jnp.concatenate(taps + [blank], 1)
+        first[pl.ds(128 * b + 64 + base, 16)] = jnp.concatenate([blank] + taps, 1)
+    tail = w[16 * 13 : 16 * 14].astype(F32)
+    total = tail[:, 64:65] + tail[:, 65:66] + tail[:, 66:67]
+    bias_one[pl.ds(base, 16)] = jnp.broadcast_to(total, (16, 128))
+
+
+def near_kernel(me_ref, bias, f0, f1, w0, w1, mask, two, field, first, bias_one, opened, second, bias_two):
+    field[0:192] = jnp.zeros((192, CY * CZ), BF)
+    field[9 * 192 : 10 * 192] = jnp.zeros((192, CY * CZ), BF)
+    opened[...] = open_cells(mask)
+    me = me_ref[0]
+    for k, (f, w) in enumerate(((f0, w0), (f1, w1))):
+        place_inputs(pl.multiple_of((me ^ k) * 16, 16), f, w, field, first, bias_one)
+    blank = jnp.zeros((16, 64), BF)
+    for e in range(3):
+        for b in range(3):
+            taps = [two[9 * a + 3 * b + e] for a in range(3)]
+            row = 96 * e + 32 * b
+            second[row : row + 16] = jnp.concatenate(taps + [blank], 1)
+            second[row + 16 : row + 32] = jnp.concatenate([blank] + taps, 1)
+    bias_two[...] = bias_column(bias, (16, 128))
+
+
+def inside():
+    lane = iota((8, CY * CZ), 1)[0:1]
+    return jnp.where(lane >= CZ, 1.0, 0.0), jnp.where(lane < (CY - 1) * CZ, 1.0, 0.0)
+
+
+def one_kernel(me_ref, f2, f3, w2, w3, opened, field_in, first_in, bias_in,
+               field, first, bias_one, hidden, rims, open_rims):
+    del field_in, first_in, bias_in
+    me = me_ref[0]
+    for k, (f, w) in enumerate(((f2, w2), (f3, w3))):
+        place_inputs(pl.multiple_of((me ^ (2 + k)) * 16, 16), f, w, field, first, bias_one)
+
+    after_first, before_last = inside()
+    hidden[0:64] = jnp.zeros((64, CY * CZ), BF)
+    hidden[9 * 64 : 10 * 64] = jnp.zeros((64, CY * CZ), BF)
+    column = bias_one[:, 0:1]
+    for q in range(4):
+        sums = dot(first[...], field[384 * q : 384 * q + 768])
+        total = roll(sums[0:128], -CZ) * after_first + sums[128:256] + roll(sums[256:384], CZ) * before_last
+        for half in range(2):
+            x = 2 * q + half
+            value = jnp.maximum(total[64 * half : 64 * half + 64] + column, 0.0) * opened[x : x + 1]
+            hidden[64 * (x + 1) : 64 * (x + 2)] = value.astype(BF)
+
+    select = pick_columns((0, 1, 30, 31))
+    for x in range(8):
+        rims[64 * x : 64 * x + 64] = dot(field[192 * (x + 1) + 64 : 192 * (x + 1) + 128], select).astype(BF)
+    open_rims[...] = dot(opened[...].astype(BF), select)
+
+
+def two_kernel(hidden, second, bias_two, opened, out_ref, inner, last):
+    after_first, before_last = inside()
+    column = bias_two[:, 0:1]
+    for q in range(4):
+        sums = dot(second[...], hidden[128 * q : 128 * q + 256])
+        moved = [sum(roll(sums[96 * e + 32 * b : 96 * e + 32 * b + 32], e - 1) for e in range(3)) for b in range(3)]
+        total = roll(moved[0], -CZ) * after_first + moved[1] + roll(moved[2], CZ) * before_last
+        for half in range(2):
+            x = 2 * q + half
+            value = jnp.maximum(total[16 * half : 16 * half + 16] + column, 0.0) * opened[x : x + 1]
+            last[16 * x : 16 * x + 16] = value.astype(BF)
+    out_ref[...] = dot(swap_rows(8, 16), last[...]).astype(BF)
+    inner[...] = dot(hidden[64 : 9 * 64], pick_columns((1, 2, 29, 30))).astype(BF)
+
+
+def edge_kernel(me_ref, h0, h1, h2, h3, mask_halo, rims, inner, open_rims, first, bias_one, second, bias_two, out_in,
+                out_ref, halo, field, hidden, last):
+    me = me_ref[0]
+    to_plane = swap_rows(16, 8)
+    for k, h in enumerate((h0, h1, h2, h3)):
+        base = pl.multiple_of((me ^ k) * 16, 16)
+        planes = dot(to_plane, h[...]).astype(BF)
+        for x in range(8):
+            halo[pl.ds(64 * x + base, 16)] = planes[16 * x : 16 * x + 16]
+
+    field[0:192] = jnp.zeros((192, 128), BF)
+    field[9 * 192 : 10 * 192] = jnp.zeros((192, 128), BF)
+    hidden[:, 0:64] = jnp.zeros((3, 64, 128), BF)
+    hidden[:, 9 * 64 : 10 * 64] = jnp.zeros((3, 64, 128), BF)
+    for e, moved in enumerate(with_neighbours(halo[...].astype(F32), rims[...].astype(F32))):
+        moved = moved.astype(BF)
+        for x in range(8):
+            field[192 * (x + 1) + 64 * e : 192 * (x + 1) + 64 * e + 64] = moved[64 * x : 64 * x + 64]
+    opened = with_neighbours(mask_halo[0:8].astype(F32), open_rims[...])[1]
+
+    y = iota((8, 128), 1)[0:1] & 31
+    after_first = jnp.where(y > 0, 1.0, 0.0)
+    before_last = jnp.where(y < CY - 1, 1.0, 0.0)
+    column = bias_one[:, 0:1]
+    for q in range(4):
+        sums = dot(first[...], field[384 * q : 384 * q + 768])
+        total = roll(sums[0:128], -1) * after_first + sums[128:256] + roll(sums[256:384], 1) * before_last
+        for half in range(2):
+            x = 2 * q + half
+            value = jnp.maximum(total[64 * half : 64 * half + 64] + column, 0.0) * opened[x : x + 1]
+            between = inner[64 * x : 64 * x + 64].astype(F32)
+            for e, moved in enumerate(with_neighbours(value.astype(BF).astype(F32), between)):
+                hidden[e, 64 * (x + 1) : 64 * (x + 2)] = moved.astype(BF)
+
+    column = bias_two[:, 0:1]
+    for q in range(4):
+        sums = dot(second[0:96], hidden[0, 128 * q : 128 * q + 256])
+        for e in (1, 2):
+            sums += dot(second[96 * e : 96 * e + 96], hidden[e, 128 * q : 128 * q + 256])
+        total = roll(sums[0:32], -1) * after_first + sums[32:64] + roll(sums[64:96], 1) * before_last
+        for half in range(2):
+            x = 2 * q + half
+            value = jnp.maximum(total[16 * half : 16 * half + 16] + column, 0.0) * open_rims[x : x + 1]
+            last[16 * x : 16 * x + 16] = value.astype(BF)
+
+    cell = iota((8, CY * CZ), 1)[0:1]
+    z = cell & 31
+    group = jnp.where(z < 2, z, z - 28)
+    row = jnp.where((z < 2) | (z >= 30), 32 * group + (cell >> 5), -1)
+    spread = jnp.where(iota((128, CY * CZ), 0) == row, 1.0, 0.0).astype(BF)
+    edges = dot(swap_rows(8, 16), dot(last[...], spread).astype(BF))
+    out_ref[...] = jnp.where(row >= 0, edges, out_in[...].astype(F32)).astype(BF)
+
+
+def cost(micros):
+    return pl.CostEstimate(flops=int(micros * 1.15e9), bytes_accessed=int(micros * 3e6), transcendentals=0)
+
+
+def one_row(features, solid_mask, weight_one, bias_one, weight_two, bias_two):
+    columns = lax.axis_size("col")
+    me = lax.axis_index("ch").astype(jnp.int32).reshape(1)
+
+    def across(v, bit):
+        return lax.ppermute(v, "ch", [(i, i ^ bit) for i in range(lax.axis_size("ch"))])
+
+    def after(v, other):
+        return lax.optimization_barrier((v, other))[0]
+
+    def exchange(v, parity):
+        route = []
+        for c in range(parity, columns - 1, 2):
+            route += [(c, c + 1), (c + 1, c)]
+        return lax.ppermute(v, "col", route)
+
+    smem = pl.BlockSpec(memory_space=pltpu.SMEM)
+    hbm = pl.BlockSpec(memory_space=pltpu.HBM)
+    vmem = pl.BlockSpec(memory_space=pltpu.VMEM)
+    mask_buffer = pltpu.VMEM((8, 1, 1024), jnp.int32)
+    weight_buffer = pltpu.VMEM((27, 16, 64), BF)
+    cell_buffer = pltpu.VMEM((128, 1024), BF)
+    bias_buffer = pltpu.SMEM((16,), F32)
+    shape = jax.ShapeDtypeStruct
+
+    cells = features.reshape(128, 1024)
+    far = across(cells, 2)
+    near = across(cells, 1)
+    rims, weights = pl.pallas_call(
+        first_kernel,
+        out_shape=[shape((144, 128), BF), shape((224, 128), BF)],
+        in_specs=[hbm] * 4,
+        out_specs=[vmem] * 2,
+        scratch_shapes=[cell_buffer, mask_buffer, weight_buffer, bias_buffer, pltpu.SemaphoreType.DMA((4,))],
+        compiler_params=pltpu.CompilerParams(vmem_limit_bytes=WHOLE),
+        cost_estimate=cost(1),
+        name="first",
+    )(cells, solid_mask, weight_one.transpose(1, 0, 2), bias_one)
+
+    odd = exchange(rims, 1)
+    even = exchange(after(rims, near), 0)
+    weights_far, weights_near = across(weights, 2), across(weights, 1)
+    cross = across(far, 1)
+
+    kept = [shape((1920, 1024), BF), shape((384, 768), BF), shape((64, 128), F32)]
+    field, first, bias, opened, second, bias_second = pl.pallas_call(
+        near_kernel,
+        out_shape=kept + [shape((8, 1024), F32), shape((288, 256), BF), shape((16, 128), F32)],
+        in_specs=[smem, smem] + [vmem] * 6,
+        out_specs=[vmem] * 6,
+        compiler_params=pltpu.CompilerParams(vmem_limit_bytes=16 << 20),
+        cost_estimate=cost(1.5),
+        name="near",
+    )(me, bias_two, cells, near, weights, weights_near, solid_mask, weight_two.transpose(1, 0, 2))
+
+    odd, even, opened = lax.optimization_barrier((odd, even, opened))
+    is_odd = lax.axis_index("col") % 2 == 1
+    side = lax.broadcasted_iota(jnp.int32, (144, 128), 1)
+    halo = jnp.where((side < 64) == is_odd, even, odd)
+    mask_halo = halo[128:]
+    halo = halo[:128]
+    weights_cross = across(after(weights_far, halo), 1)
+    halo_far = across(halo, 2)
+
+    _, first, bias, hidden, rim_cells, open_rims = pl.pallas_call(
+        one_kernel,
+        out_shape=kept + [shape((640, 1024), BF), shape((512, 128), BF), shape((8, 128), F32)],
+        in_specs=[smem] + [vmem] * 8,
+        out_specs=[vmem] * 6,
+        input_output_aliases={6: 0, 7: 1, 8: 2},
+        compiler_params=pltpu.CompilerParams(vmem_limit_bytes=24 << 20),
+        cost_estimate=cost(4),
+        name="one",
+    )(me, far, cross, weights_far, weights_cross, opened, field, first, bias)
+
+    halo_near = across(halo, 1)
+    halo_cross = across(after(halo_far, open_rims), 1)
+
+    out, inner = pl.pallas_call(
+        two_kernel,
+        out_shape=[shape((128, 1024), BF), shape((512, 128), BF)],
+        in_specs=[vmem] * 4,
+        out_specs=[vmem] * 2,
+        scratch_shapes=[pltpu.VMEM((128, 1024), BF)],
+        compiler_params=pltpu.CompilerParams(vmem_limit_bytes=16 << 20),
+        cost_estimate=cost(2),
+        name="two",
+    )(hidden, second, bias_second, opened)
+
+    result = pl.pallas_call(
+        edge_kernel,
+        out_shape=shape((128, 1024), BF),
+        in_specs=[smem] + [vmem] * 13,
+        out_specs=vmem,
+        scratch_shapes=[
+            pltpu.VMEM((512, 128), BF),
+            pltpu.VMEM((1920, 128), BF),
+            pltpu.VMEM((3, 640, 128), BF),
+            pltpu.VMEM((128, 128), BF),
+        ],
+        compiler_params=pltpu.CompilerParams(vmem_limit_bytes=16 << 20),
+        cost_estimate=cost(2),
+        name="edge",
+    )(me, halo, halo_near, halo_far, halo_cross, mask_halo, rim_cells, inner, open_rims, first, bias, second, bias_second, out)
+    return result.reshape(16, 8, 1, 1024)
 
 
 def passed_along(block, axis, distance):
@@ -19,7 +346,7 @@
     return weight.reshape(outputs, 3, 3, 3, inputs).transpose(0, 4, 1, 2, 3)
 
 
-def on_device(features, solid_mask, weight_one, bias_one, weight_two, bias_two):
+def many_rows(features, solid_mask, weight_one, bias_one, weight_two, bias_two):
     cells = features.shape[3]
     columns = lax.axis_size("col")
     grid_z = min(8, columns)
@@ -69,6 +396,11 @@
     return finish(total, bias_two, open_cells)
 
 
+def on_device(*arguments):
+    columns = lax.axis_size("col")
+    return one_row(*arguments) if columns <= 8 and columns % 2 == 0 else many_rows(*arguments)
+
+
 def solution(mesh):
     in_specs = (
         P("ch", None, "col", None),

time: 154 us -> 24.3 us (0.16)
  waiting for transfers between devices: 50.3 us -> 0.04 us
  matrix products: 42.7 us -> 0 us
  local copies, waits for them, and re-layouts: 27.7 us -> 0.83 us
  between operations: 13.7 us -> 0.16 us
  Pallas kernels: 0 us -> 11.6 us
  other arithmetic: 7.67 us -> 0.02 us
    conv_general_dilated x2 -> x0, matrix products: 42.7 us -> none  [convolve(): lax.conv_general_dilated(framed[None], kernel_of(weight), (1, 1, 1), 'VAL...]
    all_gather x2 -> x0, waiting for transfers between devices: 37.9 us -> none  [padded_inputs(): whole = lax.all_gather(field, 'ch', axis=0, tiled=True)]
    conv_general_dilated x10 -> x0, local copies, waits for them, and re-layouts: 17.7 us -> none  [convolve(): lax.conv_general_dilated(framed[None], kernel_of(weight), (1, 1, 1), 'VAL...]
    ppermute x8 -> x11, waiting for transfers between devices: 11.6 us -> 0.04 us  [the longest x9 0.02 us: across(): lax.ppermute(v, 'ch', [(i, i ^ bit) for i in range(lax.axis_size('ch'))])]
    pallas_call x0 -> x5, Pallas kernels: none -> 11.6 us  [the longest x1 3.84 us: one_row(): pl.pallas_call(one_kernel, out_shape=kept + [shape((640, 1024), BF), shap...]
    broadcast_in_dim x2 -> x0, other arithmetic: 5.23 us -> none  [convolve(): framed[None]]
    all_gather x2 -> x0, local copies, waits for them, and re-layouts: 4.72 us -> none  [padded_inputs(): whole = lax.all_gather(field, 'ch', axis=0, tiled=True)]
    another operation x2 -> x0, local copies, waits for them, and re-layouts: 1.92 us -> none  [convolve(): return result[0].reshape(weight.shape[0], depth_x, 1, cells)]
  transfers between devices with their start and end apart: 10 -> 11, of which waited for: 6 -> 0; matrix products, arithmetic and copies ran while one was open for 0% -> 0% of each run, Pallas kernels for 0% -> 37%
where the time goes in v2:
time: 24.3 us; the launch traced here: 24.1 us
  Pallas kernels  11.6 us (48%)
  starting transfers between devices  11.5 us (47%)
  local copies, waits for them, and re-layouts  0.83 us (3%)
    ppermute x9, starting transfers between devices, across(): lax.ppermute(v, 'ch', [(i, i ^ bit) for i in range(lax.axis_size('ch'))])  6.23 us
    ppermute x2, starting transfers between devices, exchange(): return lax.ppermute(v, 'col', route)  5.26 us
    pallas_call x1, Pallas kernels, one_row(): pl.pallas_call(one_kernel, out_shape=kept + [shape((640, 1024), BF), shap...  3.84 us
    pallas_call x1, Pallas kernels, one_row(): pl.pallas_call(edge_kernel, out_shape=shape((128, 1024), BF), in_specs=[s...  2.6 us
    pallas_call x1, Pallas kernels, one_row(): pl.pallas_call(first_kernel, out_shape=[shape((144, 128), BF), shape((224...  2.03 us
    pallas_call x1, Pallas kernels, one_row(): pl.pallas_call(two_kernel, out_shape=[shape((128, 1024), BF), shape((512,...  1.84 us
    pallas_call x1, Pallas kernels, one_row(): pl.pallas_call(near_kernel, out_shape=kept + [shape((8, 1024), F32), shap...  1.26 us
    unnamed x10, local copies, waits for them, and re-layouts  0.83 us
  transfers between devices with their start and end apart: 11, of which 0 were waited for; matrix products, arithmetic and copies ran while one was open for 0% of the time, Pallas kernels for 37%

profile of v2, /device:TPU:0, one launch (start us, length us, event | category | flops | bytes accessed | tf_op | source)
XLA Modules:
  0.0 24.1 jit_solution(7556178797802489358)
XLA Ops:
  0.0 0.0 copy-start
  0.0 0.0 copy-start.3
  0.0 0.0 copy-start.1
  0.0 0.0 copy-start.4
  0.0 0.5 %collective-permute-start.1 = (bf16[128,1024]{1,0:T(8,128)(2,1)}, bf16[128,1024]{1,0:T(8,128)(2,1)S(1)}, u32[]{:S(2)}, u32[]{:S(2)}) collective-permute-start(bf16[128,1024]{1,0:T(8,128)(2,1)} %bitcast.7), channel_id=1, source_target_pairs={{0,1},{1,0},{2,3},{3,2},{4,5},{5,4},{6,7},{7,6},{8,9},{9,8},{10,11... | collective-permute-start | bytes 786440 | tf_op jit(solution)/shard_map/ppermute | solution.py:235
  0.5 2.6 %collective-permute-start.6 = (bf16[128,1024]{1,0:T(8,128)(2,1)}, bf16[128,1024]{1,0:T(8,128)(2,1)S(1)}, u32[]{:S(2)}, u32[]{:S(2)}) collective-permute-start(bf16[128,1024]{1,0:T(8,128)(2,1)} %bitcast.8), channel_id=1, source_target_pairs={{0,2},{1,3},{2,0},{3,1},{4,6},{5,7},{6,4},{7,5},{8,10},{9,11},{10,... | collective-permute-start | bytes 786440 | tf_op jit(solution)/shard_map/ppermute | solution.py:235
  3.1 2.0 %first.1 = (bf16[144,128]{1,0:T(8,128)(2,1)}, bf16[224,128]{1,0:T(8,128)(2,1)}) custom-call(bf16[128,1024]{1,0:T(8,128)(2,1)} %bitcast.9, s32[8,1,1024]{2,1,0:T(1,128)} %mask.1, bf16[27,16,64]{2,1,0:T(8,128)(2,1)} %bitcast.12, f32[16]{0:T(128)} %bias_hbm.1), custom_call_target="tpu_custom_call" | custom-call | flops 1150000000 | bytes 3000000 | tf_op jit(solution)/shard_map/first/pallas_call | solution.py:258
  5.1 0.2 collective-permute-start.3
  5.4 0.3 %collective-permute-start.8 = (bf16[224,128]{1,0:T(8,128)(2,1)}, bf16[224,128]{1,0:T(8,128)(2,1)S(1)}, u32[]{:S(2)}, u32[]{:S(2)}) collective-permute-start(bf16[224,128]{1,0:T(8,128)(2,1)} %get-tuple-element.28.w0), channel_id=1, source_target_pairs={{0,2},{1,3},{2,0},{3,1},{4,6},{5,7},{6,4},{7,5},{8,10},{9,11},{10,... | collective-permute-start | bytes 172040 | tf_op jit(solution)/shard_map/ppermute | solution.py:235
  5.6 0.7 %collective-permute-start = (bf16[144,128]{1,0:T(8,128)(2,1)}, bf16[144,128]{1,0:T(8,128)(2,1)S(1)}, u32[]{:S(2)}, u32[]{:S(2)}) collective-permute-start(bf16[144,128]{1,0:T(8,128)(2,1)} %get-tuple-element.27), channel_id=1, source_target_pairs={{4,8},{8,4},{12,16},{16,12},{20,24},{24,20},{5,9},{9,5},{13,17},{1... | collective-permute-start | bytes 110600 | tf_op jit(solution)/shard_map/ppermute | solution.py:244
  6.3 0.0 collective-permute-done.1.f1
  6.3 4.6 %collective-permute-start.2 = (bf16[144,128]{1,0:T(8,128)(2,1)}, bf16[144,128]{1,0:T(8,128)(2,1)S(1)}, u32[]{:S(2)}, u32[]{:S(2)}) collective-permute-start(bf16[144,128]{1,0:T(8,128)(2,1)} %get-tuple-element.27), channel_id=1, source_target_pairs={{0,4},{4,0},{8,12},{12,8},{16,20},{20,16},{24,28},{28,24},{1,5},{5... | collective-permute-start | bytes 110600 | tf_op jit(solution)/shard_map/ppermute | solution.py:244
  11.0 0.0 collective-permute-done.6.f2
  11.0 0.0 collective-permute-start.7
  11.0 0.0 collective-permute-done.3.w1
  11.0 0.0 copy-done
  11.0 0.0 copy-done.3
  11.0 0.0 copy-done.1
  11.0 0.0 copy-done.4
  11.0 0.0 copy-start.2
  11.0 0.8 %copy-done.2 = bf16[224,128]{1,0:T(8,128)(2,1)S(1)} copy-done((bf16[224,128]{1,0:T(8,128)(2,1)S(1)}, bf16[224,128]{1,0:T(8,128)(2,1)}, u32[]{:S(2)}) %copy-start.2) | copy-done | bytes 57368
  11.8 1.3 %near.1 = (bf16[1920,1024]{1,0:T(8,128)(2,1)S(1)}, bf16[384,768]{1,0:T(8,128)(2,1)S(1)}, f32[64,128]{1,0:T(8,128)S(1)}, f32[8,1024]{1,0:T(8,128)S(1)}, bf16[288,...) custom-call(s32[1]{0:T(128)} %bitcast.me_ref, f32[16]{0:T(128)S(1)} %copy-done.4, bf16[128,1024]{1,0:T(8,128)(2,1)S(1)} %bitcast.10, ...), custom_call_target="tpu_custom_call" | custom-call | flops 1724999936 | bytes 4500000 | tf_op jit(solution)/shard_map/near/pallas_call | solution.py:275
  13.1 0.0 collective-permute-done
  13.1 0.0 collective-permute-done.2
  13.1 0.0 collective-permute-done.8.w2
  13.1 0.6 %collective-permute-start.9 = (bf16[224,128]{1,0:T(8,128)(2,1)S(1)}, bf16[224,128]{1,0:T(8,128)(2,1)S(1)}, u32[]{:S(2)}, u32[]{:S(2)}) collective-permute-start(bf16[224,128]{1,0:T(8,128)(2,1)S(1)} %collective-permute-done.8.w2), channel_id=1, source_target_pairs={{0,1},{1,0},{2,3},{3,2},{4,5},{5,4},{6,7},{7,6},{8,9},{9,8},{10,11... | collective-permute-start | bytes 172040 | tf_op jit(solution)/shard_map/ppermute | solution.py:235
  13.7 1.5 %collective-permute-start.5 = (bf16[128,128]{1,0:T(8,128)(2,1)S(1)}, bf16[128,128]{1,0:T(8,128)(2,1)S(1)}, u32[]{:S(2)}, u32[]{:S(2)}) collective-permute-start(bf16[128,128]{1,0:T(8,128)(2,1)S(1)} %slice.8.h0), channel_id=1, source_target_pairs={{0,2},{1,3},{2,0},{3,1},{4,6},{5,7},{6,4},{7,5},{8,10},{9,11},{10,... | collective-permute-start | bytes 98312 | tf_op jit(solution)/shard_map/ppermute | solution.py:235
  15.2 0.0 collective-permute-start.4
  15.2 0.0 collective-permute-done.9.w3
  15.2 0.0 collective-permute-done.7.f3
  15.2 3.8 %one.1 = (bf16[1920,1024]{1,0:T(8,128)(2,1)S(1)}, bf16[384,768]{1,0:T(8,128)(2,1)S(1)}, f32[64,128]{1,0:T(8,128)S(1)}, bf16[640,1024]{1,0:T(8,128)(2,1)S(1)}, bf...) custom-call(s32[1]{0:T(128)} %bitcast.me_ref, ...), custom_call_target="tpu_custom_call", output_to_operand_aliasing={{0}: (6, {}), {1}: (7, {}), {2}: (8, {})} | custom-call | flops 4600000000 | bytes 12000000 | tf_op jit(solution)/shard_map/one/pallas_call | solution.py:294
  19.1 0.0 collective-permute-done.5.h2
  19.1 0.6 %collective-permute-start.10 = (bf16[128,128]{1,0:T(8,128)(2,1)S(1)}, bf16[128,128]{1,0:T(8,128)(2,1)S(1)}, u32[]{:S(2)}, u32[]{:S(2)}) collective-permute-start(bf16[128,128]{1,0:T(8,128)(2,1)S(1)} %collective-permute-done.5.h2), channel_id=1, source_target_pairs={{0,1},{1,0},{2,3},{3,2},{4,5},{5,4},{6,7},{7,6},{8,9},{9,8},{10,11... | collective-permute-start | bytes 98312 | tf_op jit(solution)/shard_map/ppermute | solution.py:235
  19.6 1.8 %two.1 = (bf16[128,1024]{1,0:T(8,128)(2,1)S(1)}, bf16[512,128]{1,0:T(8,128)(2,1)S(1)}) custom-call(bf16[640,1024]{1,0:T(8,128)(2,1)S(1)} %get-tuple-element.40.hidden, bf16[288,256]{1,0:T(8,128)(2,1)S(1)} %get-tuple-element.41.second, f32[16,128]{1,0:T(8,128)S(1)} %get-tuple-element.42.bias_two, f32[8,1024]{1,0:T(8,128)S(1)} %get-tuple-element.33.opened), custom_call_target="tpu_custom_call" | custom-call | flops 2300000000 | bytes 6000000 | tf_op jit(solution)/shard_map/two/pallas_call | solution.py:308
  21.5 0.0 collective-permute-done.4.h1
  21.5 0.0 collective-permute-done.10.h3
  21.5 2.6 %edge.1 = bf16[128,1024]{1,0:T(8,128)(2,1)} custom-call(s32[1]{0:T(128)} %bitcast.me_ref, bf16[128,128]{1,0:T(8,128)(2,1)S(1)} %slice.8.h0, bf16[128,128]{1,0:T(8,128)(2,1)S(1)} %collective-permute-done.4.h1, bf16[128,128]{1,0:T(8,128)(2,1)S(1)} %collective-permute-done.5.h2, bf16[128,128]{1,0:T(8,128)(2,1)S(1)} %collective-permute-done.10.h3, ...), custom_call_target="tpu_custom_call" | custom-call | flops 2300000000 | bytes 6000000 | tf_op jit(solution)/shard_map/edge/pallas_call | solution.py:319
  (4 shorter events, 0.0 us)
Async XLA Ops:
  0.0 11.0 %copy-start = (bf16[16,8,1,1024]{3,1,2,0:T(8,128)(2,1)S(1)}, bf16[16,8,1,1024]{3,1,2,0:T(8,128)(2,1)}, u32[]{:S(2)}) copy-start(bf16[16,8,1,1024]{3,1,2,0:T(8,128)(2,1)} %param.6) | copy-start | bytes 786436
  0.0 11.0 %copy-start.3 = (s32[8,1,1024]{2,1,0:T(1,128)S(1)}, s32[8,1,1024]{2,1,0:T(1,128)}, u32[]{:S(2)}) copy-start(s32[8,1,1024]{2,1,0:T(1,128)} %mask.1) | copy-start | bytes 98308
  0.0 11.0 %copy-start.1 = (bf16[16,27,64]{2,0,1:T(8,128)(2,1)S(1)}, bf16[16,27,64]{2,0,1:T(8,128)(2,1)}, u32[]{:S(2)}) copy-start(bf16[16,27,64]{2,0,1:T(8,128)(2,1)} %param.10) | copy-start | bytes 165892
  0.0 11.0 %copy-start.4 = (f32[16]{0:T(128)S(1)}, f32[16]{0:T(128)}, u32[]{:S(2)}) copy-start(f32[16]{0:T(128)} %bias.1) | copy-start | bytes 196
  0.0 6.3 %collective-permute-start.1 = (bf16[128,1024]{1,0:T(8,128)(2,1)}, bf16[128,1024]{1,0:T(8,128)(2,1)S(1)}, u32[]{:S(2)}, u32[]{:S(2)}) collective-permute-start(bf16[128,1024]{1,0:T(8,128)(2,1)} %bitcast.7), channel_id=1, source_target_pairs={{0,1},{1,0},{2,3},{3,2},{4,5},{5,4},{6,7},{7,6},{8,9},{9,8},{10,11... | collective-permute-start | bytes 786440 | tf_op jit(solution)/shard_map/ppermute | solution.py:235
  0.5 10.4 %collective-permute-start.6 = (bf16[128,1024]{1,0:T(8,128)(2,1)}, bf16[128,1024]{1,0:T(8,128)(2,1)S(1)}, u32[]{:S(2)}, u32[]{:S(2)}) collective-permute-start(bf16[128,1024]{1,0:T(8,128)(2,1)} %bitcast.8), channel_id=1, source_target_pairs={{0,2},{1,3},{2,0},{3,1},{4,6},{5,7},{6,4},{7,5},{8,10},{9,11},{10,... | collective-permute-start | bytes 786440 | tf_op jit(solution)/shard_map/ppermute | solution.py:235
  5.1 5.8 %collective-permute-start.3 = (bf16[224,128]{1,0:T(8,128)(2,1)}, bf16[224,128]{1,0:T(8,128)(2,1)S(1)}, u32[]{:S(2)}, u32[]{:S(2)}) collective-permute-start(bf16[224,128]{1,0:T(8,128)(2,1)} %get-tuple-element.28.w0), channel_id=1, source_target_pairs={{0,1},{1,0},{2,3},{3,2},{4,5},{5,4},{6,7},{7,6},{8,9},{9,8},{10,11... | collective-permute-start | bytes 172040 | tf_op jit(solution)/shard_map/ppermute | solution.py:235
  5.4 7.8 %collective-permute-start.8 = (bf16[224,128]{1,0:T(8,128)(2,1)}, bf16[224,128]{1,0:T(8,128)(2,1)S(1)}, u32[]{:S(2)}, u32[]{:S(2)}) collective-permute-start(bf16[224,128]{1,0:T(8,128)(2,1)} %get-tuple-element.28.w0), channel_id=1, source_target_pairs={{0,2},{1,3},{2,0},{3,1},{4,6},{5,7},{6,4},{7,5},{8,10},{9,11},{10,... | collective-permute-start | bytes 172040 | tf_op jit(solution)/shard_map/ppermute | solution.py:235
  5.6 7.4 %collective-permute-start = (bf16[144,128]{1,0:T(8,128)(2,1)}, bf16[144,128]{1,0:T(8,128)(2,1)S(1)}, u32[]{:S(2)}, u32[]{:S(2)}) collective-permute-start(bf16[144,128]{1,0:T(8,128)(2,1)} %get-tuple-element.27), channel_id=1, source_target_pairs={{4,8},{8,4},{12,16},{16,12},{20,24},{24,20},{5,9},{9,5},{13,17},{1... | collective-permute-start | bytes 110600 | tf_op jit(solution)/shard_map/ppermute | solution.py:244
  6.3 6.8 %collective-permute-start.2 = (bf16[144,128]{1,0:T(8,128)(2,1)}, bf16[144,128]{1,0:T(8,128)(2,1)S(1)}, u32[]{:S(2)}, u32[]{:S(2)}) collective-permute-start(bf16[144,128]{1,0:T(8,128)(2,1)} %get-tuple-element.27), channel_id=1, source_target_pairs={{0,4},{4,0},{8,12},{12,8},{16,20},{20,16},{24,28},{28,24},{1,5},{5... | collective-permute-start | bytes 110600 | tf_op jit(solution)/shard_map/ppermute | solution.py:244
  11.0 4.3 %collective-permute-start.7 = (bf16[128,1024]{1,0:T(8,128)(2,1)S(1)}, bf16[128,1024]{1,0:T(8,128)(2,1)S(1)}, u32[]{:S(2)}, u32[]{:S(2)}) collective-permute-start(bf16[128,1024]{1,0:T(8,128)(2,1)S(1)} %collective-permute-done.6.f2), channel_id=1, source_target_pairs={{0,1},{1,0},{2,3},{3,2},{4,5},{5,4},{6,7},{7,6},{8,9},{9,8},{10,11... | collective-permute-start | bytes 786440 | tf_op jit(solution)/shard_map/ppermute | solution.py:235
  11.0 0.8 %copy-start.2 = (bf16[224,128]{1,0:T(8,128)(2,1)S(1)}, bf16[224,128]{1,0:T(8,128)(2,1)}, u32[]{:S(2)}) copy-start(bf16[224,128]{1,0:T(8,128)(2,1)} %get-tuple-element.28.w0) | copy-start | bytes 172036
  13.1 2.1 %collective-permute-start.9 = (bf16[224,128]{1,0:T(8,128)(2,1)S(1)}, bf16[224,128]{1,0:T(8,128)(2,1)S(1)}, u32[]{:S(2)}, u32[]{:S(2)}) collective-permute-start(bf16[224,128]{1,0:T(8,128)(2,1)S(1)} %collective-permute-done.8.w2), channel_id=1, source_target_pairs={{0,1},{1,0},{2,3},{3,2},{4,5},{5,4},{6,7},{7,6},{8,9},{9,8},{10,11... | collective-permute-start | bytes 172040 | tf_op jit(solution)/shard_map/ppermute | solution.py:235
  13.7 5.4 %collective-permute-start.5 = (bf16[128,128]{1,0:T(8,128)(2,1)S(1)}, bf16[128,128]{1,0:T(8,128)(2,1)S(1)}, u32[]{:S(2)}, u32[]{:S(2)}) collective-permute-start(bf16[128,128]{1,0:T(8,128)(2,1)S(1)} %slice.8.h0), channel_id=1, source_target_pairs={{0,2},{1,3},{2,0},{3,1},{4,6},{5,7},{6,4},{7,5},{8,10},{9,11},{10,... | collective-permute-start | bytes 98312 | tf_op jit(solution)/shard_map/ppermute | solution.py:235
  15.2 6.3 %collective-permute-start.4 = (bf16[128,128]{1,0:T(8,128)(2,1)S(1)}, bf16[128,128]{1,0:T(8,128)(2,1)S(1)}, u32[]{:S(2)}, u32[]{:S(2)}) collective-permute-start(bf16[128,128]{1,0:T(8,128)(2,1)S(1)} %slice.8.h0), channel_id=1, source_target_pairs={{0,1},{1,0},{2,3},{3,2},{4,5},{5,4},{6,7},{7,6},{8,9},{9,8},{10,11... | collective-permute-start | bytes 98312 | tf_op jit(solution)/shard_map/ppermute | solution.py:235
  19.1 2.4 %collective-permute-start.10 = (bf16[128,128]{1,0:T(8,128)(2,1)S(1)}, bf16[128,128]{1,0:T(8,128)(2,1)S(1)}, u32[]{:S(2)}, u32[]{:S(2)}) collective-permute-start(bf16[128,128]{1,0:T(8,128)(2,1)S(1)} %collective-permute-done.5.h2), channel_id=1, source_target_pairs={{0,1},{1,0},{2,3},{3,2},{4,5},{5,4},{6,7},{7,6},{8,9},{9,8},{10,11... | collective-permute-start | bytes 98312 | tf_op jit(solution)/shard_map/ppermute | solution.py:235

commit v3 on v2

v3 whole, which is shorter than its diff:
```python
import jax
import jax.numpy as jnp
from jax import lax
from jax.experimental import pallas as pl
from jax.experimental.pallas import tpu as pltpu
from jax.sharding import PartitionSpec as P

CY = 32
CZ = 32
BF = jnp.bfloat16
F32 = jnp.float32
SELECT = 5


def iota(shape, dimension):
    return lax.broadcasted_iota(jnp.int32, shape, dimension)


def dot(a, b):
    return jnp.dot(a, b, preferred_element_type=F32)


def roll(x, shift):
    n = x.shape[1]
    return x if shift % n == 0 else pltpu.roll(x, (-shift) % n, 1)


def swap_rows(outer, inner):
    row, col = iota((128, 128), 0), iota((128, 128), 1)
    return jnp.where((row % outer) * inner + row // outer == col, 1.0, 0.0).astype(BF)


def pick_columns(zs):
    lane = iota((8, 128), 1)[0:1]
    group = lane >> 5
    z = jnp.where(group == 0, zs[0], jnp.where(group == 1, zs[1], jnp.where(group == 2, zs[2], zs[3])))
    return jnp.where(iota((CY * CZ, 128), 0) == (lane & 31) * CZ + z, 1.0, 0.0).astype(BF)


def with_neighbours(outer, inner):
    lane = iota(outer.shape, 1) & 127
    middle = jnp.where(
        lane < 64,
        jnp.where(lane < 32, roll(outer, 32), roll(inner, -32)),
        jnp.where(lane < 96, roll(inner, 32), roll(outer, -32)),
    )
    return jnp.where(lane < 64, outer, inner), middle, jnp.where(lane < 64, inner, outer)


def open_cells(mask):
    return jnp.concatenate([(1 - mask[x]).astype(F32) for x in range(8)], 0)


def bias_column(bias, shape):
    row = iota(shape, 0)
    column = jnp.zeros(shape, F32)
    for o in range(16):
        column = jnp.where(row == o, bias[o], column)
    return column


def select_kernel(out):
    out[...] = pick_columns((30, 31, 0, 1))


def first_kernel(bias, select, f, mask, one, rims, weights):
    rims[0:128] = dot(f[...], select[...]).astype(BF)
    opened = jnp.concatenate([open_cells(mask), jnp.zeros((8, CY * CZ), F32)], 0)
    rims[128:144] = dot(opened.astype(BF), select[...]).astype(BF)
    place = iota((16, 64), 1)
    column = bias_column(bias, (16, 64))
    high = column.astype(BF).astype(F32)
    middle = (column - high).astype(BF).astype(F32)
    terms = jnp.where(place == 0, high, jnp.where(place == 1, middle, jnp.where(place == 2, column - high - middle, 0.0)))
    for t in range(14):
        other = one[t + 14] if t < 13 else terms.astype(BF)
        weights[16 * t : 16 * t + 16] = jnp.concatenate([one[t], other], 1)


def place_features(base, f, field, rims):
    planes = dot(swap_rows(16, 8), f[...])
    rim = dot(planes.astype(BF), pick_columns((0, 1, 30, 31))).astype(BF)
    for x in range(8):
        rims[pl.ds(64 * x + base, 16)] = rim[16 * x : 16 * x + 16]
    for e in range(3):
        moved = roll(planes, e - 1).astype(BF)
        for x in range(8):
            field[pl.ds(192 * (x + 1) + 64 * e + base, 16)] = moved[16 * x : 16 * x + 16]


def place_filters(base, w, first, bias_one):
    def tap(t):
        block = w[16 * (t % 14) : 16 * (t % 14) + 16]
        return block[:, 0:64] if t < 14 else block[:, 64:128]

    blank = jnp.zeros((16, 192), BF)
    for b in range(3):
        taps = [tap(9 * a + 3 * b + e) for a in range(3) for e in range(3)]
        first[pl.ds(128 * b + base, 16)] = jnp.concatenate(taps + [blank], 1)
        first[pl.ds(128 * b + 64 + base, 16)] = jnp.concatenate([blank] + taps, 1)
    tail = w[16 * 13 : 16 * 14].astype(F32)
    total = tail[:, 64:65] + tail[:, 65:66] + tail[:, 66:67]
    bias_one[pl.ds(base, 16)] = jnp.broadcast_to(total, (16, 128))


def near_kernel(me_ref, bias, f0, f1, mask, two, field, rims, opened, open_rims, second, bias_two):
    field[0:192] = jnp.zeros((192, CY * CZ), BF)
    field[9 * 192 : 10 * 192] = jnp.zeros((192, CY * CZ), BF)
    cells = open_cells(mask)
    opened[...] = cells
    open_rims[...] = dot(cells.astype(BF), pick_columns((0, 1, 30, 31)))
    me = me_ref[0]
    for k, f in enumerate((f0, f1)):
        place_features(pl.multiple_of((me ^ k) * 16, 16), f, field, rims)
    blank = jnp.zeros((16, 64), BF)
    for e in range(3):
        for b in range(3):
            taps = [two[9 * a + 3 * b + e] for a in range(3)]
            row = 96 * e + 32 * b
            second[row : row + 16] = jnp.concatenate(taps + [blank], 1)
            second[row + 16 : row + 32] = jnp.concatenate([blank] + taps, 1)
    bias_two[...] = bias_column(bias, (16, 128))


def far_kernel(me_ref, f2, field_in, rims_in, field, rims):
    del field_in, rims_in
    place_features(pl.multiple_of((me_ref[0] ^ 2) * 16, 16), f2, field, rims)


def inside():
    lane = iota((8, CY * CZ), 1)[0:1]
    return jnp.where(lane >= CZ, 1.0, 0.0), jnp.where(lane < (CY - 1) * CZ, 1.0, 0.0)


def one_kernel(me_ref, f3, w0, w1, w2, w3, opened, field_in, rims_in, field, rims, hidden, first, bias_one):
    del field_in, rims_in
    me = me_ref[0]
    for k, w in enumerate((w0, w1, w2, w3)):
        place_filters(pl.multiple_of((me ^ k) * 16, 16), w, first, bias_one)
    place_features(pl.multiple_of((me ^ 3) * 16, 16), f3, field, rims)

    after_first, before_last = inside()
    z = iota((8, CY * CZ), 1)[0:1] & 31
    settled = jnp.where((z > 0) & (z < CZ - 1), 1.0, 0.0)
    hidden[0:64] = jnp.zeros((64, CY * CZ), BF)
    hidden[9 * 64 : 10 * 64] = jnp.zeros((64, CY * CZ), BF)
    column = bias_one[:, 0:1]
    for q in range(4):
        sums = dot(first[...], field[384 * q : 384 * q + 768])
        total = roll(sums[0:128], -CZ) * after_first + sums[128:256] + roll(sums[256:384], CZ) * before_last
        for half in range(2):
            x = 2 * q + half
            value = jnp.maximum(total[64 * half : 64 * half + 64] + column, 0.0) * (opened[x : x + 1] * settled)
            hidden[64 * (x + 1) : 64 * (x + 2)] = value.astype(BF)


def two_kernel(me_ref, h0, h1, h23, mask_halo, rims, open_rims, first, bias_one, second, bias_two, opened, hidden,
               out_ref, halo, field, edge, terms, last):
    me = me_ref[0]
    to_plane = swap_rows(16, 8)
    for k, h in enumerate((h0, h1, h23.at[0:128], h23.at[128:256])):
        base = pl.multiple_of((me ^ k) * 16, 16)
        planes = dot(to_plane, h[...]).astype(BF)
        for x in range(8):
            halo[pl.ds(64 * x + base, 16)] = planes[16 * x : 16 * x + 16]

    def windows(x):
        return [(q, x + 1 - 2 * q) for q in range(4) if 0 <= x + 1 - 2 * q < 4]

    field[0:192, 0:128] = jnp.zeros((192, 128), BF)
    field[576:768, 384:512] = jnp.zeros((192, 128), BF)
    for e, moved in enumerate(with_neighbours(halo[...].astype(F32), rims[...].astype(F32))):
        moved = moved.astype(BF)
        for x in range(8):
            for q, place in windows(x):
                field[192 * place + 64 * e : 192 * place + 64 * e + 64, 128 * q : 128 * q + 128] = moved[64 * x : 64 * x + 64]
    open_edge = with_neighbours(mask_halo[0:8].astype(F32), open_rims[...])[1]

    y = iota((8, 512), 1)[0:1] & 31
    after_first = jnp.where(y > 0, 1.0, 0.0)
    before_last = jnp.where(y < CY - 1, 1.0, 0.0)
    sums = dot(first[...], field[...])
    total = roll(sums[0:128], -1) * after_first + sums[128:256] + roll(sums[256:384], 1) * before_last
    edge[0:64, 0:128] = jnp.zeros((64, 128), BF)
    edge[192:256, 384:512] = jnp.zeros((64, 128), BF)
    for half in range(2):
        opening = jnp.concatenate([open_edge[2 * q + half : 2 * q + half + 1] for q in range(4)], 1)
        value = jnp.maximum(total[64 * half : 64 * half + 64] + bias_one[:, 0:1], 0.0) * opening
        value = value.astype(BF)
        for k in range(4):
            for q, place in windows(2 * k + half):
                edge[64 * place : 64 * place + 64, 128 * q : 128 * q + 128] = value[:, 128 * k : 128 * k + 128]

    sums = dot(second[...], edge[...])
    before, same, behind = [
        roll(sums[r : r + 32], -1) * after_first + sums[r + 32 : r + 64] + roll(sums[r + 64 : r + 96], 1) * before_last
        for r in (0, 96, 192)
    ]
    lane = iota((32, 512), 1) & 127
    total = jnp.where(lane < 64, before, behind)
    total += jnp.where(lane < 32, roll(same, 32), jnp.where(lane < 96, 0.0, roll(same, -32)))
    high = total.astype(BF)
    low = (total - high.astype(F32)).astype(BF)
    for q in range(4):
        terms[32 * q : 32 * q + 32] = high[:, 128 * q : 128 * q + 128]
        terms[128 + 32 * q : 160 + 32 * q] = low[:, 128 * q : 128 * q + 128]
    cell = iota((8, CY * CZ), 1)[0:1]
    z = cell & 31
    row = jnp.where((z < 2) | (z >= 30), 32 * jnp.where(z < 2, z, z - 28) + (cell >> 5), -1)
    spread = jnp.where(iota((128, CY * CZ), 0) == row, 1.0, 0.0).astype(BF)

    after_first, before_last = inside()
    for q in range(4):
        sums = dot(second[...], hidden[128 * q : 128 * q + 256])
        moved = [sum(roll(sums[96 * e + 32 * b : 96 * e + 32 * b + 32], e - 1) for e in range(3)) for b in range(3)]
        total = roll(moved[0], -CZ) * after_first + moved[1] + roll(moved[2], CZ) * before_last
        total += dot(terms[32 * q : 32 * q + 32], spread) + dot(terms[128 + 32 * q : 160 + 32 * q], spread)
        for half in range(2):
            x = 2 * q + half
            value = jnp.maximum(total[16 * half : 16 * half + 16] + bias_two[:, 0:1], 0.0) * opened[x : x + 1]
            last[16 * x : 16 * x + 16] = value.astype(BF)
    out_ref[...] = dot(swap_rows(8, 16), last[...]).astype(BF)


def cost(micros):
    return pl.CostEstimate(flops=int(micros * 1.15e9), bytes_accessed=int(micros * 3e6), transcendentals=0)


def one_row(features, solid_mask, weight_one, bias_one, weight_two, bias_two):
    columns = lax.axis_size("col")
    me = lax.axis_index("ch").astype(jnp.int32).reshape(1)

    def across(v, bit):
        return lax.ppermute(v, "ch", [(i, i ^ bit) for i in range(lax.axis_size("ch"))])

    def after(v, other):
        return lax.optimization_barrier((v, other))[0]

    def exchange(v, parity):
        route = []
        for c in range(parity, columns - 1, 2):
            route += [(c, c + 1), (c + 1, c)]
        return lax.ppermute(v, "col", route)

    smem = pl.BlockSpec(memory_space=pltpu.SMEM)
    vmem = pl.BlockSpec(memory_space=pltpu.VMEM)
    shape = jax.ShapeDtypeStruct

    cells = features.reshape(128, 1024)
    far = across(cells, 2)
    near = across(cells, 1)
    select = pl.pallas_call(
        select_kernel,
        out_shape=shape((1024, 128), BF),
        out_specs=vmem,
        compiler_params=pltpu.CompilerParams(vmem_limit_bytes=4 << 20),
        cost_estimate=cost(SELECT),
        name="select",
    )()
    rims, weights = pl.pallas_call(
        first_kernel,
        out_shape=[shape((144, 128), BF), shape((224, 128), BF)],
        in_specs=[smem] + [vmem] * 4,
        out_specs=[vmem] * 2,
        compiler_params=pltpu.CompilerParams(vmem_limit_bytes=8 << 20),
        cost_estimate=cost(1),
        name="first",
    )(bias_one, select, cells, solid_mask, weight_one.transpose(1, 0, 2))

    odd = exchange(rims, 1)
    even = exchange(rims, 0)
    weights_far, weights_near = across(weights, 2), across(weights, 1)

    field_shape, rims_shape = shape((1920, 1024), BF), shape((512, 128), BF)
    field, rim_cells, opened, open_rims, second, bias_second = pl.pallas_call(
        near_kernel,
        out_shape=[field_shape, rims_shape, shape((8, 1024), F32), shape((8, 128), F32), shape((288, 256), BF), shape((16, 128), F32)],
        in_specs=[smem, smem] + [vmem] * 4,
        out_specs=[vmem] * 6,
        compiler_params=pltpu.CompilerParams(vmem_limit_bytes=16 << 20),
        cost_estimate=cost(0.1),
        name="near",
    )(me, bias_two, cells, near, solid_mask, weight_two.transpose(1, 0, 2))

    far = after(far, open_rims)
    cross = across(far, 1)
    field, rim_cells = pl.pallas_call(
        far_kernel,
        out_shape=[field_shape, rims_shape],
        in_specs=[smem] + [vmem] * 3,
        out_specs=[vmem] * 2,
        input_output_aliases={2: 0, 3: 1},
        compiler_params=pltpu.CompilerParams(vmem_limit_bytes=16 << 20),
        cost_estimate=cost(0.1),
        name="far",
    )(me, far, field, rim_cells)
    weights_far, rim_cells = lax.optimization_barrier((weights_far, rim_cells))
    weights_cross = across(weights_far, 1)

    odd, even, opened = lax.optimization_barrier((odd, even, opened))
    is_odd = lax.axis_index("col") % 2 == 1
    side = lax.broadcasted_iota(jnp.int32, (144, 128), 1)
    halo = jnp.where((side < 64) == is_odd, even, odd)
    mask_halo = halo[128:]
    halo = halo[:128]
    halo_near = across(halo, 1)
    halo_here, rim_cells = lax.optimization_barrier((jnp.concatenate([halo, halo_near], 0), rim_cells))
    halo_there = across(halo_here, 2)

    _, rim_cells, hidden, first, bias = pl.pallas_call(
        one_kernel,
        out_shape=[field_shape, rims_shape, shape((640, 1024), BF), shape((384, 768), BF), shape((64, 128), F32)],
        in_specs=[smem] + [vmem] * 8,
        out_specs=[vmem] * 5,
        input_output_aliases={7: 0, 8: 1},
        compiler_params=pltpu.CompilerParams(vmem_limit_bytes=24 << 20),
        cost_estimate=cost(4),
        name="one",
    )(me, cross, weights, weights_near, weights_far, weights_cross, opened, field, rim_cells)

    result = pl.pallas_call(
        two_kernel,
        out_shape=shape((128, 1024), BF),
        in_specs=[smem] + [vmem] * 12,
        out_specs=vmem,
        scratch_shapes=[
            pltpu.VMEM((512, 128), BF),
            pltpu.VMEM((768, 512), BF),
            pltpu.VMEM((256, 512), BF),
            pltpu.VMEM((256, 128), BF),
            pltpu.VMEM((128, 1024), BF),
        ],
        compiler_params=pltpu.CompilerParams(vmem_limit_bytes=16 << 20),
        cost_estimate=cost(3),
        name="two",
    )(me, halo, halo_near, halo_there, mask_halo, rim_cells, open_rims, first, bias, second, bias_second, opened, hidden)
    return result.reshape(16, 8, 1, 1024)


def passed_along(block, axis, distance):
    devices = range(lax.axis_size(axis))
    route = [(i - distance, i) for i in devices if i - distance in devices]
    return lax.ppermute(block, axis, route)


def kernel_of(weight):
    outputs = weight.shape[0]
    inputs = weight.shape[2]
    return weight.reshape(outputs, 3, 3, 3, inputs).transpose(0, 4, 1, 2, 3)


def many_rows(features, solid_mask, weight_one, bias_one, weight_two, bias_two):
    cells = features.shape[3]
    columns = lax.axis_size("col")
    grid_z = min(8, columns)
    open_cells = (1 - solid_mask).astype(jnp.float32)

    def pad_columns(field):
        depth = field.shape[0]
        depth_x = field.shape[1]
        cube = field.reshape(depth, depth_x, CY, CZ)
        below = passed_along(cube[:, :, :, CZ - 1 :], "col", 1)
        above = passed_along(cube[:, :, :, :1], "col", -1)
        place = lax.axis_index("col") % grid_z
        below = jnp.where(place > 0, below, jnp.zeros_like(below))
        above = jnp.where(place < grid_z - 1, above, jnp.zeros_like(above))
        cube = jnp.concatenate([below, cube, above], axis=3)
        south = passed_along(cube[:, :, CY - 1 :, :], "col", grid_z)
        north = passed_along(cube[:, :, :1, :], "col", -grid_z)
        return jnp.concatenate([south, cube, north], axis=2)

    def pad_planes(framed):
        return jnp.pad(framed, ((0, 0), (1, 1), (0, 0), (0, 0)))

    def padded_inputs(field):
        whole = lax.all_gather(field, "ch", axis=0, tiled=True)
        framed = pad_columns(whole)
        return pad_planes(framed)

    def convolve(framed, weight):
        depth_x = framed.shape[1] - 2
        result = lax.conv_general_dilated(
            framed[None],
            kernel_of(weight),
            (1, 1, 1),
            "VALID",
            dimension_numbers=("NCDHW", "OIDHW", "NCDHW"),
            preferred_element_type=jnp.float32,
        )
        return result[0].reshape(weight.shape[0], depth_x, 1, cells)

    def finish(total, bias, opened):
        return (jnp.maximum(total + bias[:, None, None, None], 0.0) * opened[None]).astype(
            jnp.bfloat16
        )

    hidden = finish(convolve(padded_inputs(features), weight_one), bias_one, open_cells)
    total = convolve(padded_inputs(hidden), weight_two)
    return finish(total, bias_two, open_cells)


def on_device(*arguments):
    columns = lax.axis_size("col")
    return one_row(*arguments) if columns <= 8 and columns % 2 == 0 else many_rows(*arguments)


def solution(mesh):
    in_specs = (
        P("ch", None, "col", None),
        P(None, "col", None),
        P("ch", None, None),
        P("ch"),
        P("ch", None, None),
        P("ch"),
    )
    out_specs = P("ch", None, "col", None)
    return jax.shard_map(
        on_device, mesh=mesh, in_specs=in_specs, out_specs=out_specs, check_vma=False
    )
```

time: 24.3 us -> 21 us (0.86)
  starting transfers between devices: 11.5 us -> 9.26 us
  Pallas kernels: 11.6 us -> 9.62 us
  waiting for transfers between devices: 0.04 us -> 1.49 us
  local copies, waits for them, and re-layouts: 0.83 us -> 0.03 us
    ppermute x2, starting transfers between devices: 5.26 us -> 2.23 us  [exchange(): return lax.ppermute(v, 'col', route)]
    ppermute x9 -> x8, waiting for transfers between devices: 0.02 us -> 1.48 us  [across(): lax.ppermute(v, 'ch', [(i, i ^ bit) for i in range(lax.axis_size('ch'))])]
    pallas_call x1, Pallas kernels: 2.03 us -> 0.79 us  [one_row(): pl.pallas_call(first_kernel, out_shape=[shape((144, 128), BF), shape((224...]
    unnamed x10 -> x12, local copies, waits for them, and re-layouts: 0.83 us -> 0.03 us
    ppermute x9 -> x8, starting transfers between devices: 6.23 us -> 7.03 us  [across(): lax.ppermute(v, 'ch', [(i, i ^ bit) for i in range(lax.axis_size('ch'))])]
    pallas_call x4 -> x5, Pallas kernels: 9.54 us -> 8.84 us  [the longest x1 3.59 us: one_row(): pl.pallas_call(two_kernel, out_shape=shape((128, 1024), BF), in_specs=[sm...]
  transfers between devices with their start and end apart: 11 -> 10, of which waited for: 0 -> 1; matrix products, arithmetic and copies ran while one was open for 0% -> 0% of each run, Pallas kernels for 37% -> 29%
where the time goes in v3:
time: 21 us; the launch traced here: 20.6 us
  Pallas kernels  9.62 us (46%)
  starting transfers between devices  9.26 us (44%)
  waiting for transfers between devices  1.49 us (7%)
    ppermute x8, starting transfers between devices, across(): lax.ppermute(v, 'ch', [(i, i ^ bit) for i in range(lax.axis_size('ch'))])  7.03 us
    pallas_call x1, Pallas kernels, one_row(): pl.pallas_call(two_kernel, out_shape=shape((128, 1024), BF), in_specs=[sm...  3.59 us
    pallas_call x1, Pallas kernels, one_row(): pl.pallas_call(one_kernel, out_shape=[field_shape, rims_shape, shape((640...  3.36 us
    ppermute x2, starting transfers between devices, exchange(): return lax.ppermute(v, 'col', route)  2.23 us
    ppermute x8, waiting for transfers between devices, across(): lax.ppermute(v, 'ch', [(i, i ^ bit) for i in range(lax.axis_size('ch'))])  1.48 us
    pallas_call x1, Pallas kernels, one_row(): pl.pallas_call(near_kernel, out_shape=[field_shape, rims_shape, shape((8,...  1.39 us
    pallas_call x1, Pallas kernels, one_row(): pl.pallas_call(first_kernel, out_shape=[shape((144, 128), BF), shape((224...  0.79 us
    pallas_call x1, Pallas kernels, one_row(): pl.pallas_call(far_kernel, out_shape=[field_shape, rims_shape], in_specs=...  0.43 us
  transfers between devices with their start and end apart: 10, of which 1 were waited for; matrix products, arithmetic and copies ran while one was open for 0% of the time, Pallas kernels for 29%

profile of v3, /device:TPU:0, one launch (start us, length us, event | category | flops | bytes accessed | tf_op | source)
XLA Modules:
  0.0 20.6 jit_solution(7871305851248458214)
XLA Ops:
  0.0 0.0 copy-start
  0.0 0.0 copy-start.2
  0.0 0.0 copy-start.4
  0.0 0.0 copy-start.5
  0.0 3.0 %collective-permute-start.5 = (bf16[128,1024]{1,0:T(8,128)(2,1)}, bf16[128,1024]{1,0:T(8,128)(2,1)S(1)}, u32[]{:S(2)}, u32[]{:S(2)}) collective-permute-start(bf16[128,1024]{1,0:T(8,128)(2,1)} %bitcast.7), channel_id=1, source_target_pairs={{0,2},{1,3},{2,0},{3,1},{4,6},{5,7},{6,4},{7,5},{8,10},{9,11},{10,... | collective-permute-start | bytes 786440 | tf_op jit(solution)/shard_map/ppermute | solution.py:234
  3.0 0.0 collective-permute-start.2
  3.0 0.1 select.3
  3.1 0.0 copy-start.1
  3.1 0.0 copy-start.3
  3.1 0.0 copy-done
  3.1 0.0 copy-done.2
  3.1 0.0 copy-done.4
  3.1 0.0 copy-done.5
  3.2 0.8 %first.1 = (bf16[144,128]{1,0:T(8,128)(2,1)S(1)}, bf16[224,128]{1,0:T(8,128)(2,1)S(1)}) custom-call(f32[16]{0:T(128)S(1)} %copy-done.5, bf16[1024,128]{1,0:T(8,128)(2,1)S(1)} %select.3, bf16[128,1024]{1,0:T(8,128)(2,1)S(1)} %bitcast.9, s32[8,1,1024]{2,1,0:T(1,128)S(1)} %copy-done.2, bf16[27,16,64]{2,1,0:T(8,128)(2,1)S(1)} %bitcast.12), custom_call_target="tpu_custom_call" | custom-call | flops 1150000000 | bytes 3000000 | tf_op jit(solution)/shard_map/first/pallas_call | solution.py:260
  3.9 1.6 %collective-permute-start.1 = (bf16[144,128]{1,0:T(8,128)(2,1)S(1)}, bf16[144,128]{1,0:T(8,128)(2,1)S(1)}, u32[]{:S(2)}, u32[]{:S(2)}) collective-permute-start(bf16[144,128]{1,0:T(8,128)(2,1)S(1)} %get-tuple-element.27), channel_id=1, source_target_pairs={{0,4},{4,0},{8,12},{12,8},{16,20},{20,16},{24,28},{28,24},{1,5},{5... | collective-permute-start | bytes 110600 | tf_op jit(solution)/shard_map/ppermute | solution.py:243
  5.5 0.7 %collective-permute-start = (bf16[144,128]{1,0:T(8,128)(2,1)S(1)}, bf16[144,128]{1,0:T(8,128)(2,1)S(1)}, u32[]{:S(2)}, u32[]{:S(2)}) collective-permute-start(bf16[144,128]{1,0:T(8,128)(2,1)S(1)} %get-tuple-element.27), channel_id=1, source_target_pairs={{4,8},{8,4},{12,16},{16,12},{20,24},{24,20},{5,9},{9,5},{13,17},{1... | collective-permute-start | bytes 110600 | tf_op jit(solution)/shard_map/ppermute | solution.py:243
  6.2 0.8 %collective-permute-start.4 = (bf16[224,128]{1,0:T(8,128)(2,1)S(1)}, bf16[224,128]{1,0:T(8,128)(2,1)S(1)}, u32[]{:S(2)}, u32[]{:S(2)}) collective-permute-start(bf16[224,128]{1,0:T(8,128)(2,1)S(1)} %get-tuple-element.31.w0), channel_id=1, source_target_pairs={{0,2},{1,3},{2,0},{3,1},{4,6},{5,7},{6,4},{7,5},{8,10},{9,11},{10,... | collective-permute-start | bytes 172040 | tf_op jit(solution)/shard_map/ppermute | solution.py:234
  7.0 0.0 collective-permute-done.2.f1
  7.0 0.0 copy-done.1
  7.0 0.0 copy-done.3
  7.1 1.4 %near.1 = (bf16[1920,1024]{1,0:T(8,128)(2,1)S(1)}, bf16[512,128]{1,0:T(8,128)(2,1)S(1)}, f32[8,1024]{1,0:T(8,128)S(1)}, f32[8,128]{1,0:T(8,128)S(1)}, bf16[288,2...) custom-call(s32[1]{0:T(128)} %bitcast.me_ref, f32[16]{0:T(128)S(1)} %copy-done.3, bf16[128,1024]{1,0:T(8,128)(2,1)S(1)} %bitcast.10, ...), custom_call_target="tpu_custom_call" | custom-call | flops 115000000 | bytes 300000 | tf_op jit(solution)/shard_map/near/pallas_call | solution.py:275
  8.5 0.0 collective-permute-done.1
  8.5 0.0 collective-permute-done
  8.5 1.5 %collective-permute-done.5.f2 = bf16[128,1024]{1,0:T(8,128)(2,1)S(1)} collective-permute-done((bf16[128,1024]{1,0:T(8,128)(2,1)}, bf16[128,1024]{1,0:T(8,128)(2,1)S(1)}, u32[]{:S(2)}, u32[]{:S(2)}) %collective-permute-start.5) | collective-permute-done | bytes 262176 | tf_op jit(solution)/shard_map/ppermute | solution.py:234
  9.9 0.0 collective-permute-start.7
  10.0 0.6 %collective-permute-start.3 = (bf16[128,128]{1,0:T(8,128)(2,1)S(1)}, bf16[128,128]{1,0:T(8,128)(2,1)S(1)}, u32[]{:S(2)}, u32[]{:S(2)}) collective-permute-start(bf16[128,128]{1,0:T(8,128)(2,1)S(1)} %slice.8.h0), channel_id=1, source_target_pairs={{0,1},{1,0},{2,3},{3,2},{4,5},{5,4},{6,7},{7,6},{8,9},{9,8},{10,11... | collective-permute-start | bytes 98312 | tf_op jit(solution)/shard_map/ppermute | solution.py:234
  10.5 0.1 collective-permute-start.8
  10.6 0.4 %far.1 = (bf16[1920,1024]{1,0:T(8,128)(2,1)S(1)}, bf16[512,128]{1,0:T(8,128)(2,1)S(1)}) custom-call(s32[1]{0:T(128)} %bitcast.me_ref, bf16[128,1024]{1,0:T(8,128)(2,1)S(1)} %collective-permute-done.5.f2, bf16[1920,1024]{1,0:T(8,128)(2,1)S(1)} %get-tuple-element.34.field_in, ...), custom_call_target="tpu_custom_call", output_to_operand_aliasing={{0}: (2, {}), {1}: (3, {})} | custom-call | flops 115000000 | bytes 300000 | tf_op jit(solution)/shard_map/far/pallas_call | solution.py:287
  11.1 0.0 collective-permute-done.4.w2
  11.1 0.5 %collective-permute-start.9 = (bf16[224,128]{1,0:T(8,128)(2,1)S(1)}, bf16[224,128]{1,0:T(8,128)(2,1)S(1)}, u32[]{:S(2)}, u32[]{:S(2)}) collective-permute-start(bf16[224,128]{1,0:T(8,128)(2,1)S(1)} %collective-permute-done.4.w2), channel_id=1, source_target_pairs={{0,1},{1,0},{2,3},{3,2},{4,5},{5,4},{6,7},{7,6},{8,9},{9,8},{10,11... | collective-permute-start | bytes 172040 | tf_op jit(solution)/shard_map/ppermute | solution.py:234
  11.6 0.0 collective-permute-done.3.h1
  11.6 2.0 %collective-permute-start.6 = (bf16[256,128]{1,0:T(8,128)(2,1)S(1)}, bf16[256,128]{1,0:T(8,128)(2,1)S(1)}, u32[]{:S(2)}, u32[]{:S(2)}) collective-permute-start(bf16[256,128]{1,0:T(8,128)(2,1)S(1)} %pad_maximum_fusion), channel_id=1, source_target_pairs={{0,2},{1,3},{2,0},{3,1},{4,6},{5,7},{6,4},{7,5},{8,10},{9,11},{10,... | collective-permute-start | bytes 196616 | tf_op jit(solution)/shard_map/ppermute | solution.py:234
  13.6 0.0 collective-permute-done.8.w1
  13.6 0.0 collective-permute-done.9.w3
  13.6 0.0 collective-permute-done.7.f3
  13.6 3.4 %one.1 = (bf16[1920,1024]{1,0:T(8,128)(2,1)S(1)}, bf16[512,128]{1,0:T(8,128)(2,1)S(1)}, bf16[640,1024]{1,0:T(8,128)(2,1)S(1)}, bf16[384,768]{1,0:T(8,128)(2,1)S(1)}, f32[64,128]{1,0:T(8,128)S(1)}) custom-call(s32[1]{0:T(128)} %bitcast.me_ref, bf16[128,1024]{1,0:T(8,128)(2,1)S(1)} %collective-permute-done.7.f3, ...), custom_call_target="tpu_custom_call", output_to_operand_aliasing={{0}: (7, {}), {1}: (8, {})} | custom-call | flops 4600000000 | bytes 12000000 | tf_op jit(solution)/shard_map/one/pallas_call | solution.py:310
  17.0 0.0 collective-permute-done.6.h23
  17.0 3.6 %two.1 = bf16[128,1024]{1,0:T(8,128)(2,1)} custom-call(s32[1]{0:T(128)} %bitcast.me_ref, bf16[128,128]{1,0:T(8,128)(2,1)S(1)} %slice.8.h0, bf16[128,128]{1,0:T(8,128)(2,1)S(1)} %collective-permute-done.3.h1, bf16[256,128]{1,0:T(8,128)(2,1)S(1)} %collective-permute-done.6.h23, bf16[16,128]{1,0:T(8,128)(2,1)S(1)} %slice.9.mask_halo, ...), custom_call_target="tpu_custom_call" | custom-call | flops 3449999872 | bytes 9000000 | tf_op jit(solution)/shard_map/two/pallas_call | solution.py:321
  (5 shorter events, 0.0 us)
Async XLA Ops:
  0.0 3.1 %copy-start = (bf16[16,8,1,1024]{3,1,2,0:T(8,128)(2,1)S(1)}, bf16[16,8,1,1024]{3,1,2,0:T(8,128)(2,1)}, u32[]{:S(2)}) copy-start(bf16[16,8,1,1024]{3,1,2,0:T(8,128)(2,1)} %param.6) | copy-start | bytes 786436
  0.0 3.1 %copy-start.2 = (s32[8,1,1024]{2,1,0:T(1,128)S(1)}, s32[8,1,1024]{2,1,0:T(1,128)}, u32[]{:S(2)}) copy-start(s32[8,1,1024]{2,1,0:T(1,128)} %mask.3) | copy-start | bytes 98308
  0.0 3.1 %copy-start.4 = (bf16[16,27,64]{2,0,1:T(8,128)(2,1)S(1)}, bf16[16,27,64]{2,0,1:T(8,128)(2,1)}, u32[]{:S(2)}) copy-start(bf16[16,27,64]{2,0,1:T(8,128)(2,1)} %param.8) | copy-start | bytes 165892
  0.0 3.1 %copy-start.5 = (f32[16]{0:T(128)S(1)}, f32[16]{0:T(128)}, u32[]{:S(2)}) copy-start(f32[16]{0:T(128)} %bias.2) | copy-start | bytes 196
  0.0 9.9 %collective-permute-start.5 = (bf16[128,1024]{1,0:T(8,128)(2,1)}, bf16[128,1024]{1,0:T(8,128)(2,1)S(1)}, u32[]{:S(2)}, u32[]{:S(2)}) collective-permute-start(bf16[128,1024]{1,0:T(8,128)(2,1)} %bitcast.7), channel_id=1, source_target_pairs={{0,2},{1,3},{2,0},{3,1},{4,6},{5,7},{6,4},{7,5},{8,10},{9,11},{10,... | collective-permute-start | bytes 786440 | tf_op jit(solution)/shard_map/ppermute | solution.py:234
  3.0 4.0 %collective-permute-start.2 = (bf16[128,1024]{1,0:T(8,128)(2,1)}, bf16[128,1024]{1,0:T(8,128)(2,1)S(1)}, u32[]{:S(2)}, u32[]{:S(2)}) collective-permute-start(bf16[128,1024]{1,0:T(8,128)(2,1)} %bitcast.8), channel_id=1, source_target_pairs={{0,1},{1,0},{2,3},{3,2},{4,5},{5,4},{6,7},{7,6},{8,9},{9,8},{10,11... | collective-permute-start | bytes 786440 | tf_op jit(solution)/shard_map/ppermute | solution.py:234
  3.1 3.9 %copy-start.1 = (bf16[16,27,64]{2,0,1:T(8,128)(2,1)S(1)}, bf16[16,27,64]{2,0,1:T(8,128)(2,1)}, u32[]{:S(2)}) copy-start(bf16[16,27,64]{2,0,1:T(8,128)(2,1)} %param.10) | copy-start | bytes 165892
  3.1 3.9 %copy-start.3 = (f32[16]{0:T(128)S(1)}, f32[16]{0:T(128)}, u32[]{:S(2)}) copy-start(f32[16]{0:T(128)} %bias.3) | copy-start | bytes 196
  3.9 4.5 %collective-permute-start.1 = (bf16[144,128]{1,0:T(8,128)(2,1)S(1)}, bf16[144,128]{1,0:T(8,128)(2,1)S(1)}, u32[]{:S(2)}, u32[]{:S(2)}) collective-permute-start(bf16[144,128]{1,0:T(8,128)(2,1)S(1)} %get-tuple-element.27), channel_id=1, source_target_pairs={{0,4},{4,0},{8,12},{12,8},{16,20},{20,16},{24,28},{28,24},{1,5},{5... | collective-permute-start | bytes 110600 | tf_op jit(solution)/shard_map/ppermute | solution.py:243
  5.5 2.9 %collective-permute-start = (bf16[144,128]{1,0:T(8,128)(2,1)S(1)}, bf16[144,128]{1,0:T(8,128)(2,1)S(1)}, u32[]{:S(2)}, u32[]{:S(2)}) collective-permute-start(bf16[144,128]{1,0:T(8,128)(2,1)S(1)} %get-tuple-element.27), channel_id=1, source_target_pairs={{4,8},{8,4},{12,16},{16,12},{20,24},{24,20},{5,9},{9,5},{13,17},{1... | collective-permute-start | bytes 110600 | tf_op jit(solution)/shard_map/ppermute | solution.py:243
  6.2 4.9 %collective-permute-start.4 = (bf16[224,128]{1,0:T(8,128)(2,1)S(1)}, bf16[224,128]{1,0:T(8,128)(2,1)S(1)}, u32[]{:S(2)}, u32[]{:S(2)}) collective-permute-start(bf16[224,128]{1,0:T(8,128)(2,1)S(1)} %get-tuple-element.31.w0), channel_id=1, source_target_pairs={{0,2},{1,3},{2,0},{3,1},{4,6},{5,7},{6,4},{7,5},{8,10},{9,11},{10,... | collective-permute-start | bytes 172040 | tf_op jit(solution)/shard_map/ppermute | solution.py:234
  9.9 3.7 %collective-permute-start.7 = (bf16[128,1024]{1,0:T(8,128)(2,1)S(1)}, bf16[128,1024]{1,0:T(8,128)(2,1)S(1)}, u32[]{:S(2)}, u32[]{:S(2)}) collective-permute-start(bf16[128,1024]{1,0:T(8,128)(2,1)S(1)} %collective-permute-done.5.f2), channel_id=1, source_target_pairs={{0,1},{1,0},{2,3},{3,2},{4,5},{5,4},{6,7},{7,6},{8,9},{9,8},{10,11... | collective-permute-start | bytes 786440 | tf_op jit(solution)/shard_map/ppermute | solution.py:234
  10.0 1.6 %collective-permute-start.3 = (bf16[128,128]{1,0:T(8,128)(2,1)S(1)}, bf16[128,128]{1,0:T(8,128)(2,1)S(1)}, u32[]{:S(2)}, u32[]{:S(2)}) collective-permute-start(bf16[128,128]{1,0:T(8,128)(2,1)S(1)} %slice.8.h0), channel_id=1, source_target_pairs={{0,1},{1,0},{2,3},{3,2},{4,5},{5,4},{6,7},{7,6},{8,9},{9,8},{10,11... | collective-permute-start | bytes 98312 | tf_op jit(solution)/shard_map/ppermute | solution.py:234
  10.5 3.1 %collective-permute-start.8 = (bf16[224,128]{1,0:T(8,128)(2,1)S(1)}, bf16[224,128]{1,0:T(8,128)(2,1)S(1)}, u32[]{:S(2)}, u32[]{:S(2)}) collective-permute-start(bf16[224,128]{1,0:T(8,128)(2,1)S(1)} %get-tuple-element.31.w0), channel_id=1, source_target_pairs={{0,1},{1,0},{2,3},{3,2},{4,5},{5,4},{6,7},{7,6},{8,9},{9,8},{10,11... | collective-permute-start | bytes 172040 | tf_op jit(solution)/shard_map/ppermute | solution.py:234
  11.1 2.5 %collective-permute-start.9 = (bf16[224,128]{1,0:T(8,128)(2,1)S(1)}, bf16[224,128]{1,0:T(8,128)(2,1)S(1)}, u32[]{:S(2)}, u32[]{:S(2)}) collective-permute-start(bf16[224,128]{1,0:T(8,128)(2,1)S(1)} %collective-permute-done.4.w2), channel_id=1, source_target_pairs={{0,1},{1,0},{2,3},{3,2},{4,5},{5,4},{6,7},{7,6},{8,9},{9,8},{10,11... | collective-permute-start | bytes 172040 | tf_op jit(solution)/shard_map/ppermute | solution.py:234
  11.6 5.4 %collective-permute-start.6 = (bf16[256,128]{1,0:T(8,128)(2,1)S(1)}, bf16[256,128]{1,0:T(8,128)(2,1)S(1)}, u32[]{:S(2)}, u32[]{:S(2)}) collective-permute-start(bf16[256,128]{1,0:T(8,128)(2,1)S(1)} %pad_maximum_fusion), channel_id=1, source_target_pairs={{0,2},{1,3},{2,0},{3,1},{4,6},{5,7},{6,4},{7,5},{8,10},{9,11},{10,... | collective-permute-start | bytes 196616 | tf_op jit(solution)/shard_map/ppermute | solution.py:234

commit v4 on v3

--- a/solution.py
+++ b/solution.py
@@ -63,10 +63,8 @@
     out[...] = pick_columns((30, 31, 0, 1))
 
 
-def first_kernel(bias, select, f, mask, one, rims, weights):
-    rims[0:128] = dot(f[...], select[...]).astype(BF)
-    opened = jnp.concatenate([open_cells(mask), jnp.zeros((8, CY * CZ), F32)], 0)
-    rims[128:144] = dot(opened.astype(BF), select[...]).astype(BF)
+def pack_kernel(bias, select, one, weights):
+    del select
     place = iota((16, 64), 1)
     column = bias_column(bias, (16, 64))
     high = column.astype(BF).astype(F32)
@@ -77,11 +75,21 @@
         weights[16 * t : 16 * t + 16] = jnp.concatenate([one[t], other], 1)
 
 
-def place_features(base, f, field, rims):
+def rims_kernel(odd_ref, select, f, near, mask, first_out, second_out):
+    lane = iota((144, 128), 1)
+    opened = jnp.concatenate([open_cells(mask), jnp.zeros((8, CY * CZ), F32)], 0).astype(BF)
+    own = dot(jnp.concatenate([f[...], opened], 0), select[...])
+    other = dot(jnp.concatenate([near[...], opened], 0), select[...])
+    last = jnp.where(lane < 64, own, roll(other, -64))
+    early = jnp.where(lane < 64, roll(own, 64), other)
+    odd = odd_ref[0] > 0
+    first_out[...] = jnp.where(odd, early, last).astype(BF)
+    second_out[...] = jnp.where(odd, last, early).astype(BF)
+
+
+def place_features(base, f, field, rim):
     planes = dot(swap_rows(16, 8), f[...])
-    rim = dot(planes.astype(BF), pick_columns((0, 1, 30, 31))).astype(BF)
-    for x in range(8):
-        rims[pl.ds(64 * x + base, 16)] = rim[16 * x : 16 * x + 16]
+    rim[...] = dot(planes.astype(BF), pick_columns((0, 1, 30, 31)))
     for e in range(3):
         moved = roll(planes, e - 1).astype(BF)
         for x in range(8):
@@ -103,6 +111,25 @@
     bias_one[pl.ds(base, 16)] = jnp.broadcast_to(total, (16, 128))
 
 
+def windows(x):
+    return [(q, x + 1 - 2 * q) for q in range(4) if 0 <= x + 1 - 2 * q < 4]
+
+
+def place_edges(me, chip, below, above, rims, edges):
+    to_plane = swap_rows(16, 8)
+    lane = iota((128, 128), 1)
+    below, above = dot(to_plane, below), dot(to_plane, above)
+    both = (jnp.where(lane < 64, below, roll(above, -64)), jnp.where(lane < 64, roll(below, 64), above))
+    for core, outer in enumerate(both):
+        k = 2 * chip + core
+        base = pl.multiple_of((me ^ k) * 16, 16)
+        for e, moved in enumerate(with_neighbours(outer, rims[k])):
+            moved = moved.astype(BF)
+            for x in range(8):
+                for q, place in windows(x):
+                    edges[pl.ds(192 * place + 64 * e + base, 16), 128 * q : 128 * q + 128] = moved[16 * x : 16 * x + 16]
+
+
 def near_kernel(me_ref, bias, f0, f1, mask, two, field, rims, opened, open_rims, second, bias_two):
     field[0:192] = jnp.zeros((192, CY * CZ), BF)
     field[9 * 192 : 10 * 192] = jnp.zeros((192, CY * CZ), BF)
@@ -111,7 +138,7 @@
     open_rims[...] = dot(cells.astype(BF), pick_columns((0, 1, 30, 31)))
     me = me_ref[0]
     for k, f in enumerate((f0, f1)):
-        place_features(pl.multiple_of((me ^ k) * 16, 16), f, field, rims)
+        place_features(pl.multiple_of((me ^ k) * 16, 16), f, field, rims.at[k])
     blank = jnp.zeros((16, 64), BF)
     for e in range(3):
         for b in range(3):
@@ -124,7 +151,7 @@
 
 def far_kernel(me_ref, f2, field_in, rims_in, field, rims):
     del field_in, rims_in
-    place_features(pl.multiple_of((me_ref[0] ^ 2) * 16, 16), f2, field, rims)
+    place_features(pl.multiple_of((me_ref[0] ^ 2) * 16, 16), f2, field, rims.at[2])
 
 
 def inside():
@@ -132,12 +159,16 @@
     return jnp.where(lane >= CZ, 1.0, 0.0), jnp.where(lane < (CY - 1) * CZ, 1.0, 0.0)
 
 
-def one_kernel(me_ref, f3, w0, w1, w2, w3, opened, field_in, rims_in, field, rims, hidden, first, bias_one):
+def one_kernel(me_ref, f3, w0, w1, w2, w3, opened, below, above, field_in, rims_in, field, rims, hidden, first, bias_one, edges):
     del field_in, rims_in
     me = me_ref[0]
     for k, w in enumerate((w0, w1, w2, w3)):
         place_filters(pl.multiple_of((me ^ k) * 16, 16), w, first, bias_one)
-    place_features(pl.multiple_of((me ^ 3) * 16, 16), f3, field, rims)
+    place_features(pl.multiple_of((me ^ 3) * 16, 16), f3, field, rims.at[3])
+
+    edges[0:192, 0:128] = jnp.zeros((192, 128), BF)
+    edges[576:768, 384:512] = jnp.zeros((192, 128), BF)
+    place_edges(me, 0, below[0:128], above[0:128], rims, edges)
 
     after_first, before_last = inside()
     z = iota((8, CY * CZ), 1)[0:1] & 31
@@ -154,33 +185,29 @@
             hidden[64 * (x + 1) : 64 * (x + 2)] = value.astype(BF)
 
 
-def two_kernel(me_ref, h0, h1, h23, mask_halo, rims, open_rims, first, bias_one, second, bias_two, opened, hidden,
-               out_ref, halo, field, edge, terms, last):
+def two_kernel(me_ref, below, above, there, rims, open_rims, first, bias_one, second, bias_two, opened, hidden, edges_in,
+               out_hbm, edges, edge, terms, sums, last, out, sems):
+    del edges_in
     me = me_ref[0]
-    to_plane = swap_rows(16, 8)
-    for k, h in enumerate((h0, h1, h23.at[0:128], h23.at[128:256])):
-        base = pl.multiple_of((me ^ k) * 16, 16)
-        planes = dot(to_plane, h[...]).astype(BF)
-        for x in range(8):
-            halo[pl.ds(64 * x + base, 16)] = planes[16 * x : 16 * x + 16]
-
-    def windows(x):
-        return [(q, x + 1 - 2 * q) for q in range(4) if 0 <= x + 1 - 2 * q < 4]
-
-    field[0:192, 0:128] = jnp.zeros((192, 128), BF)
-    field[576:768, 384:512] = jnp.zeros((192, 128), BF)
-    for e, moved in enumerate(with_neighbours(halo[...].astype(F32), rims[...].astype(F32))):
-        moved = moved.astype(BF)
-        for x in range(8):
-            for q, place in windows(x):
-                field[192 * place + 64 * e : 192 * place + 64 * e + 64, 128 * q : 128 * q + 128] = moved[64 * x : 64 * x + 64]
-    open_edge = with_neighbours(mask_halo[0:8].astype(F32), open_rims[...])[1]
+    has_before, has_after = inside()
+
+    def settled(q):
+        taken = dot(second[...], hidden[128 * q : 128 * q + 256])
+        moved = [sum(roll(taken[96 * e + 32 * b : 96 * e + 32 * b + 32], e - 1) for e in range(3)) for b in range(3)]
+        sums[32 * q : 32 * q + 32] = roll(moved[0], -CZ) * has_before + moved[1] + roll(moved[2], CZ) * has_after
+
+    settled(0)
+    place_edges(me, 1, there[0:128], there[128:256], rims, edges)
+    lane = iota((8, 128), 1)
+    open_halo = jnp.where(lane < 64, below[128:136].astype(F32), roll(above[128:136].astype(F32), -64))
+    open_edge = with_neighbours(open_halo, open_rims[...])[1]
+    settled(1)
 
     y = iota((8, 512), 1)[0:1] & 31
     after_first = jnp.where(y > 0, 1.0, 0.0)
     before_last = jnp.where(y < CY - 1, 1.0, 0.0)
-    sums = dot(first[...], field[...])
-    total = roll(sums[0:128], -1) * after_first + sums[128:256] + roll(sums[256:384], 1) * before_last
+    taken = dot(first[...], edges[...])
+    total = roll(taken[0:128], -1) * after_first + taken[128:256] + roll(taken[256:384], 1) * before_last
     edge[0:64, 0:128] = jnp.zeros((64, 128), BF)
     edge[192:256, 384:512] = jnp.zeros((64, 128), BF)
     for half in range(2):
@@ -190,10 +217,11 @@
         for k in range(4):
             for q, place in windows(2 * k + half):
                 edge[64 * place : 64 * place + 64, 128 * q : 128 * q + 128] = value[:, 128 * k : 128 * k + 128]
-
-    sums = dot(second[...], edge[...])
+    settled(2)
+
+    taken = dot(second[...], edge[...])
     before, same, behind = [
-        roll(sums[r : r + 32], -1) * after_first + sums[r + 32 : r + 64] + roll(sums[r + 64 : r + 96], 1) * before_last
+        roll(taken[r : r + 32], -1) * after_first + taken[r + 32 : r + 64] + roll(taken[r + 64 : r + 96], 1) * before_last
         for r in (0, 96, 192)
     ]
     lane = iota((32, 512), 1) & 127
@@ -204,22 +232,23 @@
     for q in range(4):
         terms[32 * q : 32 * q + 32] = high[:, 128 * q : 128 * q + 128]
         terms[128 + 32 * q : 160 + 32 * q] = low[:, 128 * q : 128 * q + 128]
+    settled(3)
+
     cell = iota((8, CY * CZ), 1)[0:1]
     z = cell & 31
     row = jnp.where((z < 2) | (z >= 30), 32 * jnp.where(z < 2, z, z - 28) + (cell >> 5), -1)
-    spread = jnp.where(iota((128, CY * CZ), 0) == row, 1.0, 0.0).astype(BF)
-
-    after_first, before_last = inside()
-    for q in range(4):
-        sums = dot(second[...], hidden[128 * q : 128 * q + 256])
-        moved = [sum(roll(sums[96 * e + 32 * b : 96 * e + 32 * b + 32], e - 1) for e in range(3)) for b in range(3)]
-        total = roll(moved[0], -CZ) * after_first + moved[1] + roll(moved[2], CZ) * before_last
-        total += dot(terms[32 * q : 32 * q + 32], spread) + dot(terms[128 + 32 * q : 160 + 32 * q], spread)
-        for half in range(2):
-            x = 2 * q + half
-            value = jnp.maximum(total[16 * half : 16 * half + 16] + bias_two[:, 0:1], 0.0) * opened[x : x + 1]
-            last[16 * x : 16 * x + 16] = value.astype(BF)
-    out_ref[...] = dot(swap_rows(8, 16), last[...]).astype(BF)
+    spread = dot(terms[...], jnp.where(iota((128, CY * CZ), 0) == row, 1.0, 0.0).astype(BF))
+    to_channel = swap_rows(8, 16)
+    copies = []
+    for part, lanes in enumerate((slice(0, 512), slice(512, 1024))):
+        for x in range(8):
+            total = sums[16 * x : 16 * x + 16, lanes] + spread[16 * x : 16 * x + 16, lanes] + spread[128 + 16 * x : 144 + 16 * x, lanes]
+            last[16 * x : 16 * x + 16, lanes] = (jnp.maximum(total + bias_two[:, 0:1], 0.0) * opened[x : x + 1, lanes]).astype(BF)
+        out[:, lanes] = dot(to_channel, last[:, lanes]).astype(BF)
+        copies.append(pltpu.make_async_copy(out.at[:, lanes], out_hbm.at[:, lanes], sems.at[part]))
+        copies[-1].start()
+    for copy in copies:
+        copy.wait()
 
 
 def cost(micros):
@@ -257,21 +286,30 @@
         cost_estimate=cost(SELECT),
         name="select",
     )()
-    rims, weights = pl.pallas_call(
-        first_kernel,
-        out_shape=[shape((144, 128), BF), shape((224, 128), BF)],
+    weights = pl.pallas_call(
+        pack_kernel,
+        out_shape=shape((224, 128), BF),
+        in_specs=[smem, vmem, vmem],
+        out_specs=vmem,
+        compiler_params=pltpu.CompilerParams(vmem_limit_bytes=8 << 20),
+        cost_estimate=cost(0.5),
+        name="pack",
+    )(bias_one, select, weight_one.transpose(1, 0, 2))
+    odd = (lax.axis_index("col") % 2).astype(jnp.int32)
+    met_first, met_second = pl.pallas_call(
+        rims_kernel,
+        out_shape=[shape((144, 128), BF)] * 2,
         in_specs=[smem] + [vmem] * 4,
         out_specs=[vmem] * 2,
         compiler_params=pltpu.CompilerParams(vmem_limit_bytes=8 << 20),
-        cost_estimate=cost(1),
-        name="first",
-    )(bias_one, select, cells, solid_mask, weight_one.transpose(1, 0, 2))
-
-    odd = exchange(rims, 1)
-    even = exchange(rims, 0)
+        cost_estimate=cost(0.5),
+        name="rims",
+    )(odd.reshape(1), select, cells, near, solid_mask)
+    met_second = exchange(met_second, 1)
+    met_first = exchange(met_first, 0)
     weights_far, weights_near = across(weights, 2), across(weights, 1)
 
-    field_shape, rims_shape = shape((1920, 1024), BF), shape((512, 128), BF)
+    field_shape, rims_shape = shape((1920, 1024), BF), shape((4, 128, 128), F32)
     field, rim_cells, opened, open_rims, second, bias_second = pl.pallas_call(
         near_kernel,
         out_shape=[field_shape, rims_shape, shape((8, 1024), F32), shape((8, 128), F32), shape((288, 256), BF), shape((16, 128), F32)],
@@ -297,43 +335,40 @@
     weights_far, rim_cells = lax.optimization_barrier((weights_far, rim_cells))
     weights_cross = across(weights_far, 1)
 
-    odd, even, opened = lax.optimization_barrier((odd, even, opened))
-    is_odd = lax.axis_index("col") % 2 == 1
-    side = lax.broadcasted_iota(jnp.int32, (144, 128), 1)
-    halo = jnp.where((side < 64) == is_odd, even, odd)
-    mask_halo = halo[128:]
-    halo = halo[:128]
-    halo_near = across(halo, 1)
-    halo_here, rim_cells = lax.optimization_barrier((jnp.concatenate([halo, halo_near], 0), rim_cells))
-    halo_there = across(halo_here, 2)
-
-    _, rim_cells, hidden, first, bias = pl.pallas_call(
+    met_first, met_second, rim_cells = lax.optimization_barrier((met_first, met_second, rim_cells))
+    before = jnp.where(odd == 1, met_first, met_second)
+    after_it = jnp.where(odd == 1, met_second, met_first)
+    there = across(jnp.concatenate([before[:128], after_it[:128]], 0), 2)
+
+    _, rim_cells, hidden, first, bias, edges = pl.pallas_call(
         one_kernel,
-        out_shape=[field_shape, rims_shape, shape((640, 1024), BF), shape((384, 768), BF), shape((64, 128), F32)],
-        in_specs=[smem] + [vmem] * 8,
-        out_specs=[vmem] * 5,
-        input_output_aliases={7: 0, 8: 1},
+        out_shape=[field_shape, rims_shape, shape((640, 1024), BF), shape((384, 768), BF), shape((64, 128), F32), shape((768, 512), BF)],
+        in_specs=[smem] + [vmem] * 10,
+        out_specs=[vmem] * 6,
+        input_output_aliases={9: 0, 10: 1},
         compiler_params=pltpu.CompilerParams(vmem_limit_bytes=24 << 20),
         cost_estimate=cost(4),
         name="one",
-    )(me, cross, weights, weights_near, weights_far, weights_cross, opened, field, rim_cells)
-
-    result = pl.pallas_call(
+    )(me, cross, weights, weights_near, weights_far, weights_cross, opened, before, after_it, field, rim_cells)
+
+    result, _ = pl.pallas_call(
         two_kernel,
-        out_shape=shape((128, 1024), BF),
+        out_shape=[shape((128, 1024), BF), shape((768, 512), BF)],
         in_specs=[smem] + [vmem] * 12,
-        out_specs=vmem,
+        out_specs=[pl.BlockSpec(memory_space=pltpu.HBM), vmem],
+        input_output_aliases={12: 1},
         scratch_shapes=[
-            pltpu.VMEM((512, 128), BF),
-            pltpu.VMEM((768, 512), BF),
             pltpu.VMEM((256, 512), BF),
             pltpu.VMEM((256, 128), BF),
+            pltpu.VMEM((128, 1024), F32),
             pltpu.VMEM((128, 1024), BF),
+            pltpu.VMEM((128, 1024), BF),
+            pltpu.SemaphoreType.DMA((2,)),
         ],
         compiler_params=pltpu.CompilerParams(vmem_limit_bytes=16 << 20),
         cost_estimate=cost(3),
         name="two",
-    )(me, halo, halo_near, halo_there, mask_halo, rim_cells, open_rims, first, bias, second, bias_second, opened, hidden)
+    )(me, before, after_it, there, rim_cells, open_rims, first, bias, second, bias_second, opened, hidden, edges)
     return result.reshape(16, 8, 1, 1024)
 
 

time: 21 us -> 20.3 us (0.967); the launches traced: 20.6 us -> 20.2 us
  starting transfers between devices: 9.26 us -> 8.16 us
  waiting for transfers between devices: 1.49 us -> 2.34 us
    ppermute x8 -> x7, starting transfers between devices: 7.03 us -> 5.92 us  [across(): lax.ppermute(v, 'ch', [(i, i ^ bit) for i in range(lax.axis_size('ch'))])]
    ppermute x8 -> x7, waiting for transfers between devices: 1.48 us -> 2.34 us  [across(): lax.ppermute(v, 'ch', [(i, i ^ bit) for i in range(lax.axis_size('ch'))])]
    pallas_call x2 -> x3, Pallas kernels: 4.38 us -> 4.15 us  [the longest x1 3.14 us: one_row(): pl.pallas_call(two_kernel, out_shape=[shape((128, 1024), BF), shape((768,...]
  transfers between devices with their start and end apart: 10 -> 9, of which waited for: 1 -> 2; matrix products, arithmetic and copies ran while one was open for 0% -> 0% of each run, Pallas kernels for 29% -> 31%
where the time goes in v4:
time: 20.3 us; the launch traced here: 20.2 us
  Pallas kernels  9.47 us (47%)
  starting transfers between devices  8.16 us (40%)
  waiting for transfers between devices  2.34 us (12%)
    ppermute x7, starting transfers between devices, across(): lax.ppermute(v, 'ch', [(i, i ^ bit) for i in range(lax.axis_size('ch'))])  5.92 us
    pallas_call x1, Pallas kernels, one_row(): pl.pallas_call(one_kernel, out_shape=[field_shape, rims_shape, shape((640...  3.44 us
    pallas_call x1, Pallas kernels, one_row(): pl.pallas_call(two_kernel, out_shape=[shape((128, 1024), BF), shape((768,...  3.14 us
    ppermute x7, waiting for transfers between devices, across(): lax.ppermute(v, 'ch', [(i, i ^ bit) for i in range(lax.axis_size('ch'))])  2.34 us
    ppermute x2, starting transfers between devices, exchange(): return lax.ppermute(v, 'col', route)  2.24 us
    pallas_call x1, Pallas kernels, one_row(): pl.pallas_call(near_kernel, out_shape=[field_shape, rims_shape, shape((8,...  1.38 us
    pallas_call x1, Pallas kernels, one_row(): pl.pallas_call(pack_kernel, out_shape=shape((224, 128), BF), in_specs=[sm...  0.63 us
    pallas_call x1, Pallas kernels, one_row(): pl.pallas_call(far_kernel, out_shape=[field_shape, rims_shape], in_specs=...  0.43 us
  transfers between devices with their start and end apart: 9, of which 2 were waited for; matrix products, arithmetic and copies ran while one was open for 0% of the time, Pallas kernels for 31%

profile of v4, /device:TPU:0, one launch (start us, length us, event | category | flops | bytes accessed | tf_op | source)
XLA Modules:
  0.0 20.2 jit_solution(2099073296804748058)
XLA Ops:
  0.0 0.0 copy-start.4
  0.0 0.0 copy-start.5
  0.0 0.0 copy-start
  0.0 0.0 copy-start.2
  0.0 0.5 %collective-permute-start = (bf16[128,1024]{1,0:T(8,128)(2,1)}, bf16[128,1024]{1,0:T(8,128)(2,1)S(1)}, u32[]{:S(2)}, u32[]{:S(2)}) collective-permute-start(bf16[128,1024]{1,0:T(8,128)(2,1)} %bitcast.8), channel_id=1, source_target_pairs={{0,1},{1,0},{2,3},{3,2},{4,5},{5,4},{6,7},{7,6},{8,9},{9,8},{10,11... | collective-permute-start | bytes 786440 | tf_op jit(solution)/shard_map/ppermute | solution.py:263
  0.5 2.6 %collective-permute-start.4 = (bf16[128,1024]{1,0:T(8,128)(2,1)}, bf16[128,1024]{1,0:T(8,128)(2,1)S(1)}, u32[]{:S(2)}, u32[]{:S(2)}) collective-permute-start(bf16[128,1024]{1,0:T(8,128)(2,1)} %bitcast.9), channel_id=1, source_target_pairs={{0,2},{1,3},{2,0},{3,1},{4,6},{5,7},{6,4},{7,5},{8,10},{9,11},{10,... | collective-permute-start | bytes 786440 | tf_op jit(solution)/shard_map/ppermute | solution.py:263
  3.1 0.1 select.3
  3.2 0.0 copy-start.1
  3.2 0.0 copy-start.3
  3.2 0.0 copy-done.4
  3.2 0.0 copy-done.5
  3.2 0.6 %pack.1.w0 = bf16[224,128]{1,0:T(8,128)(2,1)S(1)} custom-call(f32[16]{0:T(128)S(1)} %copy-done.5, bf16[1024,128]{1,0:T(8,128)(2,1)S(1)} %select.3, bf16[27,16,64]{2,1,0:T(8,128)(2,1)S(1)} %bitcast.13), custom_call_target="tpu_custom_call" | custom-call | flops 575000000 | bytes 1500000 | tf_op jit(solution)/shard_map/pack/pallas_call | solution.py:289
  3.8 0.7 %collective-permute-start.3 = (bf16[224,128]{1,0:T(8,128)(2,1)S(1)}, bf16[224,128]{1,0:T(8,128)(2,1)S(1)}, u32[]{:S(2)}, u32[]{:S(2)}) collective-permute-start(bf16[224,128]{1,0:T(8,128)(2,1)S(1)} %pack.1.w0), channel_id=1, source_target_pairs={{0,2},{1,3},{2,0},{3,1},{4,6},{5,7},{6,4},{7,5},{8,10},{9,11},{10,... | collective-permute-start | bytes 172040 | tf_op jit(solution)/shard_map/ppermute | solution.py:263
  4.5 0.0 collective-permute-done.near.f1
  4.5 0.0 copy-done
  4.5 0.0 copy-done.2
  4.5 0.4 %rims.1 = (bf16[144,128]{1,0:T(8,128)(2,1)S(1)}, bf16[144,128]{1,0:T(8,128)(2,1)S(1)}) custom-call(s32[1]{0:T(128)} %bitcast.1.odd_ref, bf16[1024,128]{1,0:T(8,128)(2,1)S(1)} %select.3, bf16[128,1024]{1,0:T(8,128)(2,1)S(1)} %bitcast.10, bf16[128,1024]{1,0:T(8,128)(2,1)S(1)} %collective-permute-done.near.f1, s32[8,1,1024]{2,1,0:T(1,128)S(1)} %copy-done.2), custom_call_target="tpu_custom_call" | custom-call | flops 575000000 | bytes 1500000 | tf_op jit(solution)/shard_map/rims/pallas_call | solution.py:299
  4.9 1.6 %collective-permute-start.1 = (bf16[144,128]{1,0:T(8,128)(2,1)S(1)}, bf16[144,128]{1,0:T(8,128)(2,1)S(1)}, u32[]{:S(2)}, u32[]{:S(2)}) collective-permute-start(bf16[144,128]{1,0:T(8,128)(2,1)S(1)} %get-tuple-element.27), channel_id=1, source_target_pairs={{0,4},{4,0},{8,12},{12,8},{16,20},{20,16},{24,28},{28,24},{1,5},{5... | collective-permute-start | bytes 110600 | tf_op jit(solution)/shard_map/ppermute | solution.py:272
  6.5 0.7 %collective-permute-start.2 = (bf16[144,128]{1,0:T(8,128)(2,1)S(1)}, bf16[144,128]{1,0:T(8,128)(2,1)S(1)}, u32[]{:S(2)}, u32[]{:S(2)}) collective-permute-start(bf16[144,128]{1,0:T(8,128)(2,1)S(1)} %get-tuple-element.28), channel_id=1, source_target_pairs={{4,8},{8,4},{12,16},{16,12},{20,24},{24,20},{5,9},{9,5},{13,17},{1... | collective-permute-start | bytes 110600 | tf_op jit(solution)/shard_map/ppermute | solution.py:272
  7.2 0.1 collective-permute-start.7
  7.3 0.0 copy-done.1
  7.3 0.0 copy-done.3
  7.3 1.4 %near.1 = (bf16[1920,1024]{1,0:T(8,128)(2,1)S(1)}, f32[4,128,128]{2,1,0:T(8,128)S(1)}, f32[8,1024]{1,0:T(8,128)S(1)}, f32[8,128]{1,0:T(8,128)S(1)}, bf16[288,256]{1,0:T(8,128)(2,1)S(1)}, /*index=5*/f32[16,128]{1,0:T(8,128)S(1)}) custom-call(s32[1]{0:T(128)} %bitcast.me_ref, f32[16]{0:T(128)S(1)} %copy-done.3, bf16[128,1024]{1,0:T(8,128)(2,1)S(1)} %bitcast.11, ...), custom_call_target="tpu_custom_call" | custom-call | flops 115000000 | bytes 300000 | tf_op jit(solution)/shard_map/near/pallas_call | solution.py:313
  8.7 1.8 %collective-permute-done.4.f2 = bf16[128,1024]{1,0:T(8,128)(2,1)S(1)} collective-permute-done((bf16[128,1024]{1,0:T(8,128)(2,1)}, bf16[128,1024]{1,0:T(8,128)(2,1)S(1)}, u32[]{:S(2)}, u32[]{:S(2)}) %collective-permute-start.4) | collective-permute-done | bytes 262176 | tf_op jit(solution)/shard_map/ppermute | solution.py:263
  10.5 0.0 collective-permute-start.6
  10.5 0.4 %far.1 = (bf16[1920,1024]{1,0:T(8,128)(2,1)S(1)}, f32[4,128,128]{2,1,0:T(8,128)S(1)}) custom-call(s32[1]{0:T(128)} %bitcast.me_ref, bf16[128,1024]{1,0:T(8,128)(2,1)S(1)} %collective-permute-done.4.f2, bf16[1920,1024]{1,0:T(8,128)(2,1)S(1)} %get-tuple-element.31.field_in, ...), custom_call_target="tpu_custom_call", output_to_operand_aliasing={{0}: (2, {}), {1}: (3, {})} | custom-call | flops 115000000 | bytes 300000 | tf_op jit(solution)/shard_map/far/pallas_call | solution.py:325
  10.9 0.5 %collective-permute-done.3.w2 = bf16[224,128]{1,0:T(8,128)(2,1)S(1)} collective-permute-done((bf16[224,128]{1,0:T(8,128)(2,1)S(1)}, bf16[224,128]{1,0:T(8,128)(2,1)S(1)}, u32[]{:S(2)}, u32[]{:S(2)}) %collective-permute-start.3) | collective-permute-done | bytes 57376 | tf_op jit(solution)/shard_map/ppermute | solution.py:263
  11.4 0.1 collective-permute-start.8
  11.5 0.0 collective-permute-done.1
  11.5 0.0 collective-permute-done.2
  11.6 2.0 %collective-permute-start.5 = (bf16[256,128]{1,0:T(8,128)(2,1)S(1)}, bf16[256,128]{1,0:T(8,128)(2,1)S(1)}, u32[]{:S(2)}, u32[]{:S(2)}) collective-permute-start(bf16[256,128]{1,0:T(8,128)(2,1)S(1)} %pad_maximum_fusion), channel_id=1, source_target_pairs={{0,2},{1,3},{2,0},{3,1},{4,6},{5,7},{6,4},{7,5},{8,10},{9,11},{10,... | collective-permute-start | bytes 196616 | tf_op jit(solution)/shard_map/ppermute | solution.py:263
  13.6 0.0 collective-permute-done.7.w1
  13.6 0.0 collective-permute-done.8.w3
  13.6 0.0 collective-permute-done.6.f3
  13.6 3.4 %one.1 = (bf16[1920,1024]{1,0:T(8,128)(2,1)S(1)}, f32[4,128,128]{2,1,0:T(8,128)S(1)}, bf16[640,1024]{1,0:T(8,128)(2,1)S(1)}, bf16[384,768]{1,0:T(8,128)(2,1)S(1)...) custom-call(s32[1]{0:T(128)} %bitcast.me_ref, ...), custom_call_target="tpu_custom_call", output_to_operand_aliasing={{0}: (9, {}), {1}: (10, {})} | custom-call | flops 4600000000 | bytes 12000000 | tf_op jit(solution)/shard_map/one/pallas_call | solution.py:343
  17.0 0.0 collective-permute-done.5.there
  17.0 3.1 %two.1 = (bf16[128,1024]{1,0:T(8,128)(2,1)}, bf16[768,512]{1,0:T(8,128)(2,1)S(1)}) custom-call(s32[1]{0:T(128)} %bitcast.me_ref, bf16[144,128]{1,0:T(8,128)(2,1)S(1)} %get-tuple-element.50.below, bf16[144,128]{1,0:T(8,128)(2,1)S(1)} %get-tuple-element.49.above, bf16[256,128]{1,0:T(8,128)(2,1)S(1)} %collective-permute-done.5.there, ...), custom_call_target="tpu_custom_call", output_to_operand_aliasing={{1}: (12, {})} | custom-call | flops 3449999872 | bytes 9000000 | tf_op jit(solution)/shard_map/two/pallas_call | solution.py:354
  (4 shorter events, 0.0 us)
Async XLA Ops:
  0.0 3.2 %copy-start.4 = (bf16[16,27,64]{2,0,1:T(8,128)(2,1)S(1)}, bf16[16,27,64]{2,0,1:T(8,128)(2,1)}, u32[]{:S(2)}) copy-start(bf16[16,27,64]{2,0,1:T(8,128)(2,1)} %param.8) | copy-start | bytes 165892
  0.0 3.2 %copy-start.5 = (f32[16]{0:T(128)S(1)}, f32[16]{0:T(128)}, u32[]{:S(2)}) copy-start(f32[16]{0:T(128)} %bias.2) | copy-start | bytes 196
  0.0 4.5 %copy-start = (bf16[16,8,1,1024]{3,1,2,0:T(8,128)(2,1)S(1)}, bf16[16,8,1,1024]{3,1,2,0:T(8,128)(2,1)}, u32[]{:S(2)}) copy-start(bf16[16,8,1,1024]{3,1,2,0:T(8,128)(2,1)} %param.6) | copy-start | bytes 786436
  0.0 4.5 %copy-start.2 = (s32[8,1,1024]{2,1,0:T(1,128)S(1)}, s32[8,1,1024]{2,1,0:T(1,128)}, u32[]{:S(2)}) copy-start(s32[8,1,1024]{2,1,0:T(1,128)} %mask.3) | copy-start | bytes 98308
  0.0 4.5 %collective-permute-start = (bf16[128,1024]{1,0:T(8,128)(2,1)}, bf16[128,1024]{1,0:T(8,128)(2,1)S(1)}, u32[]{:S(2)}, u32[]{:S(2)}) collective-permute-start(bf16[128,1024]{1,0:T(8,128)(2,1)} %bitcast.8), channel_id=1, source_target_pairs={{0,1},{1,0},{2,3},{3,2},{4,5},{5,4},{6,7},{7,6},{8,9},{9,8},{10,11... | collective-permute-start | bytes 786440 | tf_op jit(solution)/shard_map/ppermute | solution.py:263
  0.5 9.9 %collective-permute-start.4 = (bf16[128,1024]{1,0:T(8,128)(2,1)}, bf16[128,1024]{1,0:T(8,128)(2,1)S(1)}, u32[]{:S(2)}, u32[]{:S(2)}) collective-permute-start(bf16[128,1024]{1,0:T(8,128)(2,1)} %bitcast.9), channel_id=1, source_target_pairs={{0,2},{1,3},{2,0},{3,1},{4,6},{5,7},{6,4},{7,5},{8,10},{9,11},{10,... | collective-permute-start | bytes 786440 | tf_op jit(solution)/shard_map/ppermute | solution.py:263
  3.2 4.1 %copy-start.1 = (bf16[16,27,64]{2,0,1:T(8,128)(2,1)S(1)}, bf16[16,27,64]{2,0,1:T(8,128)(2,1)}, u32[]{:S(2)}) copy-start(bf16[16,27,64]{2,0,1:T(8,128)(2,1)} %param.10) | copy-start | bytes 165892
  3.2 4.1 %copy-start.3 = (f32[16]{0:T(128)S(1)}, f32[16]{0:T(128)}, u32[]{:S(2)}) copy-start(f32[16]{0:T(128)} %bias.3) | copy-start | bytes 196
  3.8 7.6 %collective-permute-start.3 = (bf16[224,128]{1,0:T(8,128)(2,1)S(1)}, bf16[224,128]{1,0:T(8,128)(2,1)S(1)}, u32[]{:S(2)}, u32[]{:S(2)}) collective-permute-start(bf16[224,128]{1,0:T(8,128)(2,1)S(1)} %pack.1.w0), channel_id=1, source_target_pairs={{0,2},{1,3},{2,0},{3,1},{4,6},{5,7},{6,4},{7,5},{8,10},{9,11},{10,... | collective-permute-start | bytes 172040 | tf_op jit(solution)/shard_map/ppermute | solution.py:263
  4.9 6.6 %collective-permute-start.1 = (bf16[144,128]{1,0:T(8,128)(2,1)S(1)}, bf16[144,128]{1,0:T(8,128)(2,1)S(1)}, u32[]{:S(2)}, u32[]{:S(2)}) collective-permute-start(bf16[144,128]{1,0:T(8,128)(2,1)S(1)} %get-tuple-element.27), channel_id=1, source_target_pairs={{0,4},{4,0},{8,12},{12,8},{16,20},{20,16},{24,28},{28,24},{1,5},{5... | collective-permute-start | bytes 110600 | tf_op jit(solution)/shard_map/ppermute | solution.py:272
  6.5 5.0 %collective-permute-start.2 = (bf16[144,128]{1,0:T(8,128)(2,1)S(1)}, bf16[144,128]{1,0:T(8,128)(2,1)S(1)}, u32[]{:S(2)}, u32[]{:S(2)}) collective-permute-start(bf16[144,128]{1,0:T(8,128)(2,1)S(1)} %get-tuple-element.28), channel_id=1, source_target_pairs={{4,8},{8,4},{12,16},{16,12},{20,24},{24,20},{5,9},{9,5},{13,17},{1... | collective-permute-start | bytes 110600 | tf_op jit(solution)/shard_map/ppermute | solution.py:272
  7.2 6.4 %collective-permute-start.7 = (bf16[224,128]{1,0:T(8,128)(2,1)S(1)}, bf16[224,128]{1,0:T(8,128)(2,1)S(1)}, u32[]{:S(2)}, u32[]{:S(2)}) collective-permute-start(bf16[224,128]{1,0:T(8,128)(2,1)S(1)} %pack.1.w0), channel_id=1, source_target_pairs={{0,1},{1,0},{2,3},{3,2},{4,5},{5,4},{6,7},{7,6},{8,9},{9,8},{10,11... | collective-permute-start | bytes 172040 | tf_op jit(solution)/shard_map/ppermute | solution.py:263
  10.5 3.1 %collective-permute-start.6 = (bf16[128,1024]{1,0:T(8,128)(2,1)S(1)}, bf16[128,1024]{1,0:T(8,128)(2,1)S(1)}, u32[]{:S(2)}, u32[]{:S(2)}) collective-permute-start(bf16[128,1024]{1,0:T(8,128)(2,1)S(1)} %collective-permute-done.4.f2), channel_id=1, source_target_pairs={{0,1},{1,0},{2,3},{3,2},{4,5},{5,4},{6,7},{7,6},{8,9},{9,8},{10,11... | collective-permute-start | bytes 786440 | tf_op jit(solution)/shard_map/ppermute | solution.py:263
  11.4 2.1 %collective-permute-start.8 = (bf16[224,128]{1,0:T(8,128)(2,1)S(1)}, bf16[224,128]{1,0:T(8,128)(2,1)S(1)}, u32[]{:S(2)}, u32[]{:S(2)}) collective-permute-start(bf16[224,128]{1,0:T(8,128)(2,1)S(1)} %collective-permute-done.3.w2), channel_id=1, source_target_pairs={{0,1},{1,0},{2,3},{3,2},{4,5},{5,4},{6,7},{7,6},{8,9},{9,8},{10,11... | collective-permute-start | bytes 172040 | tf_op jit(solution)/shard_map/ppermute | solution.py:263
  11.6 5.5 %collective-permute-start.5 = (bf16[256,128]{1,0:T(8,128)(2,1)S(1)}, bf16[256,128]{1,0:T(8,128)(2,1)S(1)}, u32[]{:S(2)}, u32[]{:S(2)}) collective-permute-start(bf16[256,128]{1,0:T(8,128)(2,1)S(1)} %pad_maximum_fusion), channel_id=1, source_target_pairs={{0,2},{1,3},{2,0},{3,1},{4,6},{5,7},{6,4},{7,5},{8,10},{9,11},{10,... | collective-permute-start | bytes 196616 | tf_op jit(solution)/shard_map/ppermute | solution.py:263

commit v5 on v4

--- a/solution.py
+++ b/solution.py
@@ -52,11 +52,8 @@
 
 
 def bias_column(bias, shape):
-    row = iota(shape, 0)
-    column = jnp.zeros(shape, F32)
-    for o in range(16):
-        column = jnp.where(row == o, bias[o], column)
-    return column
+    diagonal = jnp.where(iota((16, 16), 0) == iota((16, 16), 1), bias[...], 0.0)
+    return jnp.broadcast_to(jnp.sum(diagonal, 1, keepdims=True), shape)
 
 
 def select_kernel(out):
@@ -75,16 +72,11 @@
         weights[16 * t : 16 * t + 16] = jnp.concatenate([one[t], other], 1)
 
 
-def rims_kernel(odd_ref, select, f, near, mask, first_out, second_out):
-    lane = iota((144, 128), 1)
+def rims_kernel(select, f, mask, rims):
     opened = jnp.concatenate([open_cells(mask), jnp.zeros((8, CY * CZ), F32)], 0).astype(BF)
     own = dot(jnp.concatenate([f[...], opened], 0), select[...])
-    other = dot(jnp.concatenate([near[...], opened], 0), select[...])
-    last = jnp.where(lane < 64, own, roll(other, -64))
-    early = jnp.where(lane < 64, roll(own, 64), other)
-    odd = odd_ref[0] > 0
-    first_out[...] = jnp.where(odd, early, last).astype(BF)
-    second_out[...] = jnp.where(odd, last, early).astype(BF)
+    rims[0:144] = own.astype(BF)
+    rims[144:288] = roll(own, 64).astype(BF)
 
 
 def place_features(base, f, field, rim):
@@ -130,13 +122,13 @@
                     edges[pl.ds(192 * place + 64 * e + base, 16), 128 * q : 128 * q + 128] = moved[16 * x : 16 * x + 16]
 
 
-def near_kernel(me_ref, bias, f0, f1, mask, two, field, rims, opened, open_rims, second, bias_two):
+def near_kernel(bias, f0, f1, mask, two, field, rims, opened, open_rims, second, bias_two):
     field[0:192] = jnp.zeros((192, CY * CZ), BF)
     field[9 * 192 : 10 * 192] = jnp.zeros((192, CY * CZ), BF)
     cells = open_cells(mask)
     opened[...] = cells
     open_rims[...] = dot(cells.astype(BF), pick_columns((0, 1, 30, 31)))
-    me = me_ref[0]
+    me = lax.axis_index("ch")
     for k, f in enumerate((f0, f1)):
         place_features(pl.multiple_of((me ^ k) * 16, 16), f, field, rims.at[k])
     blank = jnp.zeros((16, 64), BF)
@@ -149,9 +141,9 @@
     bias_two[...] = bias_column(bias, (16, 128))
 
 
-def far_kernel(me_ref, f2, field_in, rims_in, field, rims):
+def far_kernel(f2, field_in, rims_in, field, rims):
     del field_in, rims_in
-    place_features(pl.multiple_of((me_ref[0] ^ 2) * 16, 16), f2, field, rims.at[2])
+    place_features(pl.multiple_of((lax.axis_index("ch") ^ 2) * 16, 16), f2, field, rims.at[2])
 
 
 def inside():
@@ -159,9 +151,9 @@
     return jnp.where(lane >= CZ, 1.0, 0.0), jnp.where(lane < (CY - 1) * CZ, 1.0, 0.0)
 
 
-def one_kernel(me_ref, f3, w0, w1, w2, w3, opened, below, above, field_in, rims_in, field, rims, hidden, first, bias_one, edges):
+def one_kernel(f3, w0, w1, w2, w3, opened, below, above, field_in, rims_in, field, rims, hidden, first, bias_one, edges):
     del field_in, rims_in
-    me = me_ref[0]
+    me = lax.axis_index("ch")
     for k, w in enumerate((w0, w1, w2, w3)):
         place_filters(pl.multiple_of((me ^ k) * 16, 16), w, first, bias_one)
     place_features(pl.multiple_of((me ^ 3) * 16, 16), f3, field, rims.at[3])
@@ -185,10 +177,10 @@
             hidden[64 * (x + 1) : 64 * (x + 2)] = value.astype(BF)
 
 
-def two_kernel(me_ref, below, above, there, rims, open_rims, first, bias_one, second, bias_two, opened, hidden, edges_in,
+def two_kernel(below, above, there, rims, open_rims, first, bias_one, second, bias_two, opened, hidden, edges_in,
                out_hbm, edges, edge, terms, sums, last, out, sems):
     del edges_in
-    me = me_ref[0]
+    me = lax.axis_index("ch")
     has_before, has_after = inside()
 
     def settled(q):
@@ -257,7 +249,6 @@
 
 def one_row(features, solid_mask, weight_one, bias_one, weight_two, bias_two):
     columns = lax.axis_size("col")
-    me = lax.axis_index("ch").astype(jnp.int32).reshape(1)
 
     def across(v, bit):
         return lax.ppermute(v, "ch", [(i, i ^ bit) for i in range(lax.axis_size("ch"))])
@@ -271,13 +262,11 @@
             route += [(c, c + 1), (c + 1, c)]
         return lax.ppermute(v, "col", route)
 
-    smem = pl.BlockSpec(memory_space=pltpu.SMEM)
     vmem = pl.BlockSpec(memory_space=pltpu.VMEM)
     shape = jax.ShapeDtypeStruct
 
     cells = features.reshape(128, 1024)
     far = across(cells, 2)
-    near = across(cells, 1)
     select = pl.pallas_call(
         select_kernel,
         out_shape=shape((1024, 128), BF),
@@ -289,74 +278,80 @@
     weights = pl.pallas_call(
         pack_kernel,
         out_shape=shape((224, 128), BF),
-        in_specs=[smem, vmem, vmem],
+        in_specs=[vmem, vmem, vmem],
         out_specs=vmem,
         compiler_params=pltpu.CompilerParams(vmem_limit_bytes=8 << 20),
         cost_estimate=cost(0.5),
         name="pack",
-    )(bias_one, select, weight_one.transpose(1, 0, 2))
-    odd = (lax.axis_index("col") % 2).astype(jnp.int32)
-    met_first, met_second = pl.pallas_call(
+    )(bias_one.reshape(1, 16), select, weight_one.transpose(1, 0, 2))
+    rims = pl.pallas_call(
         rims_kernel,
-        out_shape=[shape((144, 128), BF)] * 2,
-        in_specs=[smem] + [vmem] * 4,
-        out_specs=[vmem] * 2,
+        out_shape=shape((288, 128), BF),
+        in_specs=[vmem] * 3,
+        out_specs=vmem,
         compiler_params=pltpu.CompilerParams(vmem_limit_bytes=8 << 20),
         cost_estimate=cost(0.5),
         name="rims",
-    )(odd.reshape(1), select, cells, near, solid_mask)
-    met_second = exchange(met_second, 1)
-    met_first = exchange(met_first, 0)
+    )(select, cells, solid_mask)
+    rims_near = across(rims, 1)
+    near = across(after(cells, rims), 1)
+
+    odd = lax.axis_index("col") % 2 == 1
+    low = lax.broadcasted_iota(jnp.int32, (144, 128), 1) < 64
+    last = jnp.where(low, rims[:144], rims_near[144:])
+    early = jnp.where(low, rims[144:], rims_near[:144])
+    met_second = exchange(jnp.where(odd, last, early), 1)
+    met_first = exchange(jnp.where(odd, early, last), 0)
     weights_far, weights_near = across(weights, 2), across(weights, 1)
 
     field_shape, rims_shape = shape((1920, 1024), BF), shape((4, 128, 128), F32)
     field, rim_cells, opened, open_rims, second, bias_second = pl.pallas_call(
         near_kernel,
         out_shape=[field_shape, rims_shape, shape((8, 1024), F32), shape((8, 128), F32), shape((288, 256), BF), shape((16, 128), F32)],
-        in_specs=[smem, smem] + [vmem] * 4,
+        in_specs=[vmem] * 5,
         out_specs=[vmem] * 6,
         compiler_params=pltpu.CompilerParams(vmem_limit_bytes=16 << 20),
         cost_estimate=cost(0.1),
         name="near",
-    )(me, bias_two, cells, near, solid_mask, weight_two.transpose(1, 0, 2))
+    )(bias_two.reshape(1, 16), cells, near, solid_mask, weight_two.transpose(1, 0, 2))
 
     far = after(far, open_rims)
     cross = across(far, 1)
     field, rim_cells = pl.pallas_call(
         far_kernel,
         out_shape=[field_shape, rims_shape],
-        in_specs=[smem] + [vmem] * 3,
+        in_specs=[vmem] * 3,
         out_specs=[vmem] * 2,
-        input_output_aliases={2: 0, 3: 1},
+        input_output_aliases={1: 0, 2: 1},
         compiler_params=pltpu.CompilerParams(vmem_limit_bytes=16 << 20),
         cost_estimate=cost(0.1),
         name="far",
-    )(me, far, field, rim_cells)
+    )(far, field, rim_cells)
     weights_far, rim_cells = lax.optimization_barrier((weights_far, rim_cells))
     weights_cross = across(weights_far, 1)
 
-    met_first, met_second, rim_cells = lax.optimization_barrier((met_first, met_second, rim_cells))
-    before = jnp.where(odd == 1, met_first, met_second)
-    after_it = jnp.where(odd == 1, met_second, met_first)
+    met_second, met_first, rim_cells = lax.optimization_barrier((met_second, met_first, rim_cells))
+    before = jnp.where(odd, met_first, met_second)
+    after_it = jnp.where(odd, met_second, met_first)
     there = across(jnp.concatenate([before[:128], after_it[:128]], 0), 2)
 
     _, rim_cells, hidden, first, bias, edges = pl.pallas_call(
         one_kernel,
         out_shape=[field_shape, rims_shape, shape((640, 1024), BF), shape((384, 768), BF), shape((64, 128), F32), shape((768, 512), BF)],
-        in_specs=[smem] + [vmem] * 10,
+        in_specs=[vmem] * 10,
         out_specs=[vmem] * 6,
-        input_output_aliases={9: 0, 10: 1},
+        input_output_aliases={8: 0, 9: 1},
         compiler_params=pltpu.CompilerParams(vmem_limit_bytes=24 << 20),
         cost_estimate=cost(4),
         name="one",
-    )(me, cross, weights, weights_near, weights_far, weights_cross, opened, before, after_it, field, rim_cells)
+    )(cross, weights, weights_near, weights_far, weights_cross, opened, before, after_it, field, rim_cells)
 
     result, _ = pl.pallas_call(
         two_kernel,
         out_shape=[shape((128, 1024), BF), shape((768, 512), BF)],
-        in_specs=[smem] + [vmem] * 12,
+        in_specs=[vmem] * 12,
         out_specs=[pl.BlockSpec(memory_space=pltpu.HBM), vmem],
-        input_output_aliases={12: 1},
+        input_output_aliases={11: 1},
         scratch_shapes=[
             pltpu.VMEM((256, 512), BF),
             pltpu.VMEM((256, 128), BF),
@@ -368,7 +363,7 @@
         compiler_params=pltpu.CompilerParams(vmem_limit_bytes=16 << 20),
         cost_estimate=cost(3),
         name="two",
-    )(me, before, after_it, there, rim_cells, open_rims, first, bias, second, bias_second, opened, hidden, edges)
+    )(before, after_it, there, rim_cells, open_rims, first, bias, second, bias_second, opened, hidden, edges)
     return result.reshape(16, 8, 1, 1024)
 
 

time: 20.3 us -> 20.1 us (level)
  starting transfers between devices: 8.16 us -> 11.3 us
  waiting for transfers between devices: 2.34 us -> 0.15 us
  Pallas kernels: 9.47 us -> 8.28 us
    ppermute x2, starting transfers between devices: 2.24 us -> 5.01 us  [exchange(): return lax.ppermute(v, 'col', route)]
    ppermute x7 -> x8, waiting for transfers between devices: 2.34 us -> 0.02 us  [across(): lax.ppermute(v, 'ch', [(i, i ^ bit) for i in range(lax.axis_size('ch'))])]
    pallas_call x1, Pallas kernels: 1.38 us -> 0.75 us  [one_row(): pl.pallas_call(near_kernel, out_shape=[field_shape, rims_shape, shape((8,...]
    pallas_call x2, Pallas kernels: 1.01 us -> 0.45 us  [the longest x1 0.3 us: one_row(): pl.pallas_call(rims_kernel, out_shape=shape((288, 128), BF), in_specs=[vm...]
    ppermute x7 -> x8, starting transfers between devices: 5.92 us -> 6.25 us  [across(): lax.ppermute(v, 'ch', [(i, i ^ bit) for i in range(lax.axis_size('ch'))])]
  transfers between devices with their start and end apart: 9 -> 10, of which waited for: 2 -> 1; matrix products, arithmetic and copies ran while one was open for 0% -> 0% of each run, Pallas kernels for 31% -> 26%
where the time goes in v5:
time: 20.1 us; the launch traced here: 19.9 us
  starting transfers between devices  11.3 us (56%)
  Pallas kernels  8.28 us (41%)
    ppermute x8, starting transfers between devices, across(): lax.ppermute(v, 'ch', [(i, i ^ bit) for i in range(lax.axis_size('ch'))])  6.25 us
    ppermute x2, starting transfers between devices, exchange(): return lax.ppermute(v, 'col', route)  5.01 us
    pallas_call x1, Pallas kernels, one_row(): pl.pallas_call(one_kernel, out_shape=[field_shape, rims_shape, shape((640...  3.47 us
    pallas_call x1, Pallas kernels, one_row(): pl.pallas_call(two_kernel, out_shape=[shape((128, 1024), BF), shape((768,...  3.12 us
    pallas_call x1, Pallas kernels, one_row(): pl.pallas_call(near_kernel, out_shape=[field_shape, rims_shape, shape((8,...  0.75 us
    pallas_call x1, Pallas kernels, one_row(): pl.pallas_call(far_kernel, out_shape=[field_shape, rims_shape], in_specs=...  0.44 us
  transfers between devices with their start and end apart: 10, of which 1 were waited for; matrix products, arithmetic and copies ran while one was open for 0% of the time, Pallas kernels for 26%

profile of v5, /device:TPU:0, one launch (start us, length us, event | category | flops | bytes accessed | tf_op | source)
XLA Modules:
  0.0 19.9 jit_solution(11106890550255545223)
XLA Ops:
  0.0 0.0 copy-start
  0.0 0.0 copy-start.2
  0.0 0.0 copy-start.4
  0.0 0.0 copy-start.5
  0.0 3.0 %collective-permute-start.4 = (bf16[128,1024]{1,0:T(8,128)(2,1)}, bf16[128,1024]{1,0:T(8,128)(2,1)S(1)}, u32[]{:S(2)}, u32[]{:S(2)}) collective-permute-start(bf16[128,1024]{1,0:T(8,128)(2,1)} %bitcast.8), channel_id=1, source_target_pairs={{0,2},{1,3},{2,0},{3,1},{4,6},{5,7},{6,4},{7,5},{8,10},{9,11},{10,... | collective-permute-start | bytes 786440 | tf_op jit(solution)/shard_map/ppermute | solution.py:254
  3.0 0.1 select.3
  3.1 0.0 copy-done
  3.1 0.0 copy-done.2
  3.1 0.0 copy-start.1
  3.1 0.0 copy-start.3
  3.1 0.3 %rims.1 = bf16[288,128]{1,0:T(8,128)(2,1)S(1)} custom-call(bf16[1024,128]{1,0:T(8,128)(2,1)S(1)} %select.3, bf16[128,1024]{1,0:T(8,128)(2,1)S(1)} %bitcast.9, s32[8,1,1024]{2,1,0:T(1,128)S(1)} %copy-done.2), custom_call_target="tpu_custom_call" | custom-call | flops 575000000 | bytes 1500000 | tf_op jit(solution)/shard_map/rims/pallas_call | solution.py:287
  3.4 0.1 collective-permute-start
  3.5 0.5 %collective-permute-start.5 = (bf16[128,1024]{1,0:T(8,128)(2,1)S(1)}, bf16[128,1024]{1,0:T(8,128)(2,1)S(1)}, u32[]{:S(2)}, u32[]{:S(2)}) collective-permute-start(bf16[128,1024]{1,0:T(8,128)(2,1)S(1)} %bitcast.10), channel_id=1, source_target_pairs={{0,1},{1,0},{2,3},{3,2},{4,5},{5,4},{6,7},{7,6},{8,9},{9,8},{10,11... | collective-permute-start | bytes 786440 | tf_op jit(solution)/shard_map/ppermute | solution.py:254
  4.0 0.0 copy-done.4
  4.0 0.0 copy-done.5
  4.0 0.2 pack.1.w0
  4.2 0.8 %collective-permute-start.3 = (bf16[224,128]{1,0:T(8,128)(2,1)S(1)}, bf16[224,128]{1,0:T(8,128)(2,1)S(1)}, u32[]{:S(2)}, u32[]{:S(2)}) collective-permute-start(bf16[224,128]{1,0:T(8,128)(2,1)S(1)} %pack.1.w0), channel_id=1, source_target_pairs={{0,2},{1,3},{2,0},{3,1},{4,6},{5,7},{6,4},{7,5},{8,10},{9,11},{10,... | collective-permute-start | bytes 172040 | tf_op jit(solution)/shard_map/ppermute | solution.py:254
  4.9 0.0 collective-permute-done
  5.0 0.7 %collective-permute-start.1 = (bf16[144,128]{1,0:T(8,128)(2,1)S(1)}, bf16[144,128]{1,0:T(8,128)(2,1)S(1)}, u32[]{:S(2)}, u32[]{:S(2)}) collective-permute-start(bf16[144,128]{1,0:T(8,128)(2,1)S(1)} %get-tuple-element.48), channel_id=1, source_target_pairs={{4,8},{8,4},{12,16},{16,12},{20,24},{24,20},{5,9},{9,5},{13,17},{1... | collective-permute-start | bytes 110600 | tf_op jit(solution)/shard_map/ppermute | solution.py:263
  5.6 4.3 %collective-permute-start.2 = (bf16[144,128]{1,0:T(8,128)(2,1)S(1)}, bf16[144,128]{1,0:T(8,128)(2,1)S(1)}, u32[]{:S(2)}, u32[]{:S(2)}) collective-permute-start(bf16[144,128]{1,0:T(8,128)(2,1)S(1)} %get-tuple-element.47), channel_id=1, source_target_pairs={{0,4},{4,0},{8,12},{12,8},{16,20},{20,16},{24,28},{28,24},{1,5},{5... | collective-permute-start | bytes 110600 | tf_op jit(solution)/shard_map/ppermute | solution.py:263
  10.0 0.0 collective-permute-done.5.f1
  10.0 0.0 collective-permute-start.8
  10.0 0.0 copy-done.1
  10.0 0.0 copy-done.3
  10.0 0.7 %near.1 = (bf16[1920,1024]{1,0:T(8,128)(2,1)S(1)}, f32[4,128,128]{2,1,0:T(8,128)S(1)}, f32[8,1024]{1,0:T(8,128)S(1)}, f32[8,128]{1,0:T(8,128)S(1)}, bf16[288,256]{1,0:T(8,128)(2,1)S(1)}, /*index=5*/f32[16,128]{1,0:T(8,128)S(1)}) custom-call(f32[1,16]{1,0:T(1,128)S(1)} %bitcast.13, bf16[128,1024]{1,0:T(8,128)(2,1)S(1)} %bitcast.11, ...), custom_call_target="tpu_custom_call" | custom-call | flops 115000000 | bytes 300000 | tf_op jit(solution)/shard_map/near/pallas_call | solution.py:308
  10.8 0.0 collective-permute-done.4.f2
  10.8 0.6 %collective-permute-start.7 = (bf16[128,1024]{1,0:T(8,128)(2,1)S(1)}, bf16[128,1024]{1,0:T(8,128)(2,1)S(1)}, u32[]{:S(2)}, u32[]{:S(2)}) collective-permute-start(bf16[128,1024]{1,0:T(8,128)(2,1)S(1)} %collective-permute-done.4.f2), channel_id=1, source_target_pairs={{0,1},{1,0},{2,3},{3,2},{4,5},{5,4},{6,7},{7,6},{8,9},{9,8},{10,11... | collective-permute-start | bytes 786440 | tf_op jit(solution)/shard_map/ppermute | solution.py:254
  11.3 0.4 %far.1 = (bf16[1920,1024]{1,0:T(8,128)(2,1)S(1)}, f32[4,128,128]{2,1,0:T(8,128)S(1)}) custom-call(bf16[128,1024]{1,0:T(8,128)(2,1)S(1)} %collective-permute-done.4.f2, bf16[1920,1024]{1,0:T(8,128)(2,1)S(1)} %get-tuple-element.29.field_in, f32[4,128,128]{2,1,0:T(8,128)S(1)} %get-tuple-element.30.rims_in), custom_call_target="tpu_custom_call", output_to_operand_aliasing={{0}: (1, {}), {1}: (2, {})} | custom-call | flops 115000000 | bytes 300000 | tf_op jit(solution)/shard_map/far/pallas_call | solution.py:320
  11.8 0.0 collective-permute-done.3.w2
  11.8 0.0 collective-permute-done.1
  11.8 0.1 collective-permute-done.2
  11.9 0.0 collective-permute-start.9
  12.0 1.3 %collective-permute-start.6 = (bf16[256,128]{1,0:T(8,128)(2,1)S(1)}, bf16[256,128]{1,0:T(8,128)(2,1)S(1)}, u32[]{:S(2)}, u32[]{:S(2)}) collective-permute-start(bf16[256,128]{1,0:T(8,128)(2,1)S(1)} %pad_maximum_fusion), channel_id=1, source_target_pairs={{0,2},{1,3},{2,0},{3,1},{4,6},{5,7},{6,4},{7,5},{8,10},{9,11},{10,... | collective-permute-start | bytes 196616 | tf_op jit(solution)/shard_map/ppermute | solution.py:254
  13.3 0.0 collective-permute-done.8.w1
  13.3 0.0 collective-permute-done.9.w3
  13.3 0.0 collective-permute-done.7.f3
  13.3 3.5 %one.1 = (bf16[1920,1024]{1,0:T(8,128)(2,1)S(1)}, f32[4,128,128]{2,1,0:T(8,128)S(1)}, bf16[640,1024]{1,0:T(8,128)(2,1)S(1)}, bf16[384,768]{1,0:T(8,128)(2,1)S(1)...) custom-call(bf16[128,1024]{1,0:T(8,128)(2,1)S(1)} %collective-permute-done.7., ...), custom_call_target="tpu_custom_call", output_to_operand_aliasing={{0}: (8, {}), {1}: (9, {})} | custom-call | flops 4600000000 | bytes 12000000 | tf_op jit(solution)/shard_map/one/pallas_call | solution.py:338
  16.8 0.0 collective-permute-done.6.there
  16.8 3.1 %two.1 = (bf16[128,1024]{1,0:T(8,128)(2,1)}, bf16[768,512]{1,0:T(8,128)(2,1)S(1)}) custom-call(bf16[144,128]{1,0:T(8,128)(2,1)S(1)} %get-tuple-element.50.below, bf16[144,128]{1,0:T(8,128)(2,1)S(1)} %get-tuple-element.49.above, bf16[256,128]{1,0:T(8,128)(2,1)S(1)} %collective-permute-done.6.there, ...), custom_call_target="tpu_custom_call", output_to_operand_aliasing={{1}: (11, {})} | custom-call | flops 3449999872 | bytes 9000000 | tf_op jit(solution)/shard_map/two/pallas_call | solution.py:349
  (6 shorter events, 0.0 us)
Async XLA Ops:
  0.0 3.1 %copy-start = (bf16[16,8,1,1024]{3,1,2,0:T(8,128)(2,1)S(1)}, bf16[16,8,1,1024]{3,1,2,0:T(8,128)(2,1)}, u32[]{:S(2)}) copy-start(bf16[16,8,1,1024]{3,1,2,0:T(8,128)(2,1)} %param.6) | copy-start | bytes 786436
  0.0 3.1 %copy-start.2 = (s32[8,1,1024]{2,1,0:T(1,128)S(1)}, s32[8,1,1024]{2,1,0:T(1,128)}, u32[]{:S(2)}) copy-start(s32[8,1,1024]{2,1,0:T(1,128)} %mask.3) | copy-start | bytes 98308
  0.0 4.0 %copy-start.4 = (bf16[16,27,64]{2,0,1:T(8,128)(2,1)S(1)}, bf16[16,27,64]{2,0,1:T(8,128)(2,1)}, u32[]{:S(2)}) copy-start(bf16[16,27,64]{2,0,1:T(8,128)(2,1)} %param.8) | copy-start | bytes 165892
  0.0 4.0 %copy-start.5 = (f32[16]{0:T(128)S(1)}, f32[16]{0:T(128)}, u32[]{:S(2)}) copy-start(f32[16]{0:T(128)} %param.9) | copy-start | bytes 196
  0.0 10.8 %collective-permute-start.4 = (bf16[128,1024]{1,0:T(8,128)(2,1)}, bf16[128,1024]{1,0:T(8,128)(2,1)S(1)}, u32[]{:S(2)}, u32[]{:S(2)}) collective-permute-start(bf16[128,1024]{1,0:T(8,128)(2,1)} %bitcast.8), channel_id=1, source_target_pairs={{0,2},{1,3},{2,0},{3,1},{4,6},{5,7},{6,4},{7,5},{8,10},{9,11},{10,... | collective-permute-start | bytes 786440 | tf_op jit(solution)/shard_map/ppermute | solution.py:254
  3.1 6.9 %copy-start.1 = (bf16[16,27,64]{2,0,1:T(8,128)(2,1)S(1)}, bf16[16,27,64]{2,0,1:T(8,128)(2,1)}, u32[]{:S(2)}) copy-start(bf16[16,27,64]{2,0,1:T(8,128)(2,1)} %param.10) | copy-start | bytes 165892
  3.1 6.9 %copy-start.3 = (f32[16]{0:T(128)S(1)}, f32[16]{0:T(128)}, u32[]{:S(2)}) copy-start(f32[16]{0:T(128)} %param.11) | copy-start | bytes 196
  3.4 1.5 %collective-permute-start = (bf16[288,128]{1,0:T(8,128)(2,1)S(1)}, bf16[288,128]{1,0:T(8,128)(2,1)S(1)}, u32[]{:S(2)}, u32[]{:S(2)}) collective-permute-start(bf16[288,128]{1,0:T(8,128)(2,1)S(1)} %rims.1), channel_id=1, source_target_pairs={{0,1},{1,0},{2,3},{3,2},{4,5},{5,4},{6,7},{7,6},{8,9},{9,8},{10,11... | collective-permute-start | bytes 221192 | tf_op jit(solution)/shard_map/ppermute | solution.py:254
  3.5 6.5 %collective-permute-start.5 = (bf16[128,1024]{1,0:T(8,128)(2,1)S(1)}, bf16[128,1024]{1,0:T(8,128)(2,1)S(1)}, u32[]{:S(2)}, u32[]{:S(2)}) collective-permute-start(bf16[128,1024]{1,0:T(8,128)(2,1)S(1)} %bitcast.10), channel_id=1, source_target_pairs={{0,1},{1,0},{2,3},{3,2},{4,5},{5,4},{6,7},{7,6},{8,9},{9,8},{10,11... | collective-permute-start | bytes 786440 | tf_op jit(solution)/shard_map/ppermute | solution.py:254
  4.2 7.6 %collective-permute-start.3 = (bf16[224,128]{1,0:T(8,128)(2,1)S(1)}, bf16[224,128]{1,0:T(8,128)(2,1)S(1)}, u32[]{:S(2)}, u32[]{:S(2)}) collective-permute-start(bf16[224,128]{1,0:T(8,128)(2,1)S(1)} %pack.1.w0), channel_id=1, source_target_pairs={{0,2},{1,3},{2,0},{3,1},{4,6},{5,7},{6,4},{7,5},{8,10},{9,11},{10,... | collective-permute-start | bytes 172040 | tf_op jit(solution)/shard_map/ppermute | solution.py:254
  5.0 6.8 %collective-permute-start.1 = (bf16[144,128]{1,0:T(8,128)(2,1)S(1)}, bf16[144,128]{1,0:T(8,128)(2,1)S(1)}, u32[]{:S(2)}, u32[]{:S(2)}) collective-permute-start(bf16[144,128]{1,0:T(8,128)(2,1)S(1)} %get-tuple-element.48), channel_id=1, source_target_pairs={{4,8},{8,4},{12,16},{16,12},{20,24},{24,20},{5,9},{9,5},{13,17},{1... | collective-permute-start | bytes 110600 | tf_op jit(solution)/shard_map/ppermute | solution.py:263
  5.6 6.3 %collective-permute-start.2 = (bf16[144,128]{1,0:T(8,128)(2,1)S(1)}, bf16[144,128]{1,0:T(8,128)(2,1)S(1)}, u32[]{:S(2)}, u32[]{:S(2)}) collective-permute-start(bf16[144,128]{1,0:T(8,128)(2,1)S(1)} %get-tuple-element.47), channel_id=1, source_target_pairs={{0,4},{4,0},{8,12},{12,8},{16,20},{20,16},{24,28},{28,24},{1,5},{5... | collective-permute-start | bytes 110600 | tf_op jit(solution)/shard_map/ppermute | solution.py:263
  10.0 3.3 %collective-permute-start.8 = (bf16[224,128]{1,0:T(8,128)(2,1)S(1)}, bf16[224,128]{1,0:T(8,128)(2,1)S(1)}, u32[]{:S(2)}, u32[]{:S(2)}) collective-permute-start(bf16[224,128]{1,0:T(8,128)(2,1)S(1)} %pack.1.w0), channel_id=1, source_target_pairs={{0,1},{1,0},{2,3},{3,2},{4,5},{5,4},{6,7},{7,6},{8,9},{9,8},{10,11... | collective-permute-start | bytes 172040 | tf_op jit(solution)/shard_map/ppermute | solution.py:254
  10.8 2.5 %collective-permute-start.7 = (bf16[128,1024]{1,0:T(8,128)(2,1)S(1)}, bf16[128,1024]{1,0:T(8,128)(2,1)S(1)}, u32[]{:S(2)}, u32[]{:S(2)}) collective-permute-start(bf16[128,1024]{1,0:T(8,128)(2,1)S(1)} %collective-permute-done.4.f2), channel_id=1, source_target_pairs={{0,1},{1,0},{2,3},{3,2},{4,5},{5,4},{6,7},{7,6},{8,9},{9,8},{10,11... | collective-permute-start | bytes 786440 | tf_op jit(solution)/shard_map/ppermute | solution.py:254
  11.9 1.4 %collective-permute-start.9 = (bf16[224,128]{1,0:T(8,128)(2,1)S(1)}, bf16[224,128]{1,0:T(8,128)(2,1)S(1)}, u32[]{:S(2)}, u32[]{:S(2)}) collective-permute-start(bf16[224,128]{1,0:T(8,128)(2,1)S(1)} %collective-permute-done.3.w2), channel_id=1, source_target_pairs={{0,1},{1,0},{2,3},{3,2},{4,5},{5,4},{6,7},{7,6},{8,9},{9,8},{10,11... | collective-permute-start | bytes 172040 | tf_op jit(solution)/shard_map/ppermute | solution.py:254
  12.0 4.8 %collective-permute-start.6 = (bf16[256,128]{1,0:T(8,128)(2,1)S(1)}, bf16[256,128]{1,0:T(8,128)(2,1)S(1)}, u32[]{:S(2)}, u32[]{:S(2)}) collective-permute-start(bf16[256,128]{1,0:T(8,128)(2,1)S(1)} %pad_maximum_fusion), channel_id=1, source_target_pairs={{0,2},{1,3},{2,0},{3,1},{4,6},{5,7},{6,4},{7,5},{8,10},{9,11},{10,... | collective-permute-start | bytes 196616 | tf_op jit(solution)/shard_map/ppermute | solution.py:254

commit v6 on v5

--- a/solution.py
+++ b/solution.py
@@ -294,7 +294,7 @@
         name="rims",
     )(select, cells, solid_mask)
     rims_near = across(rims, 1)
-    near = across(after(cells, rims), 1)
+    near = across(after(cells, weights), 1)
 
     odd = lax.axis_index("col") % 2 == 1
     low = lax.broadcasted_iota(jnp.int32, (144, 128), 1) < 64

time: 20.1 us -> 19.8 us (0.985)
  starting transfers between devices: 11.3 us -> 10.9 us
    ppermute x8, starting transfers between devices: 6.25 us -> 5.88 us  [across(): lax.ppermute(v, 'ch', [(i, i ^ bit) for i in range(lax.axis_size('ch'))])]
  transfers between devices with their start and end apart: 10 -> 10, of which waited for: 1 -> 2; matrix products, arithmetic and copies ran while one was open for 0% -> 0% of each run, Pallas kernels for 26% -> 26%
where the time goes in v6:
time: 19.8 us; the launch traced here: 19.7 us
  starting transfers between devices  10.9 us (55%)
  Pallas kernels  8.29 us (42%)
  waiting for transfers between devices  0.25 us (1%)
    ppermute x8, starting transfers between devices, across(): lax.ppermute(v, 'ch', [(i, i ^ bit) for i in range(lax.axis_size('ch'))])  5.88 us
    ppermute x2, starting transfers between devices, exchange(): return lax.ppermute(v, 'col', route)  5.01 us
    pallas_call x1, Pallas kernels, one_row(): pl.pallas_call(one_kernel, out_shape=[field_shape, rims_shape, shape((640...  3.46 us
    pallas_call x1, Pallas kernels, one_row(): pl.pallas_call(two_kernel, out_shape=[shape((128, 1024), BF), shape((768,...  3.12 us
    pallas_call x1, Pallas kernels, one_row(): pl.pallas_call(near_kernel, out_shape=[field_shape, rims_shape, shape((8,...  0.75 us
    pallas_call x1, Pallas kernels, one_row(): pl.pallas_call(far_kernel, out_shape=[field_shape, rims_shape], in_specs=...  0.43 us
  transfers between devices with their start and end apart: 10, of which 2 were waited for; matrix products, arithmetic and copies ran while one was open for 0% of the time, Pallas kernels for 26%

profile of v6, /device:TPU:0, one launch (start us, length us, event | category | flops | bytes accessed | tf_op | source)
XLA Modules:
  0.0 19.7 jit_solution(10027144558579828603)
XLA Ops:
  0.0 0.0 copy-start
  0.0 0.0 copy-start.2
  0.0 0.0 copy-start.4
  0.0 0.0 copy-start.5
  0.0 3.0 %collective-permute-start.4 = (bf16[128,1024]{1,0:T(8,128)(2,1)}, bf16[128,1024]{1,0:T(8,128)(2,1)S(1)}, u32[]{:S(2)}, u32[]{:S(2)}) collective-permute-start(bf16[128,1024]{1,0:T(8,128)(2,1)} %bitcast.8), channel_id=1, source_target_pairs={{0,2},{1,3},{2,0},{3,1},{4,6},{5,7},{6,4},{7,5},{8,10},{9,11},{10,... | collective-permute-start | bytes 786440 | tf_op jit(solution)/shard_map/ppermute | solution.py:254
  3.0 0.1 select.3
  3.1 0.0 copy-done
  3.1 0.0 copy-done.2
  3.1 0.0 copy-start.1
  3.1 0.0 copy-start.3
  3.1 0.3 %rims.1 = bf16[288,128]{1,0:T(8,128)(2,1)S(1)} custom-call(bf16[1024,128]{1,0:T(8,128)(2,1)S(1)} %select.3, bf16[128,1024]{1,0:T(8,128)(2,1)S(1)} %bitcast.9, s32[8,1,1024]{2,1,0:T(1,128)S(1)} %copy-done.2), custom_call_target="tpu_custom_call" | custom-call | flops 575000000 | bytes 1500000 | tf_op jit(solution)/shard_map/rims/pallas_call | solution.py:287
  3.4 0.1 collective-permute-start
  3.5 0.0 copy-done.4
  3.5 0.0 copy-done.5
  3.5 0.2 pack.1.w0
  3.7 0.8 %collective-permute-start.3 = (bf16[224,128]{1,0:T(8,128)(2,1)S(1)}, bf16[224,128]{1,0:T(8,128)(2,1)S(1)}, u32[]{:S(2)}, u32[]{:S(2)}) collective-permute-start(bf16[224,128]{1,0:T(8,128)(2,1)S(1)} %pack.1.w0), channel_id=1, source_target_pairs={{0,2},{1,3},{2,0},{3,1},{4,6},{5,7},{6,4},{7,5},{8,10},{9,11},{10,... | collective-permute-start | bytes 172040 | tf_op jit(solution)/shard_map/ppermute | solution.py:254
  4.5 0.2 %collective-permute-start.5 = (bf16[128,1024]{1,0:T(8,128)(2,1)S(1)}, bf16[128,1024]{1,0:T(8,128)(2,1)S(1)}, u32[]{:S(2)}, u32[]{:S(2)}) collective-permute-start(bf16[128,1024]{1,0:T(8,128)(2,1)S(1)} %bitcast.10), channel_id=1, source_target_pairs={{0,1},{1,0},{2,3},{3,2},{4,5},{5,4},{6,7},{7,6},{8,9},{9,8},{10,11... | collective-permute-start | bytes 786440 | tf_op jit(solution)/shard_map/ppermute | solution.py:254
  4.7 0.1 collective-permute-done
  4.8 0.7 %collective-permute-start.1 = (bf16[144,128]{1,0:T(8,128)(2,1)S(1)}, bf16[144,128]{1,0:T(8,128)(2,1)S(1)}, u32[]{:S(2)}, u32[]{:S(2)}) collective-permute-start(bf16[144,128]{1,0:T(8,128)(2,1)S(1)} %get-tuple-element.48), channel_id=1, source_target_pairs={{4,8},{8,4},{12,16},{16,12},{20,24},{24,20},{5,9},{9,5},{13,17},{1... | collective-permute-start | bytes 110600 | tf_op jit(solution)/shard_map/ppermute | solution.py:263
  5.5 4.3 %collective-permute-start.2 = (bf16[144,128]{1,0:T(8,128)(2,1)S(1)}, bf16[144,128]{1,0:T(8,128)(2,1)S(1)}, u32[]{:S(2)}, u32[]{:S(2)}) collective-permute-start(bf16[144,128]{1,0:T(8,128)(2,1)S(1)} %get-tuple-element.47), channel_id=1, source_target_pairs={{0,4},{4,0},{8,12},{12,8},{16,20},{20,16},{24,28},{28,24},{1,5},{5... | collective-permute-start | bytes 110600 | tf_op jit(solution)/shard_map/ppermute | solution.py:263
  9.8 0.0 collective-permute-done.5.f1
  9.8 0.0 collective-permute-start.8
  9.8 0.0 copy-done.1
  9.8 0.0 copy-done.3
  9.8 0.7 %near.1 = (bf16[1920,1024]{1,0:T(8,128)(2,1)S(1)}, f32[4,128,128]{2,1,0:T(8,128)S(1)}, f32[8,1024]{1,0:T(8,128)S(1)}, f32[8,128]{1,0:T(8,128)S(1)}, bf16[288,256]{1,0:T(8,128)(2,1)S(1)}, /*index=5*/f32[16,128]{1,0:T(8,128)S(1)}) custom-call(f32[1,16]{1,0:T(1,128)S(1)} %bitcast.13, bf16[128,1024]{1,0:T(8,128)(2,1)S(1)} %bitcast.11, ...), custom_call_target="tpu_custom_call" | custom-call | flops 115000000 | bytes 300000 | tf_op jit(solution)/shard_map/near/pallas_call | solution.py:308
  10.6 0.0 collective-permute-done.4.f2
  10.6 0.6 %collective-permute-start.7 = (bf16[128,1024]{1,0:T(8,128)(2,1)S(1)}, bf16[128,1024]{1,0:T(8,128)(2,1)S(1)}, u32[]{:S(2)}, u32[]{:S(2)}) collective-permute-start(bf16[128,1024]{1,0:T(8,128)(2,1)S(1)} %collective-permute-done.4.f2), channel_id=1, source_target_pairs={{0,1},{1,0},{2,3},{3,2},{4,5},{5,4},{6,7},{7,6},{8,9},{9,8},{10,11... | collective-permute-start | bytes 786440 | tf_op jit(solution)/shard_map/ppermute | solution.py:254
  11.2 0.4 %far.1 = (bf16[1920,1024]{1,0:T(8,128)(2,1)S(1)}, f32[4,128,128]{2,1,0:T(8,128)S(1)}) custom-call(bf16[128,1024]{1,0:T(8,128)(2,1)S(1)} %collective-permute-done.4.f2, bf16[1920,1024]{1,0:T(8,128)(2,1)S(1)} %get-tuple-element.29.field_in, f32[4,128,128]{2,1,0:T(8,128)S(1)} %get-tuple-element.30.rims_in), custom_call_target="tpu_custom_call", output_to_operand_aliasing={{0}: (1, {}), {1}: (2, {})} | custom-call | flops 115000000 | bytes 300000 | tf_op jit(solution)/shard_map/far/pallas_call | solution.py:320
  11.6 0.0 collective-permute-done.3.w2
  11.6 0.0 collective-permute-done.1
  11.6 0.1 collective-permute-done.2
  11.7 0.0 collective-permute-start.9
  11.8 1.3 %collective-permute-start.6 = (bf16[256,128]{1,0:T(8,128)(2,1)S(1)}, bf16[256,128]{1,0:T(8,128)(2,1)S(1)}, u32[]{:S(2)}, u32[]{:S(2)}) collective-permute-start(bf16[256,128]{1,0:T(8,128)(2,1)S(1)} %pad_maximum_fusion), channel_id=1, source_target_pairs={{0,2},{1,3},{2,0},{3,1},{4,6},{5,7},{6,4},{7,5},{8,10},{9,11},{10,... | collective-permute-start | bytes 196616 | tf_op jit(solution)/shard_map/ppermute | solution.py:254
  13.1 0.0 collective-permute-done.8.w1
  13.1 0.0 collective-permute-done.9.w3
  13.1 0.0 collective-permute-done.7.f3
  13.1 3.5 %one.1 = (bf16[1920,1024]{1,0:T(8,128)(2,1)S(1)}, f32[4,128,128]{2,1,0:T(8,128)S(1)}, bf16[640,1024]{1,0:T(8,128)(2,1)S(1)}, bf16[384,768]{1,0:T(8,128)(2,1)S(1)...) custom-call(bf16[128,1024]{1,0:T(8,128)(2,1)S(1)} %collective-permute-done.7., ...), custom_call_target="tpu_custom_call", output_to_operand_aliasing={{0}: (8, {}), {1}: (9, {})} | custom-call | flops 4600000000 | bytes 12000000 | tf_op jit(solution)/shard_map/one/pallas_call | solution.py:338
  16.5 0.0 collective-permute-done.6.there
  16.6 3.1 %two.1 = (bf16[128,1024]{1,0:T(8,128)(2,1)}, bf16[768,512]{1,0:T(8,128)(2,1)S(1)}) custom-call(bf16[144,128]{1,0:T(8,128)(2,1)S(1)} %get-tuple-element.50.below, bf16[144,128]{1,0:T(8,128)(2,1)S(1)} %get-tuple-element.49.above, bf16[256,128]{1,0:T(8,128)(2,1)S(1)} %collective-permute-done.6.there, ...), custom_call_target="tpu_custom_call", output_to_operand_aliasing={{1}: (11, {})} | custom-call | flops 3449999872 | bytes 9000000 | tf_op jit(solution)/shard_map/two/pallas_call | solution.py:349
  (6 shorter events, 0.0 us)
Async XLA Ops:
  0.0 3.1 %copy-start = (bf16[16,8,1,1024]{3,1,2,0:T(8,128)(2,1)S(1)}, bf16[16,8,1,1024]{3,1,2,0:T(8,128)(2,1)}, u32[]{:S(2)}) copy-start(bf16[16,8,1,1024]{3,1,2,0:T(8,128)(2,1)} %param.6) | copy-start | bytes 786436
  0.0 3.1 %copy-start.2 = (s32[8,1,1024]{2,1,0:T(1,128)S(1)}, s32[8,1,1024]{2,1,0:T(1,128)}, u32[]{:S(2)}) copy-start(s32[8,1,1024]{2,1,0:T(1,128)} %mask.3) | copy-start | bytes 98308
  0.0 3.5 %copy-start.4 = (bf16[16,27,64]{2,0,1:T(8,128)(2,1)S(1)}, bf16[16,27,64]{2,0,1:T(8,128)(2,1)}, u32[]{:S(2)}) copy-start(bf16[16,27,64]{2,0,1:T(8,128)(2,1)} %param.8) | copy-start | bytes 165892
  0.0 3.5 %copy-start.5 = (f32[16]{0:T(128)S(1)}, f32[16]{0:T(128)}, u32[]{:S(2)}) copy-start(f32[16]{0:T(128)} %param.9) | copy-start | bytes 196
  0.0 10.6 %collective-permute-start.4 = (bf16[128,1024]{1,0:T(8,128)(2,1)}, bf16[128,1024]{1,0:T(8,128)(2,1)S(1)}, u32[]{:S(2)}, u32[]{:S(2)}) collective-permute-start(bf16[128,1024]{1,0:T(8,128)(2,1)} %bitcast.8), channel_id=1, source_target_pairs={{0,2},{1,3},{2,0},{3,1},{4,6},{5,7},{6,4},{7,5},{8,10},{9,11},{10,... | collective-permute-start | bytes 786440 | tf_op jit(solution)/shard_map/ppermute | solution.py:254
  3.1 6.7 %copy-start.1 = (bf16[16,27,64]{2,0,1:T(8,128)(2,1)S(1)}, bf16[16,27,64]{2,0,1:T(8,128)(2,1)}, u32[]{:S(2)}) copy-start(bf16[16,27,64]{2,0,1:T(8,128)(2,1)} %param.10) | copy-start | bytes 165892
  3.1 6.7 %copy-start.3 = (f32[16]{0:T(128)S(1)}, f32[16]{0:T(128)}, u32[]{:S(2)}) copy-start(f32[16]{0:T(128)} %param.11) | copy-start | bytes 196
  3.4 1.3 %collective-permute-start = (bf16[288,128]{1,0:T(8,128)(2,1)S(1)}, bf16[288,128]{1,0:T(8,128)(2,1)S(1)}, u32[]{:S(2)}, u32[]{:S(2)}) collective-permute-start(bf16[288,128]{1,0:T(8,128)(2,1)S(1)} %rims.1), channel_id=1, source_target_pairs={{0,1},{1,0},{2,3},{3,2},{4,5},{5,4},{6,7},{7,6},{8,9},{9,8},{10,11... | collective-permute-start | bytes 221192 | tf_op jit(solution)/shard_map/ppermute | solution.py:254
  3.7 7.9 %collective-permute-start.3 = (bf16[224,128]{1,0:T(8,128)(2,1)S(1)}, bf16[224,128]{1,0:T(8,128)(2,1)S(1)}, u32[]{:S(2)}, u32[]{:S(2)}) collective-permute-start(bf16[224,128]{1,0:T(8,128)(2,1)S(1)} %pack.1.w0), channel_id=1, source_target_pairs={{0,2},{1,3},{2,0},{3,1},{4,6},{5,7},{6,4},{7,5},{8,10},{9,11},{10,... | collective-permute-start | bytes 172040 | tf_op jit(solution)/shard_map/ppermute | solution.py:254
  4.5 5.3 %collective-permute-start.5 = (bf16[128,1024]{1,0:T(8,128)(2,1)S(1)}, bf16[128,1024]{1,0:T(8,128)(2,1)S(1)}, u32[]{:S(2)}, u32[]{:S(2)}) collective-permute-start(bf16[128,1024]{1,0:T(8,128)(2,1)S(1)} %bitcast.10), channel_id=1, source_target_pairs={{0,1},{1,0},{2,3},{3,2},{4,5},{5,4},{6,7},{7,6},{8,9},{9,8},{10,11... | collective-permute-start | bytes 786440 | tf_op jit(solution)/shard_map/ppermute | solution.py:254
  4.8 6.8 %collective-permute-start.1 = (bf16[144,128]{1,0:T(8,128)(2,1)S(1)}, bf16[144,128]{1,0:T(8,128)(2,1)S(1)}, u32[]{:S(2)}, u32[]{:S(2)}) collective-permute-start(bf16[144,128]{1,0:T(8,128)(2,1)S(1)} %get-tuple-element.48), channel_id=1, source_target_pairs={{4,8},{8,4},{12,16},{16,12},{20,24},{24,20},{5,9},{9,5},{13,17},{1... | collective-permute-start | bytes 110600 | tf_op jit(solution)/shard_map/ppermute | solution.py:263
  5.5 6.3 %collective-permute-start.2 = (bf16[144,128]{1,0:T(8,128)(2,1)S(1)}, bf16[144,128]{1,0:T(8,128)(2,1)S(1)}, u32[]{:S(2)}, u32[]{:S(2)}) collective-permute-start(bf16[144,128]{1,0:T(8,128)(2,1)S(1)} %get-tuple-element.47), channel_id=1, source_target_pairs={{0,4},{4,0},{8,12},{12,8},{16,20},{20,16},{24,28},{28,24},{1,5},{5... | collective-permute-start | bytes 110600 | tf_op jit(solution)/shard_map/ppermute | solution.py:263
  9.8 3.3 %collective-permute-start.8 = (bf16[224,128]{1,0:T(8,128)(2,1)S(1)}, bf16[224,128]{1,0:T(8,128)(2,1)S(1)}, u32[]{:S(2)}, u32[]{:S(2)}) collective-permute-start(bf16[224,128]{1,0:T(8,128)(2,1)S(1)} %pack.1.w0), channel_id=1, source_target_pairs={{0,1},{1,0},{2,3},{3,2},{4,5},{5,4},{6,7},{7,6},{8,9},{9,8},{10,11... | collective-permute-start | bytes 172040 | tf_op jit(solution)/shard_map/ppermute | solution.py:254
  10.6 2.5 %collective-permute-start.7 = (bf16[128,1024]{1,0:T(8,128)(2,1)S(1)}, bf16[128,1024]{1,0:T(8,128)(2,1)S(1)}, u32[]{:S(2)}, u32[]{:S(2)}) collective-permute-start(bf16[128,1024]{1,0:T(8,128)(2,1)S(1)} %collective-permute-done.4.f2), channel_id=1, source_target_pairs={{0,1},{1,0},{2,3},{3,2},{4,5},{5,4},{6,7},{7,6},{8,9},{9,8},{10,11... | collective-permute-start | bytes 786440 | tf_op jit(solution)/shard_map/ppermute | solution.py:254
  11.7 1.3 %collective-permute-start.9 = (bf16[224,128]{1,0:T(8,128)(2,1)S(1)}, bf16[224,128]{1,0:T(8,128)(2,1)S(1)}, u32[]{:S(2)}, u32[]{:S(2)}) collective-permute-start(bf16[224,128]{1,0:T(8,128)(2,1)S(1)} %collective-permute-done.3.w2), channel_id=1, source_target_pairs={{0,1},{1,0},{2,3},{3,2},{4,5},{5,4},{6,7},{7,6},{8,9},{9,8},{10,11... | collective-permute-start | bytes 172040 | tf_op jit(solution)/shard_map/ppermute | solution.py:254
  11.8 4.7 %collective-permute-start.6 = (bf16[256,128]{1,0:T(8,128)(2,1)S(1)}, bf16[256,128]{1,0:T(8,128)(2,1)S(1)}, u32[]{:S(2)}, u32[]{:S(2)}) collective-permute-start(bf16[256,128]{1,0:T(8,128)(2,1)S(1)} %pad_maximum_fusion), channel_id=1, source_target_pairs={{0,2},{1,3},{2,0},{3,1},{4,6},{5,7},{6,4},{7,5},{8,10},{9,11},{10,... | collective-permute-start | bytes 196616 | tf_op jit(solution)/shard_map/ppermute | solution.py:254
